TPU v7x, 32 devices: a whole 2x2x4 slice. The times are simulated.
32 devices in a mesh: fsdp: 4 (over x, core), ctx: 2 (over y), tp: 4 (over z).
Axes of the slice: x: 2, y: 2, z: 4, core: 2. Of those that a mesh axis runs over, the one named last changes fastest.
Arguments:
- hidden_in: bfloat16 [4, 1408, 2048], P('fsdp', 'ctx'), may hold values from -6 to 6
- doc_lengths: int32 [4, 4], P('fsdp'), may hold values from 1 to 1024, 1408 in all within a row
- expert_ids: int32 [4, 1408, 4], P('fsdp', 'ctx'), may hold values from 0 to 7, all different within a row
- fill_rank: int32 [4, 2, 704], P('fsdp', 'ctx'), may hold values from 0 to 703, each once within a row
- norm_gains: bfloat16 [2, 2048], replicated, may hold values from 0.5 to 1.5
- qkv_weight: bfloat16 [2048, 3, 2048], P(('fsdp', 'ctx'), None, 'tp'), may hold values from -0.125 to 0.125
- qkv_bias: bfloat16 [3, 2048], P(None, 'tp'), may hold values from -1 to 1
- out_weight: bfloat16 [2048, 2048], P('tp', ('fsdp', 'ctx')), may hold values from -2 to 2
- router_weight: bfloat16 [2048, 8], replicated, may hold values from -0.0625 to 0.0625
- blend_weight: bfloat16 [2048], replicated, may hold values from -0.125 to 0.125
- shared_inner: bfloat16 [2048, 2, 5632], P(('fsdp', 'ctx'), None, 'tp'), may hold values from -0.125 to 0.125
- shared_outer: bfloat16 [5632, 2048], P('tp', ('fsdp', 'ctx')), may hold values from -0.15625 to 0.15625
- expert_inner: bfloat16 [8, 2048, 2, 1408], P(('fsdp', 'ctx'), None, None, 'tp'), may hold values from -0.125 to 0.125
- expert_outer: bfloat16 [8, 1408, 2048], P(('fsdp', 'ctx'), 'tp'), may hold values from -0.4375 to 0.4375
- cotangent: bfloat16 [4, 1408, 2048], P('fsdp', 'ctx'), may hold values from -6 to 6
Outputs:
- layer_out: bfloat16 [4, 1408, 2048], P('fsdp', 'ctx')
- input_grad: bfloat16 [4, 1408, 2048], P('fsdp', 'ctx')
- gains_grad: float32 [2, 2048], replicated
- qkv_grad: float32 [2048, 3, 2048], P(('fsdp', 'ctx'), None, 'tp')
- bias_grad: float32 [3, 2048], P(None, 'tp')
- projection_grad: float32 [2048, 2048], P('tp', ('fsdp', 'ctx'))
- router_grad: float32 [2048, 8], replicated
- blend_grad: float32 [2048], replicated
- inner_shared: float32 [2048, 2, 5632], P(('fsdp', 'ctx'), None, 'tp')
- outer_shared: float32 [5632, 2048], P('tp', ('fsdp', 'ctx'))
- inner_expert: float32 [8, 2048, 2, 1408], P(('fsdp', 'ctx'), None, None, 'tp')
- outer_expert: float32 [8, 1408, 2048], P(('fsdp', 'ctx'), 'tp')
Inputs may be any that keep to these rules, and one draw needn't show every extreme that they name: `doc_lengths`: in each sequence the 4 lengths add up to 1408 and the longest is exactly 1024. `expert_ids`: each token names 4 different experts. `fill_rank`: for each index of fsdp and ctx, the 704 priorities of its block (its sequences' positions in order) are a permutation; a lower priority takes a slot first.
All inputs are finite; a program needn't handle non-finite values.
Results may differ from a plain program's by a relative error of at most 0.022.
Values may be sent and summed in bfloat16 or wider, within the bound.
No kernel may reach another device: no remote copies, remote signals or barrier semaphores. Data moves between devices by JAX's collectives and lax.ppermute only.
A program may use at most 384 MiB of HBM per device.

v0:
```python
import math

import jax
import jax.numpy as jnp
from jax import lax
from jax.sharding import PartitionSpec as P

HEAD_DIM = 128
TOP = 4
WINDOW = 1024


rotary_base = 1000000.0
norm_epsilon = 1e-06
masked_score = -1e30


def from_behind(block, axis, distance):
    devices = range(lax.axis_size(axis))
    route = [(i - distance, i) for i in devices if i - distance in devices]
    return lax.ppermute(block, axis, route)


def rotary_tables(positions):
    exponent = jnp.arange(HEAD_DIM // 2, dtype=jnp.float32) * (2.0 / HEAD_DIM)
    inverse = jnp.exp(-math.log(rotary_base) * exponent)
    angle = positions.astype(jnp.float32)[..., None] * inverse
    cosine = jnp.cos(angle)
    sine_table = jnp.sin(angle)
    return (
        jnp.concatenate([cosine, cosine], axis=-1),
        jnp.concatenate([sine_table, sine_table], axis=-1),
    )


def rotate(values, cosine, sine_table):
    half_dim = values.shape[-1] // 2
    turned = jnp.concatenate([-values[..., half_dim:], values[..., :half_dim]], axis=-1)
    return values * cosine + turned * sine_table


def rotate_back(grads, cosine, sine_table):
    half_dim = grads.shape[-1] // 2
    scaled = grads * sine_table
    turned = jnp.concatenate([scaled[..., half_dim:], -scaled[..., :half_dim]], axis=-1)
    return grads * cosine + turned


def document_layout(lengths, positions):
    ends = jnp.cumsum(lengths)
    number = jnp.sum((positions[:, None] >= ends[None, :-1]).astype(jnp.int32), axis=1)
    starts = ends - lengths
    picked = jnp.arange(lengths.shape[0], dtype=jnp.int32)[None, :] == number[:, None]
    first = jnp.sum(jnp.where(picked, starts[None, :], 0), axis=1)
    return (number, positions - first)


def root_norm(values, gain):
    scale = lax.rsqrt(jnp.mean(values * values, axis=-1, keepdims=True) + norm_epsilon)
    return values * scale * gain


def silu_parts(gate_pre):
    sigma = jax.nn.sigmoid(gate_pre)
    return (gate_pre * sigma, sigma * (1.0 + gate_pre * (1.0 - sigma)))


def attend_forward(queries, keys_all, values_all, allowed, score_scale):
    scores = (
        jnp.einsum("qhd,khd->hqk", queries, keys_all, preferred_element_type=jnp.float32)
        * score_scale
    )
    scores = jnp.where(allowed[None], scores, masked_score)
    row_max = jnp.max(scores, axis=-1, keepdims=True)
    row_total = jnp.sum(jnp.exp(scores - row_max), axis=-1, keepdims=True)
    log_total = row_max + jnp.log(row_total)
    weights_low = jnp.exp(scores - log_total).astype(jnp.bfloat16)
    mixed_result = jnp.einsum(
        "hqk,khd->qhd", weights_low, values_all, preferred_element_type=jnp.float32
    )
    return (mixed_result.astype(jnp.bfloat16), log_total)


def attend_backward(queries, keys_all, values_all, allowed, log_total, grad_mixed, score_scale):
    scores = (
        jnp.einsum("qhd,khd->hqk", queries, keys_all, preferred_element_type=jnp.float32)
        * score_scale
    )
    scores = jnp.where(allowed[None], scores, masked_score)
    soft = jnp.exp(scores - log_total)
    grad_soft = jnp.einsum(
        "qhd,khd->hqk", grad_mixed, values_all, preferred_element_type=jnp.float32
    )
    centre = jnp.sum(soft * grad_soft, axis=-1, keepdims=True)
    grad_scores = (soft * (grad_soft - centre)).astype(jnp.bfloat16)
    grad_queries = (
        jnp.einsum("hqk,khd->qhd", grad_scores, keys_all, preferred_element_type=jnp.float32)
        * score_scale
    )
    grad_keys = (
        jnp.einsum("hqk,qhd->khd", grad_scores, queries, preferred_element_type=jnp.float32)
        * score_scale
    )
    grad_values = jnp.einsum(
        "hqk,qhd->khd", soft.astype(jnp.bfloat16), grad_mixed, preferred_element_type=jnp.float32
    )
    return (grad_queries, grad_keys, grad_values)


def on_device(
    hidden_in,
    doc_lengths,
    expert_ids,
    fill_rank,
    norm_gains,
    qkv_weight,
    qkv_bias,
    out_weight,
    router_weight,
    blend_weight,
    shared_inner,
    shared_outer,
    expert_inner,
    expert_outer,
    cotangent,
):
    seq_count, half_len, width = hidden_in.shape
    tokens = seq_count * half_len
    local_width = qkv_weight.shape[2]
    local_heads = local_width // HEAD_DIM
    experts = router_weight.shape[1]
    expert_local = expert_inner.shape[0]
    groups = experts // expert_local
    capacity = tokens * TOP // experts
    score_scale = 1.0 / math.sqrt(HEAD_DIM)
    gains = norm_gains.astype(jnp.float32)
    qkv_full, out_full, inner_full, outer_full = (
        lax.all_gather(qkv_weight, ("fsdp", "ctx"), axis=0, tiled=True),
        lax.all_gather(out_weight, ("fsdp", "ctx"), axis=1, tiled=True),
        lax.all_gather(shared_inner, ("fsdp", "ctx"), axis=0, tiled=True),
        lax.all_gather(shared_outer, ("fsdp", "ctx"), axis=1, tiled=True),
    )
    positions = lax.axis_index("ctx") * half_len + jnp.arange(half_len, dtype=jnp.int32)
    earlier_pos = positions - half_len
    own_number, own_place = jax.vmap(document_layout, in_axes=(0, None))(doc_lengths, positions)
    prior_number = jax.vmap(document_layout, in_axes=(0, None))(doc_lengths, earlier_pos)[0]
    cosine, sine_table = rotary_tables(own_place)
    cosine = cosine[:, :, None, :]
    sine_table = sine_table[:, :, None, :]
    key_positions = jnp.concatenate([earlier_pos, positions])
    distance = positions[:, None] - key_positions[None, :]
    base_allowed = (distance >= 0) & (distance < WINDOW) & (key_positions[None, :] >= 0)
    key_numbers = jnp.concatenate([prior_number, own_number], axis=1)
    allowed = base_allowed[None] & (own_number[:, :, None] == key_numbers[:, None, :])
    residual = hidden_in.reshape(tokens, width).astype(jnp.float32)
    first_normalized = root_norm(residual, gains[0]).astype(jnp.bfloat16)
    linear_projection = (
        jnp.einsum("td,dcm->tcm", first_normalized, qkv_full, preferred_element_type=jnp.float32)
        + qkv_bias.astype(jnp.float32)[None]
    )
    heads = linear_projection.reshape(seq_count, half_len, 3, local_heads, HEAD_DIM)
    queries = rotate(heads[:, :, 0], cosine, sine_table).astype(jnp.bfloat16)
    keys_own = rotate(heads[:, :, 1], cosine, sine_table).astype(jnp.bfloat16)
    values_own = heads[:, :, 2].astype(jnp.bfloat16)
    keys_prior, values_prior = from_behind((keys_own, values_own), "ctx", 1)
    keys_all = jnp.concatenate([keys_prior, keys_own], axis=1)
    values_all = jnp.concatenate([values_prior, values_own], axis=1)
    sequence = 0
    mixed_one, log_one = attend_forward(
        queries[sequence], keys_all[sequence], values_all[sequence], allowed[sequence], score_scale
    )
    mixed_parts = [mixed_one]
    log_parts = [log_one]
    mixed_result = jnp.stack(mixed_parts).reshape(tokens, local_width)
    attn_part = jnp.dot(mixed_result, out_full, preferred_element_type=jnp.float32)
    after_attn = residual + lax.psum(attn_part, "tp")
    second_normalized = root_norm(after_attn, gains[1]).astype(jnp.bfloat16)
    router_logits = jnp.dot(second_normalized, router_weight, preferred_element_type=jnp.float32)
    router_probs = jax.nn.softmax(router_logits, axis=-1)
    route_rows = expert_ids.reshape(tokens, TOP)
    onehot = (route_rows[:, :, None] == jnp.arange(experts, dtype=jnp.int32)[None, None, :]).astype(
        jnp.float32
    )
    gate_values = jnp.sum(onehot * router_probs[:, None, :], axis=-1)
    membership = jnp.sum(onehot, axis=1).astype(jnp.bfloat16)
    priority = fill_rank.reshape(tokens)
    earlier = (priority[None, :] < priority[:, None]).astype(jnp.bfloat16)
    slot_counts = jnp.dot(earlier, membership, preferred_element_type=jnp.float32)
    slot_index = jnp.sum(onehot * slot_counts[:, None, :], axis=-1).astype(jnp.int32)
    kept_pairs = slot_index < capacity
    keep_weight = kept_pairs.astype(jnp.float32)
    flat_index = route_rows * capacity + slot_index
    target = jnp.where(kept_pairs, flat_index, experts * capacity).reshape(-1)
    pair_index = jnp.where(kept_pairs, flat_index, 0)
    token_ids = jnp.broadcast_to(
        jnp.arange(tokens, dtype=jnp.int32)[:, None], (tokens, TOP)
    ).reshape(-1)
    source = jnp.zeros((experts * capacity,), jnp.int32).at[target].set(token_ids, mode="drop")
    filled = jnp.zeros((experts * capacity,), jnp.bool_).at[target].set(True, mode="drop")
    slot_gate = (
        jnp.zeros((experts * capacity,), jnp.float32)
        .at[target]
        .set(gate_values.reshape(-1), mode="drop")
    )
    dispatch = jnp.where(filled[:, None], second_normalized[source], jnp.zeros((), jnp.bfloat16))
    expert_rows = lax.all_to_all(
        dispatch.reshape(groups, expert_local, capacity, width),
        ("fsdp", "ctx"),
        split_axis=0,
        concat_axis=2,
        tiled=True,
    )[0]
    expert_pre = jnp.einsum(
        "erd,edgf->ergf", expert_rows, expert_inner, preferred_element_type=jnp.float32
    )
    expert_act, expert_slope = silu_parts(expert_pre[:, :, 0])
    expert_hidden = (expert_act * expert_pre[:, :, 1]).astype(jnp.bfloat16)
    expert_result = jnp.einsum(
        "erf,efd->erd", expert_hidden, expert_outer, preferred_element_type=jnp.float32
    )
    returned = (
        lax.all_to_all(
            expert_result[None].astype(jnp.bfloat16),
            ("fsdp", "ctx"),
            split_axis=2,
            concat_axis=0,
            tiled=True,
        )
        .astype(jnp.float32)
        .reshape(experts * capacity, width)
    )
    common_expert_preactivation = jnp.einsum(
        "td,dgf->tgf", second_normalized, inner_full, preferred_element_type=jnp.float32
    )
    shared_act, shared_slope = silu_parts(common_expert_preactivation[:, 0])
    common_expert_hidden = (shared_act * common_expert_preactivation[:, 1]).astype(jnp.bfloat16)
    shared_part = jnp.dot(common_expert_hidden, outer_full, preferred_element_type=jnp.float32)
    blend = jax.nn.sigmoid(
        jnp.dot(second_normalized, blend_weight, preferred_element_type=jnp.float32)
    )
    expert_part = jnp.zeros((tokens, width), jnp.float32)
    for route_slot in range(TOP):
        expert_part = (
            expert_part
            + (keep_weight[:, route_slot] * gate_values[:, route_slot])[:, None]
            * returned[pair_index[:, route_slot]]
        )
    branch = lax.psum(
        (blend[:, None] * shared_part + expert_part).astype(jnp.bfloat16), "tp"
    ).astype(jnp.float32)
    layer_out = (after_attn + branch).astype(jnp.bfloat16).reshape(seq_count, half_len, width)
    grad_y = cotangent.reshape(tokens, width).astype(jnp.float32)
    shared_dot = jnp.sum(grad_y * shared_part, axis=-1)
    gate_dots = []
    for route_slot in range(TOP):
        gate_dots.append(jnp.sum(grad_y * returned[pair_index[:, route_slot]], axis=-1))
    gate_dot = jnp.stack(gate_dots, axis=1)
    grad_shared = (blend[:, None] * grad_y).astype(jnp.bfloat16)
    grad_shared_hidden = jnp.einsum(
        "td,fd->tf", grad_shared, outer_full, preferred_element_type=jnp.float32
    )
    grad_shared_pre = jnp.stack(
        [
            grad_shared_hidden * common_expert_preactivation[:, 1] * shared_slope,
            grad_shared_hidden * shared_act,
        ],
        axis=1,
    ).astype(jnp.bfloat16)
    inner_grad_full = jnp.einsum(
        "td,tgf->dgf", second_normalized, grad_shared_pre, preferred_element_type=jnp.float32
    )
    outer_grad_full = jnp.einsum(
        "tf,td->fd", common_expert_hidden, grad_shared, preferred_element_type=jnp.float32
    )
    grad_normed_part = jnp.einsum(
        "tgf,dgf->td", grad_shared_pre, inner_full, preferred_element_type=jnp.float32
    )
    grad_result = jnp.where(filled[:, None], slot_gate[:, None] * grad_y[source], 0.0).astype(
        jnp.bfloat16
    )
    grad_rows_in = lax.all_to_all(
        grad_result.reshape(groups, expert_local, capacity, width),
        ("fsdp", "ctx"),
        split_axis=0,
        concat_axis=2,
        tiled=True,
    )[0]
    grad_expert_hidden = jnp.einsum(
        "erd,efd->erf", grad_rows_in, expert_outer, preferred_element_type=jnp.float32
    )
    grad_expert_pre = jnp.stack(
        [grad_expert_hidden * expert_pre[:, :, 1] * expert_slope, grad_expert_hidden * expert_act],
        axis=2,
    ).astype(jnp.bfloat16)
    outer_expert = jnp.einsum(
        "erf,erd->efd", expert_hidden, grad_rows_in, preferred_element_type=jnp.float32
    )
    inner_expert = jnp.einsum(
        "erd,ergf->edgf", expert_rows, grad_expert_pre, preferred_element_type=jnp.float32
    )
    grad_rows_out = jnp.einsum(
        "ergf,edgf->erd", grad_expert_pre, expert_inner, preferred_element_type=jnp.float32
    )
    returned_back = (
        lax.all_to_all(
            grad_rows_out[None].astype(jnp.bfloat16),
            ("fsdp", "ctx"),
            split_axis=2,
            concat_axis=0,
            tiled=True,
        )
        .astype(jnp.float32)
        .reshape(experts * capacity, width)
    )
    for route_slot in range(TOP):
        grad_normed_part = (
            grad_normed_part
            + keep_weight[:, route_slot][:, None] * returned_back[pair_index[:, route_slot]]
        )
    grad_normed_sum, shared_total, gate_total = lax.psum(
        (grad_normed_part, shared_dot, gate_dot), "tp"
    )
    grad_blend = (blend * (1.0 - blend) * shared_total).astype(jnp.bfloat16)
    grad_gate = keep_weight * gate_total
    grad_probs = jnp.sum(onehot * grad_gate[:, :, None], axis=1)
    grad_logits = (
        router_probs * (grad_probs - jnp.sum(router_probs * grad_probs, axis=-1, keepdims=True))
    ).astype(jnp.bfloat16)
    router_grad_part = jnp.einsum(
        "td,te->de", second_normalized, grad_logits, preferred_element_type=jnp.float32
    )
    blend_grad_part = jnp.einsum(
        "td,t->d", second_normalized, grad_blend, preferred_element_type=jnp.float32
    )
    grad_normed_two = (
        grad_normed_sum
        + jnp.einsum("te,de->td", grad_logits, router_weight, preferred_element_type=jnp.float32)
        + grad_blend.astype(jnp.float32)[:, None] * blend_weight.astype(jnp.float32)[None, :]
    )
    after_norm_grad, gain_two_grad = jax.vjp(root_norm, after_attn, gains[1])[1](grad_normed_two)
    grad_after = grad_y + after_norm_grad
    grad_attn = grad_after.astype(jnp.bfloat16)
    projection_full = jnp.einsum(
        "tm,td->md", mixed_result, grad_attn, preferred_element_type=jnp.float32
    )
    grad_mixed = (
        jnp.einsum("td,md->tm", grad_attn, out_full, preferred_element_type=jnp.float32)
        .astype(jnp.bfloat16)
        .reshape(seq_count, half_len, local_heads, HEAD_DIM)
    )
    sequence = 0
    grad_query, grad_key, grad_value = attend_backward(
        queries[sequence],
        keys_all[sequence],
        values_all[sequence],
        allowed[sequence],
        log_parts[sequence],
        grad_mixed[sequence],
        score_scale,
    )
    query_parts = [grad_query]
    key_parts = [grad_key]
    value_parts = [grad_value]
    grad_queries = jnp.stack(query_parts)
    grad_keys = jnp.stack(key_parts)
    grad_values = jnp.stack(value_parts)
    sent_keys, sent_values = (
        from_behind(grad_keys[:, :half_len].astype(jnp.bfloat16), "ctx", -1).astype(jnp.float32),
        from_behind(grad_values[:, :half_len].astype(jnp.bfloat16), "ctx", -1).astype(jnp.float32),
    )
    grad_keys_own = grad_keys[:, half_len:] + sent_keys
    grad_values_own = grad_values[:, half_len:] + sent_values
    grad_linear = (
        jnp.stack(
            [
                rotate_back(grad_queries, cosine, sine_table),
                rotate_back(grad_keys_own, cosine, sine_table),
                grad_values_own,
            ],
            axis=2,
        )
        .astype(jnp.bfloat16)
        .reshape(tokens, 3, local_width)
    )
    bias_part = jnp.sum(grad_linear.astype(jnp.float32), axis=0)
    qkv_grad_full = jnp.einsum(
        "td,tcm->dcm", first_normalized, grad_linear, preferred_element_type=jnp.float32
    )
    grad_normed_one = lax.psum(
        jnp.einsum("tcm,dcm->td", grad_linear, qkv_full, preferred_element_type=jnp.float32).astype(
            jnp.bfloat16
        ),
        "tp",
    ).astype(jnp.float32)
    residual_norm_grad, gain_one_grad = jax.vjp(root_norm, residual, gains[0])[1](grad_normed_one)
    input_grad = (
        (grad_after + residual_norm_grad).astype(jnp.bfloat16).reshape(seq_count, half_len, width)
    )
    qkv_grad, projection_grad, inner_shared, outer_shared = (
        lax.psum_scatter(
            qkv_grad_full.astype(jnp.bfloat16), ("fsdp", "ctx"), scatter_dimension=0, tiled=True
        ).astype(jnp.float32),
        lax.psum_scatter(
            projection_full.astype(jnp.bfloat16), ("fsdp", "ctx"), scatter_dimension=1, tiled=True
        ).astype(jnp.float32),
        lax.psum_scatter(
            inner_grad_full.astype(jnp.bfloat16), ("fsdp", "ctx"), scatter_dimension=0, tiled=True
        ).astype(jnp.float32),
        lax.psum_scatter(
            outer_grad_full.astype(jnp.bfloat16), ("fsdp", "ctx"), scatter_dimension=1, tiled=True
        ).astype(jnp.float32),
    )
    gains_grad, bias_grad, router_grad, blend_grad = (
        lax.psum(
            jnp.stack([gain_one_grad, gain_two_grad]).astype(jnp.bfloat16), ("fsdp", "ctx")
        ).astype(jnp.float32),
        lax.psum(bias_part.astype(jnp.bfloat16), ("fsdp", "ctx")).astype(jnp.float32),
        lax.psum(router_grad_part.astype(jnp.bfloat16), ("fsdp", "ctx")).astype(jnp.float32),
        lax.psum(blend_grad_part.astype(jnp.bfloat16), ("fsdp", "ctx")).astype(jnp.float32),
    )
    return (
        layer_out,
        input_grad,
        gains_grad,
        qkv_grad,
        bias_grad,
        projection_grad,
        router_grad,
        blend_grad,
        inner_shared,
        outer_shared,
        inner_expert,
        outer_expert,
    )


def solution(mesh):
    placed = (
        P("fsdp", "ctx", None),
        P("fsdp", None),
        P("fsdp", "ctx", None),
        P("fsdp", "ctx", None),
        P(),
        P(("fsdp", "ctx"), None, "tp"),
        P(None, "tp"),
        P("tp", ("fsdp", "ctx")),
        P(),
        P(),
        P(("fsdp", "ctx"), None, "tp"),
        P("tp", ("fsdp", "ctx")),
        P(("fsdp", "ctx"), None, None, "tp"),
        P(("fsdp", "ctx"), "tp", None),
        P("fsdp", "ctx", None),
    )
    return jax.shard_map(
        on_device,
        mesh=mesh,
        in_specs=placed,
        out_specs=(
            P("fsdp", "ctx", None),
            P("fsdp", "ctx", None),
            P(),
            P(("fsdp", "ctx"), None, "tp"),
            P(None, "tp"),
            P("tp", ("fsdp", "ctx")),
            P(),
            P(),
            P(("fsdp", "ctx"), None, "tp"),
            P("tp", ("fsdp", "ctx")),
            P(("fsdp", "ctx"), None, None, "tp"),
            P(("fsdp", "ctx"), "tp", None),
        ),
        check_vma=False,
    )
```

profile of v0, /device:TPU:0, one launch (start us, length us, event | category | flops | bytes accessed | tf_op | source)
XLA Modules:
  0.0 2266.8 jit_solution(9873135265742089650)
XLA Ops:
  18.2 40.0 %all-gather.5.cloned.1.call-done = bf16[2048,3,512]{2,0,1:T(8,128)(2,1)} async-done(((bf16[256,3,512]{2,0,1:T(8,128)(2,1)}), bf16[2048,3,512]{2,0,1:T(8,128)(2,1)}) %all-gather.5.cloned.1.call-update) | async-done | bytes 6291472 | tf_op jit(solution)/shard_map/all_gather | solution.py:138
  138.3 16.5 scatter_custom_fusion
  166.0 175.4 %all-reduce.7.cloned.1.call-done = f32[704,2048]{1,0:T(8,128)} async-done(((f32[704,2048]{1,0:T(8,128)}), f32[704,2048]{1,0:T(8,128)}) %all-reduce.7.cloned.1.call-update) | async-done | bytes 5767184 | tf_op jit(solution)/shard_map/psum | solution.py:176
  350.3 24.6 %gather_fusion = bf16[2816,2048]{1,0:T(8,128)(2,1)} fusion(bf16[704,2048]{1,0:T(8,128)(2,1)} %multiply_convert_fusion.1, s32[3072]{0:T(1024)S(1)} %pad_clamp_fusion), kind=kCustom, calls=%fused_computation | custom fusion | bytes 23079936 | tf_op jit(solution)/shard_map/gather | solution.py:205
  382.3 149.5 %all_to_all.16 = bf16[8,1,352,2048]{3,2,1,0:T(8,128)(2,1)S(1)} all-to-all(bf16[8,1,352,2048]{3,2,1,0:T(8,128)(2,1)S(1)} %broadcast_select_fusion), channel_id=1, replica_groups=mesh['fsdp'=4,'ctx'=2,'tp'=4] {'fsdp','ctx'}, dimensions={0} | all-to-all | bytes 23068672 | tf_op jit(solution)/shard_map/all_to_all | solution.py:206
  551.2 66.3 %copy.149 = bf16[1,1,2816,2048]{3,1,0,2:T(2,128)(2,1)} copy(bf16[1,1,2816,2048]{3,2,1,0:T(8,128)(2,1)S(1)} %convert_bitcast_fusion) | data formatting | bytes 23068672 | tf_op jit(solution)/shard_map/convert_element_type | solution.py:223
  618.0 69.2 %reduce.35 = bf16[2816,2048]{1,0:T(8,128)(2,1)} reduce(bf16[2816,1,1,2048]{3,2,1,0:T(2,128)(2,1)} %bitcast.329, bf16[]{:T(256)} %broadcast.695), dimensions={1,2}, to_apply=%bitcast.323.reduce_sub_computation | reduce | bytes 23068674
  711.7 24.3 %gather_fusion.5 = f32[2816,2048]{1,0:T(8,128)} fusion(f32[704,2048]{1,0:T(8,128)} %convert_bitcast_fusion.1, s32[3072]{0:T(1024)S(1)} %pad_clamp_fusion), kind=kCustom, calls=%fused_computation.5 | custom fusion | bytes 46148608 | tf_op jit(solution)/shard_map/gather | solution.py:278
  739.5 14.7 fusion.59
  754.3 101.8 %all-to-all-done.1 = bf16[8,2,360448]{2,1,0:T(2,128)(2,1)} async-done(((bf16[8,2,360448]{2,1,0:T(2,128)(2,1)}), bf16[8,2,360448]{2,1,0:T(2,128)(2,1)}, u32[]{:S(2)}, u32[]{:S(2)}) %all-to-all-start.1) | async-done | bytes 11534368 | tf_op jit(solution)/shard_map/all_to_all | solution.py:222
  856.1 16.8 reshape.985
  872.9 21.2 bitcast_convert_fusion.2
  908.7 15.0 gather_fusion.3
  923.8 14.7 gather_fusion.2
  938.4 14.6 gather_fusion.1
  953.0 21.1 fusion.19
  974.2 18.7 all-reduce
  1014.4 129.7 %all_to_all.17 = bf16[8,1,352,2048]{3,2,1,0:T(8,128)(2,1)S(1)} all-to-all(bf16[8,1,352,2048]{3,2,1,0:T(8,128)(2,1)S(1)} %select_convert_fusion), channel_id=1, replica_groups=mesh['fsdp'=4,'ctx'=2,'tp'=4] {'fsdp','ctx'}, dimensions={0} | all-to-all | bytes 23068672 | tf_op jit(solution)/shard_map/all_to_all | solution.py:281
  1167.9 66.1 %copy.148 = bf16[1,1,2816,2048]{3,1,0,2:T(2,128)(2,1)} copy(bf16[1,1,2816,2048]{3,2,1,0:T(8,128)(2,1)S(1)} %fusion.1) | data formatting | bytes 23068672 | tf_op jit(solution)/shard_map/convert_element_type | solution.py:306
  1234.0 69.2 %reduce.36 = bf16[2816,2048]{1,0:T(8,128)(2,1)} reduce(bf16[2816,1,1,2048]{3,2,1,0:T(2,128)(2,1)} %bitcast.330, bf16[]{:T(256)} %broadcast.695), dimensions={1,2}, to_apply=%bitcast.322.reduce_sub_computation | reduce | bytes 23068674
  1336.0 113.2 %all-to-all-done.3 = bf16[8,2,360448]{2,1,0:T(2,128)(2,1)} async-done(((bf16[8,2,360448]{2,1,0:T(2,128)(2,1)}), bf16[8,2,360448]{2,1,0:T(2,128)(2,1)}, u32[]{:S(2)}, u32[]{:S(2)}) %all-to-all-start.3) | async-done | bytes 11534368 | tf_op jit(solution)/shard_map/all_to_all | solution.py:305
  1449.2 16.8 reshape.987
  1466.0 21.4 bitcast_convert_fusion.1
  1502.0 14.6 gather_fusion.8
  1531.1 15.0 gather_fusion.6
  1546.2 18.5 fusion.27
  1607.2 160.7 %all-reduce.9.cloned.1.call-done = f32[704,2048]{1,0:T(8,128)} async-done(((f32[704,2048]{1,0:T(8,128)}), f32[704,2048]{1,0:T(8,128)}) %all-reduce.9.cloned.1.call-update) | async-done | bytes 5767184 | tf_op jit(solution)/shard_map/psum | solution.py:320
  1913.1 26.3 %reduce-scatter.9.cloned.1.call-done = bf16[256,2,1408]{2,0,1:T(8,128)(2,1)} async-done(((bf16[2048,2,1408]{2,0,1:T(8,128)(2,1)}), bf16[256,2,1408]{2,0,1:T(8,128)(2,1)}) %reduce-scatter.9.cloned.1.call-update) | async-done | bytes 1441808 | tf_op jit(solution)/shard_map/reduce_scatter | solution.py:406
  1945.6 38.7 %reduce-scatter.7.cloned.1.call-done = bf16[512,256]{1,0:T(8,128)(2,1)} async-done(((bf16[512,2048]{1,0:T(8,128)(2,1)}), bf16[512,256]{1,0:T(8,128)(2,1)}) %reduce-scatter.7.cloned.1.call-update) | async-done | bytes 262160 | tf_op jit(solution)/shard_map/reduce_scatter | solution.py:403
  1986.1 207.3 %all-reduce.11.cloned.1.call-done = (bf16[704,2048]{1,0:T(8,128)(2,1)}, bf16[704,2048]{1,0:T(8,128)(2,1)}) async-done(((bf16[704,2048]{1,0:T(8,128)(2,1)}, bf16[704,2048]{1,0:T(8,128)(2,1)}), (bf16[704,2048]{1,0:T(8,128)(2,1)}, bf16[704,2048]{1,0:T(8,128)(2,1)})) %all-reduce.11.cloned.1.call-update) | async-done | bytes 5767184 | tf_op jit(solution)/shard_map/psum | solution.py:248
  2197.7 24.9 %all-reduce.1 = (bf16[2,2048]{1,0:T(2,128)(2,1)S(1)}, bf16[3,512]{1,0:T(4,128)(2,1)S(1)}, bf16[2048,8]{0,1:T(8,128)(2,1)S(1)}, bf16[2048]{0:T(1024)(128)(2,1)S(1)}) all-reduce(bf16[2,2048]{1,0:T(2,128)(2,1)S(1)} %pad_maximum_fusion.8, bf16[3,512]{1,0:T(4,128)(2,1)S(1)} %fusion.151, ...), channel_id=1, replica_groups=mesh['fsdp'=4,'ctx'=2,'tp'=4] {'fsdp','ctx'}, use_global_device_ids=true, to_apply=%region_34.35 | all-reduce | flops 24064 | bytes 96256 | tf_op jit(solution)/shard_map/psum | solution.py:414
  2236.6 20.9 reduce-scatter.5.cloned.1.call-done
  (386 shorter events, 503.4 us)
Async XLA Ops:
  7.2 524.7 %copy-start = (bf16[1,2048,2,352]{1,3,2,0:T(8,128)(2,1)S(1)}, bf16[1,2048,2,352]{1,3,2,0:T(8,128)(2,1)}, u32[]{:S(2)}) copy-start(bf16[1,2048,2,352]{1,3,2,0:T(8,128)(2,1)} %param.27) | copy-start | bytes 8650756
  7.2 51.0 %all-gather.5.cloned.1.call-start = ((), (), s32[]{:S(2)}) async-start(), calls=%async_computation.8 | async-start | bytes 7077888 | tf_op jit(solution)/shard_map/all_gather | solution.py:138
  7.9 119.3 %all-gather.7.cloned.1.call-start = ((), (), s32[]{:S(2)}) async-start(), calls=%async_computation.9 | async-start | bytes 2359296 | tf_op jit(solution)/shard_map/all_gather | solution.py:139
  8.7 332.8 %all-reduce.7.cloned.1.call-start = ((), (), s32[]{:S(2)}) async-start(), calls=%async_computation.10 | async-start | bytes 11534336 | tf_op jit(solution)/shard_map/psum | solution.py:176
  14.9 330.9 %copy-start.46 = (f32[1,2048]{1,0:T(1,128)}, f32[1,2048]{1,0:T(1,128)S(1)}, u32[]{:S(2)}) copy-start(f32[1,2048]{1,0:T(1,128)S(1)} %get-tuple-element.115) | copy-start | bytes 24580
  77.7 22.1 collective-permute-start.1
  85.6 32.1 %collective-permute-start = (bf16[1,704,4,128]{3,1,2,0:T(8,128)(2,1)}, bf16[1,704,4,128]{3,1,2,0:T(8,128)(2,1)}, u32[]{:S(2)}, u32[]{:S(2)}) collective-permute-start(bf16[1,704,4,128]{3,1,2,0:T(8,128)(2,1)} %bitcast.321), channel_id=1, source_target_pairs={{0,4},{1,5},{2,6},{3,7},{8,12},{9,13},{10,14},{11,15},{16,20},{17,... | collective-permute-start | bytes 2162696 | tf_op jit(solution)/shard_map/ppermute | solution.py:21
  133.2 606.3 %all-gather.9.cloned.1.call-start = ((), (), s32[]{:S(2)}) async-start(), calls=%async_computation.11 | async-start | bytes 12976128 | tf_op jit(solution)/shard_map/all_gather | solution.py:140
  138.3 207.5 %copy-start.81 = (s32[2816]{0:T(1024)}, s32[2816]{0:T(1024)S(1)}, u32[]{:S(2)}) copy-start(s32[2816]{0:T(1024)S(1)} %fusion.116) | copy-start | bytes 33796
  154.9 220.0 %copy-start.72 = (pred[8,352]{1,0:T(8,128)(4,1)}, pred[8,352]{1,0:T(8,128)(4,1)S(1)}, u32[]{:S(2)}) copy-start(pred[8,352]{1,0:T(8,128)(4,1)S(1)} %broadcast_in_dim.79) | copy-start | bytes 8452
  700.8 155.3 %all-to-all-start.1 = ((bf16[8,2,360448]{2,1,0:T(2,128)(2,1)}), bf16[8,2,360448]{2,1,0:T(2,128)(2,1)}, u32[]{:S(2)}, u32[]{:S(2)}) async-start(bf16[8,2,360448]{2,1,0:T(2,128)(2,1)} %reshape.984), calls=%async_computation.1 | async-start | bytes 23068672 | tf_op jit(solution)/shard_map/all_to_all | solution.py:222
  706.0 247.0 %all-gather.11.cloned.1.call-start = ((), (), s32[]{:S(2)}) async-start(), calls=%async_computation.12 | async-start | bytes 6488064 | tf_op jit(solution)/shard_map/all_gather | solution.py:141
  736.1 187.6 %copy-start.62 = (s32[1024]{0:T(1024)}, s32[1024]{0:T(1024)S(1)}, u32[]{:S(2)}) copy-start(s32[1024]{0:T(1024)S(1)} %get-tuple-element.134) | copy-start | bytes 12292
  736.1 202.3 %copy-start.60 = (s32[1024]{0:T(1024)}, s32[1024]{0:T(1024)S(1)}, u32[]{:S(2)}) copy-start(s32[1024]{0:T(1024)S(1)} %get-tuple-element.135) | copy-start | bytes 12292
  736.2 158.0 %copy-start.66 = (s32[1024]{0:T(1024)}, s32[1024]{0:T(1024)S(1)}, u32[]{:S(2)}) copy-start(s32[1024]{0:T(1024)S(1)} %get-tuple-element.132) | copy-start | bytes 12292
  736.2 172.5 %copy-start.64 = (s32[1024]{0:T(1024)}, s32[1024]{0:T(1024)S(1)}, u32[]{:S(2)}) copy-start(s32[1024]{0:T(1024)S(1)} %get-tuple-element.133) | copy-start | bytes 12292
  1014.4 129.8 %copy-start.85 = (bf16[1,352,2048]{2,1,0:T(8,128)(2,1)S(1)}, bf16[1,352,2048]{2,1,0:T(8,128)(2,1)}, u32[]{:S(2)}) copy-start(bf16[1,352,2048]{2,1,0:T(8,128)(2,1)} %param.28) | copy-start | bytes 4325380
  1316.8 132.5 %all-to-all-start.3 = ((bf16[8,2,360448]{2,1,0:T(2,128)(2,1)}), bf16[8,2,360448]{2,1,0:T(2,128)(2,1)}, u32[]{:S(2)}, u32[]{:S(2)}) async-start(bf16[8,2,360448]{2,1,0:T(2,128)(2,1)} %reshape.986), calls=%async_computation.3 | async-start | bytes 23068672 | tf_op jit(solution)/shard_map/all_to_all | solution.py:305
  1322.3 445.6 %all-reduce.9.cloned.1.call-start = ((), (), s32[]{:S(2)}) async-start(), calls=%async_computation.13 | async-start | bytes 11534336 | tf_op jit(solution)/shard_map/psum | solution.py:320
  1564.7 321.9 %reduce-scatter.11.cloned.1.call-start = ((), (), s32[]{:S(2)}) async-start(), calls=%async_computation.17 | async-start | bytes 6488064 | tf_op jit(solution)/shard_map/reduce_scatter | solution.py:409
  1577.4 362.0 %reduce-scatter.9.cloned.1.call-start = ((), (), s32[]{:S(2)}) async-start(), calls=%async_computation.16 | async-start | bytes 12976128 | tf_op jit(solution)/shard_map/reduce_scatter | solution.py:406
  1591.8 392.5 %reduce-scatter.7.cloned.1.call-start = ((), (), s32[]{:S(2)}) async-start(), calls=%async_computation.15 | async-start | bytes 2359296 | tf_op jit(solution)/shard_map/reduce_scatter | solution.py:403
  1595.1 172.9 %copy-start.45 = (bf16[2048,8]{0,1:T(8,128)(2,1)S(1)}, bf16[2048,8]{0,1:T(8,128)(2,1)}, u32[]{:S(2)}) copy-start(bf16[2048,8]{0,1:T(8,128)(2,1)} %param.23) | copy-start | bytes 98308
  1595.1 172.9 %copy-start.47 = (f32[1,2048]{1,0:T(1,128)S(1)}, f32[1,2048]{1,0:T(1,128)}, u32[]{:S(2)}) copy-start(f32[1,2048]{1,0:T(1,128)} %copy-done.46) | copy-start | bytes 24580
  1595.1 172.9 %copy-start.57 = (f32[704]{0:T(1024)S(1)}, f32[704]{0:T(1024)}, u32[]{:S(2)}) copy-start(f32[704]{0:T(1024)} %copy-done.56) | copy-start | bytes 8452
  1595.1 172.9 %copy-start.74 = (f32[704]{0:T(1024)S(1)}, f32[704]{0:T(1024)}, u32[]{:S(2)}) copy-start(f32[704]{0:T(1024)} %get-tuple-element.97) | copy-start | bytes 8452
  1797.1 47.5 %collective-permute-start.3 = (bf16[1,704,4,128]{3,1,2,0:T(8,128)(2,1)}, bf16[1,704,4,128]{3,1,2,0:T(8,128)(2,1)}, u32[]{:S(2)}, u32[]{:S(2)}) collective-permute-start(bf16[1,704,4,128]{3,1,2,0:T(8,128)(2,1)} %copy.105), channel_id=1, source_target_pairs={{4,0},{5,1},{6,2},{7,3},{12,8},{13,9},{14,10},{15,11},{20,16},{21,... | collective-permute-start | bytes 2162696 | tf_op jit(solution)/shard_map/ppermute | solution.py:21
  1828.6 26.7 %collective-permute-start.2 = (bf16[1,704,4,128]{3,1,2,0:T(8,128)(2,1)}, bf16[1,704,4,128]{3,1,2,0:T(8,128)(2,1)}, u32[]{:S(2)}, u32[]{:S(2)}) collective-permute-start(bf16[1,704,4,128]{3,1,2,0:T(8,128)(2,1)} %slice.288), channel_id=1, source_target_pairs={{4,0},{5,1},{6,2},{7,3},{12,8},{13,9},{14,10},{15,11},{20,16},{21,... | collective-permute-start | bytes 2162696 | tf_op jit(solution)/shard_map/ppermute | solution.py:21
  1833.1 360.3 %all-reduce.11.cloned.1.call-start = ((), (), s32[]{:S(2)}) async-start(), calls=%async_computation.18 | async-start | bytes 11534336 | tf_op jit(solution)/shard_map/psum | solution.py:248
  1875.0 382.5 %reduce-scatter.5.cloned.1.call-start = ((), (), s32[]{:S(2)}) async-start(), calls=%async_computation.14 | async-start | bytes 7077888 | tf_op jit(solution)/shard_map/reduce_scatter | solution.py:400
  1913.1 280.3 %copy-start.4 = (bf16[1,704,2048]{2,1,0:T(8,128)(2,1)S(1)}, bf16[1,704,2048]{2,1,0:T(8,128)(2,1)}, u32[]{:S(2)}) copy-start(bf16[1,704,2048]{2,1,0:T(8,128)(2,1)} %param.15) | copy-start | bytes 8650756
  1944.0 281.1 %copy-start.69 = (f32[704]{0:T(1024)S(1)}, f32[704]{0:T(1024)}, u32[]{:S(2)}) copy-start(f32[704]{0:T(1024)} %copy-done.68) | copy-start | bytes 8452
  (82 other events, 849.0 us)
Sparse Core Ops, SparseCore 0:
  9.9 48.2 all-gather.4
  60.1 28.1 all-gather.6
  133.4 208.0 all-reduce.6
  343.8 103.6 all-gather.8
  708.4 88.8 all-gather.10
  1564.8 203.0 all-reduce.8
  1771.4 75.5 reduce-scatter.10
  1850.8 88.5 reduce-scatter.8
  1943.1 41.1 reduce-scatter.6
  1987.1 206.2 all-reduce.10
  2196.8 60.6 reduce-scatter.4
where the time goes:
time: 2280 us; the launch traced here: 2270 us
  waiting for transfers between devices  900 us (39%)
  local copies, waits for them, and re-layouts  456 us (20%)
  blocking collectives  323 us (14%)
  other arithmetic  299 us (13%)
  matrix products  253 us (11%)
    psum x1, waiting for transfers between devices, on_device(): lax.psum((blend[:, None] * shared_part + expert_part).astype(jnp.bfloat16...  207 us
    psum x1, waiting for transfers between devices, on_device(): after_attn = residual + lax.psum(attn_part, 'tp')  175 us
    psum x1, waiting for transfers between devices, on_device(): lax.psum((grad_normed_part, shared_dot, gate_dot), 'tp')  161 us
    all_to_all x1, blocking collectives, on_device(): lax.all_to_all(dispatch.reshape(groups, expert_local, capacity, width), (...  150 us
    unnamed x5, other arithmetic  138 us
    all_to_all x1, blocking collectives, on_device(): lax.all_to_all(grad_result.reshape(groups, expert_local, capacity, width)...  130 us
    all_to_all x1, waiting for transfers between devices, on_device(): lax.all_to_all(grad_rows_out[None].astype(jnp.bfloat16), ('fsdp', 'ctx'),...  113 us
    all_to_all x1, waiting for transfers between devices, on_device(): lax.all_to_all(expert_result[None].astype(jnp.bfloat16), ('fsdp', 'ctx'),...  102 us
  transfers between devices with their start and end apart: 17, of which 11 were waited for; matrix products, arithmetic and copies ran while one was open for 29% of the time, Pallas kernels for 0%

commit v1 on v0

--- a/solution.py
+++ b/solution.py
@@ -107,7 +107,7 @@
     return (grad_queries, grad_keys, grad_values)
 
 
-def on_device(
+def general_plan(
     hidden_in,
     doc_lengths,
     expert_ids,
@@ -434,6 +434,493 @@
     )
 
 
+def after(values, *earlier):
+    return lax.optimization_barrier((values, earlier))[0]
+
+
+def swap_x(values):
+    return lax.ppermute(values, "fsdp", [(f, f ^ 2) for f in range(4)])
+
+
+def swap_core(values):
+    return lax.ppermute(values, "fsdp", [(f, f ^ 1) for f in range(4)])
+
+
+def swap_y(values):
+    return lax.ppermute(values, "ctx", [(0, 1), (1, 0)])
+
+
+def own_number():
+    return lax.axis_index("fsdp") * 2 + lax.axis_index("ctx")
+
+
+def exchange_order(parts):
+    number = own_number()
+    for bit in (4, 2, 1):
+        taken = (number & bit) != 0
+        parts = [jnp.where(taken, parts[i ^ bit], parts[i]) for i in range(8)]
+    return parts
+
+
+def spread_chips(block):
+    half = block.shape[0] // 2
+    from_x = swap_x(block)
+    from_y = swap_y(block)
+    low_part = swap_x(from_y[:half])
+    high_part = swap_y(from_x[half:])
+    return [block, from_y, from_x, jnp.concatenate([low_part, high_part])]
+
+
+def gather_eight(block):
+    own, from_y, from_x, from_both = spread_chips(block)
+    return [
+        own,
+        from_y,
+        swap_core(own),
+        swap_core(from_y),
+        from_x,
+        from_both,
+        swap_core(from_x),
+        swap_core(from_both),
+    ]
+
+
+def add_low(one, other):
+    return (one.astype(jnp.float32) + other.astype(jnp.float32)).astype(jnp.bfloat16)
+
+
+def reduce_chips(own, for_y, for_x, for_both):
+    half = own.shape[0] // 2
+    low_part = swap_x(for_both[:half])
+    high_part = swap_y(for_both[half:])
+    for_y = jnp.concatenate([add_low(for_y[:half], low_part), for_y[half:]])
+    for_x = jnp.concatenate([for_x[:half], add_low(for_x[half:], high_part)])
+    return (
+        own.astype(jnp.float32)
+        + swap_x(for_x).astype(jnp.float32)
+        + swap_y(for_y).astype(jnp.float32)
+    )
+
+
+def reduce_eight(parts):
+    return reduce_chips(
+        add_low(parts[0], swap_core(parts[2])),
+        add_low(parts[1], swap_core(parts[3])),
+        add_low(parts[4], swap_core(parts[6])),
+        add_low(parts[5], swap_core(parts[7])),
+    )
+
+
+def trade_eight(parts):
+    rows = parts[0].shape[0]
+    from_y = swap_y(jnp.concatenate([parts[1], parts[3]]))
+    from_x = swap_x(jnp.concatenate([parts[4], parts[6]]))
+    both = lax.ppermute(
+        jnp.concatenate([parts[5], parts[7]]),
+        ("fsdp", "ctx"),
+        [(d, d ^ 5) for d in range(8)],
+    )
+    sibling = swap_core(
+        jnp.concatenate([parts[2], from_y[rows:], from_x[rows:], both[rows:]])
+    )
+    return [
+        parts[0],
+        from_y[:rows],
+        sibling[:rows],
+        sibling[rows : 2 * rows],
+        from_x[:rows],
+        both[:rows],
+        sibling[2 * rows : 3 * rows],
+        sibling[3 * rows :],
+    ]
+
+
+def pick(blocks, index):
+    return lax.dynamic_index_in_dim(blocks, index, axis=0, keepdims=False)
+
+
+def line_gather(block):
+    count = lax.axis_size("tp")
+    me = lax.axis_index("tp")
+    right, left = block, block
+    result = jnp.broadcast_to(block[None], (count,) + block.shape)
+    for step in range(1, count):
+        right = lax.ppermute(right, "tp", [(i, i + 1) for i in range(step - 1, count - 1)])
+        left = lax.ppermute(left, "tp", [(i, i - 1) for i in range(1, count - step + 1)])
+        place = jnp.arange(count, dtype=jnp.int32).reshape((count,) + (1,) * block.ndim)
+        result = jnp.where(
+            place == me - step, right[None], jnp.where(place == me + step, left[None], result)
+        )
+    return result
+
+
+def line_reduce(blocks):
+    count = blocks.shape[0]
+    me = lax.axis_index("tp")
+    right, left = None, None
+    for step in range(1, count):
+        to_right = pick(blocks, jnp.minimum(count - step + me, count - 1))
+        to_left = pick(blocks, jnp.maximum(step + me - count, 0))
+        if step > 1:
+            to_right, to_left = add_low(to_right, right), add_low(to_left, left)
+        right = lax.ppermute(to_right, "tp", [(i, i + 1) for i in range(min(step, count - 1))])
+        left = lax.ppermute(
+            to_left, "tp", [(i, i - 1) for i in range(max(count - step, 1), count)]
+        )
+    return (
+        pick(blocks, me).astype(jnp.float32)
+        + right.astype(jnp.float32)
+        + left.astype(jnp.float32)
+    )
+
+
+def columns_of(values, count):
+    wide = values.shape[1] // count
+    return [values[:, i * wide : (i + 1) * wide] for i in range(count)]
+
+
+def mixture_chunk(rows, grads, kept, inner, outer, mine, sizes):
+    hid_e, hid, pad, experts = sizes
+    pre = lax.dot_general(
+        rows, inner, (((1,), (1,)), ((), ())), preferred_element_type=jnp.float32
+    )
+    upstream = lax.dot_general(
+        grads, outer, (((1,), (1,)), ((), ())), preferred_element_type=jnp.float32
+    )
+    gate_pre = pre[:, :hid]
+    up_pre = pre[:, pad:]
+    probs = jax.nn.softmax(pre[:, hid : hid + experts], axis=-1)
+    own_prob = jnp.sum(probs * mine, axis=-1, keepdims=True)
+    blend = jax.nn.sigmoid(pre[:, hid + experts : hid + experts + 1])
+    gate = kept * own_prob
+    of_expert = jnp.arange(hid)[None, :] < hid_e
+    weight = jnp.where(of_expert, gate, blend)
+    act, slope = silu_parts(gate_pre)
+    hidden = (act * up_pre).astype(jnp.bfloat16).astype(jnp.float32)
+    product = hidden * upstream
+    gate_dot = kept * jnp.sum(jnp.where(of_expert, product, 0.0), axis=-1, keepdims=True)
+    blend_dot = jnp.sum(jnp.where(of_expert, 0.0, product), axis=-1, keepdims=True)
+    grad_logits = probs * gate_dot * (mine - own_prob)
+    grad_blend = blend * (1.0 - blend) * blend_dot
+    scaled = weight * upstream
+    grad_pre = jnp.concatenate(
+        [
+            scaled * up_pre * slope,
+            grad_logits,
+            grad_blend,
+            jnp.zeros((rows.shape[0], pad - hid - experts - 1), jnp.float32),
+            scaled * act,
+        ],
+        axis=1,
+    ).astype(jnp.bfloat16)
+    weighted = (weight * hidden).astype(jnp.bfloat16)
+    back = jnp.dot(grad_pre, inner, preferred_element_type=jnp.float32).astype(jnp.bfloat16)
+    return (grad_pre, weighted, back)
+
+
+def eight_plan(
+    hidden_in,
+    doc_lengths,
+    expert_ids,
+    fill_rank,
+    norm_gains,
+    qkv_weight,
+    qkv_bias,
+    out_weight,
+    router_weight,
+    blend_weight,
+    shared_inner,
+    shared_outer,
+    expert_inner,
+    expert_outer,
+    cotangent,
+):
+    _, tokens, width = hidden_in.shape
+    local_width = qkv_weight.shape[2]
+    local_heads = local_width // HEAD_DIM
+    experts = router_weight.shape[1]
+    capacity = tokens * TOP // experts
+    score_scale = 1.0 / math.sqrt(HEAD_DIM)
+    gains = norm_gains.astype(jnp.float32)
+    me_tp = lax.axis_index("tp")
+    tp = lax.axis_size("tp")
+    share = tokens // tp
+    number = own_number()
+
+    def own_rows(values):
+        return lax.dynamic_slice_in_dim(values, me_tp * share, share, axis=0)
+
+    qkv_parts = gather_eight(qkv_weight)
+    qkv_rel = jnp.concatenate(qkv_parts, axis=0)
+
+    route_rows = expert_ids.reshape(tokens, TOP)
+    named = jnp.sum(
+        (route_rows[:, :, None] == jnp.arange(experts, dtype=jnp.int32)[None, None, :]).astype(
+            jnp.float32
+        ),
+        axis=1,
+    )
+    priority = fill_rank.reshape(tokens)
+    earlier = (priority[None, :] < priority[:, None]).astype(jnp.bfloat16)
+    slot_counts = jnp.dot(
+        earlier, named.astype(jnp.bfloat16), preferred_element_type=jnp.float32
+    )
+    kept_all = named * (slot_counts < capacity).astype(jnp.float32)
+    kept_blocks = lax.all_to_all(
+        kept_all.T.reshape(experts, 1, tokens),
+        ("fsdp", "ctx"),
+        split_axis=0,
+        concat_axis=0,
+        tiled=True,
+    )
+    kept_rel = exchange_order([kept_blocks[i].reshape(tokens, 1) for i in range(8)])
+
+    half_len = tokens
+    positions = lax.axis_index("ctx") * half_len + jnp.arange(half_len, dtype=jnp.int32)
+    earlier_pos = positions - half_len
+    own_number_doc, own_place = document_layout(doc_lengths[0], positions)
+    prior_number = document_layout(doc_lengths[0], earlier_pos)[0]
+    cosine, sine_table = rotary_tables(own_place)
+    cosine = cosine[:, None, :]
+    sine_table = sine_table[:, None, :]
+    key_positions = jnp.concatenate([earlier_pos, positions])
+    distance = positions[:, None] - key_positions[None, :]
+    key_numbers = jnp.concatenate([prior_number, own_number_doc])
+    allowed = (
+        (distance >= 0)
+        & (distance < WINDOW)
+        & (key_positions[None, :] >= 0)
+        & (own_number_doc[:, None] == key_numbers[None, :])
+    )
+    residual = hidden_in.reshape(tokens, width).astype(jnp.float32)
+    first_normalized = root_norm(residual, gains[0]).astype(jnp.bfloat16)
+    first_rel = jnp.concatenate(exchange_order(columns_of(first_normalized, 8)), axis=1)
+    linear_projection = (
+        jnp.einsum("td,dcm->tcm", first_rel, qkv_rel, preferred_element_type=jnp.float32)
+        + qkv_bias.astype(jnp.float32)[None]
+    )
+    heads = linear_projection.reshape(tokens, 3, local_heads, HEAD_DIM)
+    queries = rotate(heads[:, 0], cosine, sine_table).astype(jnp.bfloat16)
+    keys_own = rotate(heads[:, 1], cosine, sine_table).astype(jnp.bfloat16)
+    values_own = heads[:, 2].astype(jnp.bfloat16)
+    keys_prior, values_prior = from_behind((keys_own, values_own), "ctx", 1)
+    keys_all = jnp.concatenate([keys_prior, keys_own], axis=0)
+    values_all = jnp.concatenate([values_prior, values_own], axis=0)
+
+    shared_t = jnp.transpose(after(shared_inner, qkv_parts[5]), (1, 2, 0))
+    hid_s = shared_t.shape[1] // 8
+    pieces = [
+        jnp.concatenate(
+            [
+                shared_t[0, d * hid_s : (d + 1) * hid_s],
+                shared_t[1, d * hid_s : (d + 1) * hid_s],
+                shared_outer[d * hid_s : (d + 1) * hid_s],
+            ]
+        )
+        for d in range(8)
+    ]
+    shared_rows = jnp.concatenate(
+        exchange_order(trade_eight(exchange_order(pieces))), axis=1
+    )
+    out_own = jnp.concatenate(
+        exchange_order(gather_eight(after(out_weight, qkv_parts[5]))), axis=1
+    )
+    half_rows = local_width // 2
+    core = lax.axis_index("fsdp") % 2
+    out_half = line_gather(
+        lax.dynamic_slice_in_dim(out_own, core * half_rows, half_rows, axis=0)
+    )
+    out_other = swap_core(out_half)
+    out_full = jnp.stack(
+        [
+            jnp.where(core == 0, out_half, out_other),
+            jnp.where(core == 0, out_other, out_half),
+        ],
+        axis=1,
+    ).reshape(tp * local_width, width)
+
+    mixed_result, log_total = attend_forward(queries, keys_all, values_all, allowed, score_scale)
+    mixed_result = mixed_result.reshape(tokens, local_width)
+
+    grad_rows = cotangent.reshape(tokens, width)
+    grad_parts = gather_eight(after(grad_rows, keys_prior, values_prior, shared_rows))
+
+    mixed_all = line_gather(mixed_result)
+    attended = jnp.concatenate([mixed_all[i] for i in range(tp)], axis=1)
+    after_attn = residual + jnp.dot(attended, out_full, preferred_element_type=jnp.float32)
+    second_normalized = root_norm(after_attn, gains[1]).astype(jnp.bfloat16)
+
+    hid_e = expert_inner.shape[3]
+    hid = hid_e + hid_s
+    pad = -(-(hid + experts + 1) // 128) * 128
+    expert_t = jnp.transpose(expert_inner[0], (1, 2, 0))
+    inner = jnp.concatenate(
+        [
+            expert_t[0],
+            shared_rows[:hid_s],
+            router_weight.T,
+            blend_weight[None],
+            jnp.zeros((pad - hid - experts - 1, width), jnp.bfloat16),
+            expert_t[1],
+            shared_rows[hid_s : 2 * hid_s],
+        ]
+    )
+    outer = jnp.concatenate([expert_outer[0], shared_rows[2 * hid_s :]])
+    mine = (jnp.arange(experts, dtype=jnp.int32) == number).astype(jnp.float32)[None]
+    sizes = (hid_e, hid, pad, experts)
+
+    row_parts = gather_eight(after(second_normalized, grad_parts[5]))
+    pre_list, weighted_list, back_list = [], [], []
+    for pair in (0, 1, 4, 5):
+        grad_pre, weighted, back = mixture_chunk(
+            jnp.concatenate([row_parts[pair], row_parts[pair + 2]]),
+            jnp.concatenate([grad_parts[pair], grad_parts[pair + 2]]),
+            jnp.concatenate([kept_rel[pair], kept_rel[pair + 2]]),
+            inner,
+            outer,
+            mine,
+            sizes,
+        )
+        pre_list.append(grad_pre)
+        weighted_list.append(weighted)
+        back_list.append(back)
+
+    def to_chips(chunks):
+        return reduce_chips(
+            *[add_low(chunk[:tokens], swap_core(chunk[tokens:])) for chunk in chunks]
+        ).astype(jnp.bfloat16)
+
+    back_sum = to_chips(back_list)
+    grad_normed_two = line_reduce(back_sum.reshape(tp, share, width))
+
+    forward_list = [
+        jnp.dot(w, outer, preferred_element_type=jnp.float32).astype(jnp.bfloat16)
+        for w in weighted_list
+    ]
+    forward_list = after(forward_list, back_sum)
+    forward_sum = to_chips(forward_list)
+
+    grad_y = own_rows(grad_rows).astype(jnp.float32)
+    after_own = own_rows(after_attn)
+    after_norm_grad, gain_two_grad = jax.vjp(root_norm, after_own, gains[1])[1](grad_normed_two)
+    grad_after = grad_y + after_norm_grad
+    grad_attn = line_gather(grad_after.astype(jnp.bfloat16)).reshape(tokens, width)
+
+    grad_mixed = lax.dot_general(
+        grad_attn, out_own, (((1,), (1,)), ((), ())), preferred_element_type=jnp.float32
+    )
+    grad_mixed = grad_mixed.astype(jnp.bfloat16).reshape(tokens, local_heads, HEAD_DIM)
+    grad_query, grad_key, grad_value = attend_backward(
+        queries, keys_all, values_all, allowed, log_total, grad_mixed, score_scale
+    )
+    sent_keys, sent_values = from_behind(
+        (grad_key[:half_len].astype(jnp.bfloat16), grad_value[:half_len].astype(jnp.bfloat16)),
+        "ctx",
+        -1,
+    )
+    grad_linear = (
+        jnp.stack(
+            [
+                rotate_back(grad_query, cosine, sine_table),
+                rotate_back(
+                    grad_key[half_len:] + sent_keys.astype(jnp.float32), cosine, sine_table
+                ),
+                grad_value[half_len:] + sent_values.astype(jnp.float32),
+            ],
+            axis=1,
+        )
+        .astype(jnp.bfloat16)
+        .reshape(tokens, 3, local_width)
+    )
+    grad_one_part = jnp.einsum(
+        "tcm,dcm->td", grad_linear, qkv_rel, preferred_element_type=jnp.float32
+    ).astype(jnp.bfloat16)
+    grad_one_rel = line_reduce(grad_one_part.reshape(tp, share, width))
+    grad_normed_one = jnp.concatenate(exchange_order(columns_of(grad_one_rel, 8)), axis=1)
+    residual_norm_grad, gain_one_grad = jax.vjp(root_norm, own_rows(residual), gains[0])[1](
+        grad_normed_one
+    )
+    input_grad = line_gather((grad_after + residual_norm_grad).astype(jnp.bfloat16)).reshape(
+        1, tokens, width
+    )
+
+    layer_own = own_rows(after_attn) + line_reduce(forward_sum.reshape(tp, share, width))
+    layer_out = line_gather(layer_own.astype(jnp.bfloat16)).reshape(1, tokens, width)
+
+    qkv_full = jnp.einsum(
+        "td,tcm->dcm", first_rel, grad_linear, preferred_element_type=jnp.float32
+    ).astype(jnp.bfloat16)
+    rows_each = width // 8
+    qkv_grad = reduce_eight([qkv_full[i * rows_each : (i + 1) * rows_each] for i in range(8)])
+    projection_full = lax.dot_general(
+        mixed_result, grad_attn, (((0,), (0,)), ((), ())), preferred_element_type=jnp.float32
+    ).astype(jnp.bfloat16)
+    projection_grad = reduce_eight(exchange_order(columns_of(projection_full, 8)))
+
+    all_rows = jnp.concatenate([row_parts[i] for p in (0, 1, 4, 5) for i in (p, p + 2)])
+    all_grads = jnp.concatenate([grad_parts[i] for p in (0, 1, 4, 5) for i in (p, p + 2)])
+    inner_grad = lax.dot_general(
+        jnp.concatenate(pre_list),
+        all_rows,
+        (((0,), (0,)), ((), ())),
+        preferred_element_type=jnp.float32,
+    )
+    outer_grad = lax.dot_general(
+        jnp.concatenate(weighted_list),
+        all_grads,
+        (((0,), (0,)), ((), ())),
+        preferred_element_type=jnp.float32,
+    )
+    inner_expert = jnp.transpose(
+        jnp.stack([inner_grad[:hid_e], inner_grad[pad : pad + hid_e]]), (2, 0, 1)
+    )[None]
+    outer_expert = outer_grad[:hid_e][None]
+    shared_grad = jnp.concatenate(
+        [inner_grad[hid_e:hid], inner_grad[pad + hid_e :], outer_grad[hid_e:]]
+    ).astype(jnp.bfloat16)
+    shared_parts = exchange_order(trade_eight(exchange_order(columns_of(shared_grad, 8))))
+    inner_shared = jnp.transpose(
+        jnp.stack(
+            [
+                jnp.concatenate([p[:hid_s] for p in shared_parts]),
+                jnp.concatenate([p[hid_s : 2 * hid_s] for p in shared_parts]),
+            ]
+        ),
+        (2, 0, 1),
+    ).astype(jnp.float32)
+    outer_shared = jnp.concatenate([p[2 * hid_s :] for p in shared_parts]).astype(jnp.float32)
+
+    everywhere = ("fsdp", "ctx", "tp")
+    small = lax.psum(
+        jnp.concatenate(
+            [
+                inner_grad[hid : hid + experts + 1],
+                gain_one_grad[None],
+                gain_two_grad[None],
+            ]
+        ),
+        everywhere,
+    )
+    router_grad = small[:experts].T
+    blend_grad = small[experts]
+    gains_grad = small[experts + 1 :]
+    bias_grad = lax.psum(jnp.sum(grad_linear.astype(jnp.float32), axis=0), ("fsdp", "ctx"))
+    return (
+        layer_out,
+        input_grad,
+        gains_grad,
+        qkv_grad,
+        bias_grad,
+        projection_grad,
+        router_grad,
+        blend_grad,
+        inner_shared,
+        outer_shared,
+        inner_expert,
+        outer_expert,
+    )
+
+
 def solution(mesh):
     placed = (
         P("fsdp", "ctx", None),
@@ -452,8 +939,9 @@
         P(("fsdp", "ctx"), "tp", None),
         P("fsdp", "ctx", None),
     )
+    plan = eight_plan if mesh.shape["fsdp"] == 4 and mesh.shape["ctx"] == 2 else general_plan
     return jax.shard_map(
-        on_device,
+        plan,
         mesh=mesh,
         in_specs=placed,
         out_specs=(

time: 2280 us -> 1550 us (0.68)
  waiting for transfers between devices: 900 us -> 514 us
  blocking collectives: 323 us -> 17.2 us
  starting transfers between devices: 20.3 us -> 193 us
  local copies, waits for them, and re-layouts: 456 us -> 300 us
  other arithmetic: 299 us -> 206 us
  matrix products: 253 us -> 290 us
    psum x3 -> x1, waiting for transfers between devices: 543 us -> 117 us  [eight_plan(): lax.psum(jnp.concatenate([inner_grad[hid:hid + experts + 1], gain_one_gra...]
    ppermute x0 -> x121, waiting for transfers between devices: none -> 396 us  [the longest x18 137 us: swap_y(): return lax.ppermute(values, 'ctx', [(0, 1), (1, 0)])]
    all_to_all x2 -> x0, blocking collectives: 279 us -> none  [the longest x1 150 us: on_device(): lax.all_to_all(dispatch.reshape(groups, expert_local, capacity, width), (...]
    all_to_all x2 -> x1, waiting for transfers between devices: 215 us -> 0.01 us  [eight_plan(): lax.all_to_all(kept_all.T.reshape(experts, 1, tokens), ('fsdp', 'ctx'), s...]
    ppermute x0 -> x121, starting transfers between devices: none -> 180 us  [the longest x15 48.5 us: line_gather(): lax.ppermute(right, 'tp', [(i, i + 1) for i in range(step - 1, count - 1)])]
    gather x10 -> x0, local copies, waits for them, and re-layouts: 167 us -> none  [the longest x4 58.9 us: on_device(): returned[pair_index[:, route_slot]]]
    convert_element_type x5 -> x0, local copies, waits for them, and re-layouts: 133 us -> none  [the longest x1 66.3 us: on_device(): expert_result[None].astype(jnp.bfloat16)]
    unnamed x5 -> x41, other arithmetic: 138 us -> 9.73 us
  transfers between devices with their start and end apart: 17 -> 127, of which waited for: 11 -> 41; matrix products, arithmetic and copies ran while one was open for 29% -> 43% of each run, Pallas kernels for 0% -> 0%
where the time goes in v1:
time: 1550 us; the launch traced here: 1540 us
  waiting for transfers between devices  514 us (33%)
  local copies, waits for them, and re-layouts  300 us (19%)
  matrix products  290 us (19%)
  other arithmetic  206 us (13%)
  starting transfers between devices  193 us (12%)
  between operations  18.6 us (1%)
  blocking collectives  17.2 us (1%)
    ppermute x18, waiting for transfers between devices, swap_y(): return lax.ppermute(values, 'ctx', [(0, 1), (1, 0)])  137 us
    ppermute x15, waiting for transfers between devices, line_gather(): lax.ppermute(left, 'tp', [(i, i - 1) for i in range(1, count - step + 1)])  120 us
    psum x1, waiting for transfers between devices, eight_plan(): lax.psum(jnp.concatenate([inner_grad[hid:hid + experts + 1], gain_one_gra...  117 us
    unnamed x461, local copies, waits for them, and re-layouts  95.9 us
    ppermute x9, waiting for transfers between devices, line_reduce(): lax.ppermute(to_right, 'tp', [(i, i + 1) for i in range(min(step, count -...  67.6 us
    concatenate x4, local copies, waits for them, and re-layouts, mixture_chunk(): jnp.concatenate([scaled * up_pre * slope, grad_logits, grad_blend, jnp.ze...  67.6 us
    ppermute x18, waiting for transfers between devices, swap_x(): return lax.ppermute(values, 'fsdp', [(f, f ^ 2) for f in range(4)])  64.2 us
    ppermute x15, starting transfers between devices, line_gather(): lax.ppermute(right, 'tp', [(i, i + 1) for i in range(step - 1, count - 1)])  48.5 us
  transfers between devices with their start and end apart: 127, of which 41 were waited for; matrix products, arithmetic and copies ran while one was open for 43% of the time, Pallas kernels for 0%

profile of v1, /device:TPU:0, one launch (start us, length us, event | category | flops | bytes accessed | tf_op | source)
XLA Modules:
  0.0 1539.0 jit_solution(6269854310570736463)
XLA Ops:
  72.0 14.0 collective-permute-done.17
  180.3 15.2 collective-permute-done.13
  199.0 17.0 %collective-permute-done.28 = bf16[256,2048]{1,0:T(8,128)(2,1)} collective-permute-done((bf16[256,2048]{1,0:T(8,128)(2,1)}, bf16[256,2048]{1,0:T(8,128)(2,1)}, u32[]{:S(2)}, u32[]{:S(2)}) %collective-permute-start.28) | collective-permute-done | bytes 1048608 | tf_op jit(solution)/shard_map/ppermute | solution.py:549
  221.3 35.6 %collective-permute-done.14 = bf16[704,512]{1,0:T(8,128)(2,1)} collective-permute-done((bf16[704,512]{1,0:T(8,128)(2,1)}, bf16[704,512]{1,0:T(8,128)(2,1)}, u32[]{:S(2)}, u32[]{:S(2)}) %collective-permute-start.14) | collective-permute-done | bytes 720928 | tf_op jit(solution)/shard_map/ppermute | solution.py:549
  265.7 13.7 collective-permute-done.15
  312.4 18.9 %collective-permute-done.36 = bf16[352,2048]{1,0:T(8,128)(2,1)S(1)} collective-permute-done((bf16[352,2048]{1,0:T(8,128)(2,1)S(1)}, bf16[352,2048]{1,0:T(8,128)(2,1)S(1)}, u32[]{:S(2)}, u32[]{:S(2)}) %collective-permute-start.36) | collective-permute-done | bytes 1441824 | tf_op jit(solution)/shard_map/ppermute | solution.py:442
  381.3 26.0 %concatenate.299 = bf16[1168,2048]{1,0:T(8,128)(2,1)} concatenate(bf16[352,2048]{1,0:T(8,128)(2,1)} %get-tuple-element.258, bf16[176,2048]{1,0:T(8,128)(2,1)} %get-tuple-element.266, bf16[8,2048]{1,0:T(8,128)(2,1)S(1)} %bitcast.425, bf16[1,2048]{1,0:T(2,128)(2,1)S(1)} %broadcast_in_dim.723, bf16[103,2048]{1,0:T(8,128)(2,1)S(1)} %broadcast_in_dim.724, ...), dimensions={0} | concatenate | bytes 9568256 | tf_op jit(solution)/shard_map/concatenate | solution.py:757
  456.0 20.0 %collective-permute-done.45 = bf16[352,2048]{1,0:T(8,128)(2,1)S(1)} collective-permute-done((bf16[352,2048]{1,0:T(8,128)(2,1)S(1)}, bf16[352,2048]{1,0:T(8,128)(2,1)S(1)}, u32[]{:S(2)}, u32[]{:S(2)}) %collective-permute-start.45) | collective-permute-done | bytes 1441824 | tf_op jit(solution)/shard_map/ppermute | solution.py:450
  491.3 13.3 fusion.26
  504.8 13.3 fusion.30
  520.9 17.1 %select_reduce_fusion.6 = (f32[1408]{0:T(1024)S(1)}, f32[1408]{0:T(1024)S(1)}, f32[1408]{0:T(1024)S(1)}, f32[1408]{0:T(1024)S(1)}, f32[1408]{0:T(1024)S(1)}, /*i...) fusion(pred[528]{0:T(1024)(128)(4,1)S(1)} %iota_compare_fusion., ...), kind=kOutput, calls=%fused_computation.131 | convolution fusion | flops 3096596480 | bytes 49607184 | tf_op jit(solution)/shard_map/dot_general | solution.py:587
  544.5 11.3 multiply_convert_fusion.6
  555.8 20.1 %concatenate.313 = bf16[1408,1168]{0,1:T(8,128)(2,1)} concatenate(bf16[1408,528]{0,1:T(8,128)(2,1)} %get-tuple-element.390, bf16[1408,8]{0,1:T(8,128)(2,1)S(1)} %get-tuple-element.394, bf16[1408,1]{0,1:T(2,128)(2,1)S(1)} %get-tuple-element.157, bf16[1408,103]{0,1:T(8,128)(2,1)S(1)} %broadcast.1060, bf16[1408,528]{0,1:T(8,128)(2,1)} %get-tuple-element.391), dimensions={1} | concatenate | bytes 6578176 | tf_op jit(solution)/shard_map/concatenate | solution.py:606
  600.8 20.1 %concatenate.316 = bf16[1408,1168]{0,1:T(8,128)(2,1)} concatenate(bf16[1408,528]{0,1:T(8,128)(2,1)} %get-tuple-element.387, bf16[1408,8]{0,1:T(8,128)(2,1)S(1)} %multiply_convert_fusion.14, bf16[1408,1]{0,1:T(2,128)(2,1)S(1)} %get-tuple-element.159, bf16[1408,103]{0,1:T(8,128)(2,1)S(1)} %broadcast.1060, bf16[1408,528]{0,1:T(8,128)(2,1)} %get-tuple-element.388), dimensions={1} | concatenate | bytes 6578176 | tf_op jit(solution)/shard_map/concatenate | solution.py:606
  635.4 13.7 concatenate.311
  663.7 13.8 concatenate.309
  703.5 13.9 collective-permute-done.57
  720.3 13.8 collective-permute-done.53
  763.4 31.5 %collective-permute-done.58 = bf16[704,2048]{1,0:T(8,128)(2,1)S(1)} collective-permute-done((bf16[704,2048]{1,0:T(8,128)(2,1)}, bf16[704,2048]{1,0:T(8,128)(2,1)S(1)}, u32[]{:S(2)}, u32[]{:S(2)}) %collective-permute-start.58) | collective-permute-done | bytes 2883616 | tf_op jit(solution)/shard_map/ppermute | solution.py:450
  847.2 39.0 %fusion.234 = (bf16[1168,2048]{1,0:T(8,128)(2,1)}, f32[1168,2048]{1,0:T(8,128)}) fusion(bf16[5632,2048]{1,0:T(8,128)(2,1)} %constant_dynamic-update-slice_fusion.23, bf16[1408,1168]{0,1:T(8,128)(2,1)} %concatenate.313, bf16[1408,1168]{0,1:T(8,128)(2,1)} %concatenate.311, bf16[1408,1168]{0,1:T(8,128)(2,1)} %concatenate.316, bf16[1408,1168]{0,1:T(8,128)(2,1)} %concatenate.309), kind=kOutput, calls=%fused_computation.762 | convolution fusion | flops 26999226368 | bytes 50577408 | tf_op jit(solution)/shard_map/dot_general | solution.py:862
  904.4 25.5 %collective-permute-done.62 = bf16[352,2048]{1,0:T(8,128)(2,1)S(1)} collective-permute-done((bf16[352,2048]{1,0:T(8,128)(2,1)S(1)}, bf16[352,2048]{1,0:T(8,128)(2,1)S(1)}, u32[]{:S(2)}, u32[]{:S(2)}) %collective-permute-start.62) | collective-permute-done | bytes 1441824 | tf_op jit(solution)/shard_map/ppermute | solution.py:450
  932.6 19.8 %fusion.10 = f32[528,2048]{1,0:T(8,128)} fusion(bf16[5632,2048]{1,0:T(8,128)(2,1)} %constant_dynamic-update-slice_fusion.32, bf16[1408,528]{0,1:T(8,128)(2,1)} %get-tuple-element.389, bf16[1408,528]{0,1:T(8,128)(2,1)S(1)} %copy-done.84, bf16[1408,528]{0,1:T(8,128)(2,1)} %get-tuple-element.386, bf16[1408,528]{0,1:T(8,128)(2,1)} %get-tuple-element.370), kind=kOutput, calls=%fused_computation.24 | convolution fusion | flops 12204048384 | bytes 33341440 | tf_op jit(solution)/shard_map/dot_general | solution.py:868
  964.2 27.0 %collective-permute-done.66 = bf16[704,2048]{1,0:T(8,128)(2,1)} collective-permute-done((bf16[704,2048]{1,0:T(8,128)(2,1)}, bf16[704,2048]{1,0:T(8,128)(2,1)}, u32[]{:S(2)}, u32[]{:S(2)}) %collective-permute-start.66) | collective-permute-done | bytes 2883616 | tf_op jit(solution)/shard_map/ppermute | solution.py:450
  1009.0 13.5 collective-permute-done.67
  1093.0 15.7 %collective-permute-start.85 = (bf16[176,2048]{1,0:T(8,128)(2,1)S(1)}, bf16[176,2048]{1,0:T(8,128)(2,1)S(1)}, u32[]{:S(2)}, u32[]{:S(2)}) collective-permute-start(bf16[176,2048]{1,0:T(8,128)(2,1)S(1)} %get-tuple-element.151), channel_id=1, source_target_pairs={{0,1},{1,2},{2,3},{4,5},{5,6},{6,7},{8,9},{9,10},{10,11},{12,13},{... | collective-permute-start | bytes 2162696 | tf_op jit(solution)/shard_map/ppermute | solution.py:548
  1121.9 14.2 collective-permute-done.89
  1176.3 12.6 multiply_reduce_fusion
  1188.9 11.6 multiply_convert_fusion
  1292.0 20.1 %collective-permute-start.95 = (bf16[176,2048]{1,0:T(8,128)(2,1)S(1)}, bf16[176,2048]{1,0:T(8,128)(2,1)S(1)}, u32[]{:S(2)}, u32[]{:S(2)}) collective-permute-start(bf16[176,2048]{1,0:T(8,128)(2,1)S(1)} %get-tuple-element.237), channel_id=1, source_target_pairs={{0,1},{1,2},{2,3},{4,5},{5,6},{6,7},{8,9},{9,10},{10,11},{12,13},{... | collective-permute-start | bytes 2162696 | tf_op jit(solution)/shard_map/ppermute | solution.py:566
  1316.7 11.4 collective-permute-done.95
  1376.9 17.2 %psum.15 = f32[3,512]{1,0:T(4,128)} all-reduce(f32[3,512]{1,0:T(4,128)S(1)} %convert_reduce_fusion), channel_id=1, replica_groups=mesh['fsdp'=4,'ctx'=2,'tp'=4] {'fsdp','ctx'}, use_global_device_ids=true, to_apply=%region_38.39 | all-reduce | flops 1536 | bytes 12288 | tf_op jit(solution)/shard_map/psum | solution.py:907
  1400.3 117.3 %all-reduce.2.cloned.1.call-done = f32[11,2048]{1,0:T(8,128)} async-done(((f32[11,2048]{1,0:T(8,128)}), f32[11,2048]{1,0:T(8,128)}) %all-reduce.2.cloned.1.call-update) | async-done | bytes 90128 | tf_op jit(solution)/shard_map/psum | solution.py:894
  (1024 shorter events, 833.4 us)
Async XLA Ops:
  95.1 62.5 %collective-permute-start.34 = (bf16[2112,256]{1,0:T(8,128)(2,1)}, bf16[2112,256]{1,0:T(8,128)(2,1)}, u32[]{:S(2)}, u32[]{:S(2)}) collective-permute-start(bf16[2112,256]{1,0:T(8,128)(2,1)} %pad_maximum_fusion.11), channel_id=1, source_target_pairs={{0,8},{8,0},{16,24},{24,16},{1,9},{9,1},{17,25},{25,17},{2,10},{10... | collective-permute-start | bytes 3244040 | tf_op jit(solution)/shard_map/ppermute | solution.py:446
  127.6 48.0 %collective-permute-start.27 = (bf16[256,2048]{1,0:T(8,128)(2,1)}, bf16[256,2048]{1,0:T(8,128)(2,1)}, u32[]{:S(2)}, u32[]{:S(2)}) collective-permute-start(bf16[256,2048]{1,0:T(8,128)(2,1)} %constant_dynamic-slice_fusion), channel_id=1, source_target_pairs={{1,0},{2,1},{3,2},{5,4},{6,5},{7,6},{9,8},{10,9},{11,10},{13,12},{... | collective-permute-start | bytes 3145736 | tf_op jit(solution)/shard_map/ppermute | solution.py:549
  128.9 48.1 %collective-permute-start.24 = (bf16[256,2048]{1,0:T(8,128)(2,1)}, bf16[256,2048]{1,0:T(8,128)(2,1)}, u32[]{:S(2)}, u32[]{:S(2)}) collective-permute-start(bf16[256,2048]{1,0:T(8,128)(2,1)} %constant_dynamic-slice_fusion), channel_id=1, source_target_pairs={{0,1},{1,2},{2,3},{4,5},{5,6},{6,7},{8,9},{9,10},{10,11},{12,13},{... | collective-permute-start | bytes 3145736 | tf_op jit(solution)/shard_map/ppermute | solution.py:548
  163.6 96.3 %collective-permute-start.35 = (bf16[704,2048]{1,0:T(8,128)(2,1)}, bf16[704,2048]{1,0:T(8,128)(2,1)}, u32[]{:S(2)}, u32[]{:S(2)}) collective-permute-start(bf16[704,2048]{1,0:T(8,128)(2,1)} %bitcast.23), channel_id=1, source_target_pairs={{0,4},{4,0},{1,5},{5,1},{2,6},{6,2},{3,7},{7,3},{8,12},{12,8},{9,1... | collective-permute-start | bytes 8650760 | tf_op jit(solution)/shard_map/ppermute | solution.py:450
  178.6 102.3 %collective-permute-start.37 = (bf16[704,2048]{1,0:T(8,128)(2,1)}, bf16[704,2048]{1,0:T(8,128)(2,1)}, u32[]{:S(2)}, u32[]{:S(2)}) collective-permute-start(bf16[704,2048]{1,0:T(8,128)(2,1)} %bitcast.23), channel_id=1, source_target_pairs={{0,16},{8,24},{16,0},{24,8},{1,17},{9,25},{17,1},{25,9},{2,18},{10... | collective-permute-start | bytes 8650760 | tf_op jit(solution)/shard_map/ppermute | solution.py:442
  259.9 46.4 %collective-permute-start.55 = (bf16[704,2048]{1,0:T(8,128)(2,1)}, bf16[704,2048]{1,0:T(8,128)(2,1)}, u32[]{:S(2)}, u32[]{:S(2)}) collective-permute-start(bf16[704,2048]{1,0:T(8,128)(2,1)} %collective-permute-done.35), channel_id=1, source_target_pairs={{0,8},{8,0},{16,24},{24,16},{1,9},{9,1},{17,25},{25,17},{2,10},{10... | collective-permute-start | bytes 8650760 | tf_op jit(solution)/shard_map/ppermute | solution.py:446
  265.6 77.9 %collective-permute-start.30 = (bf16[4,256,2048]{2,1,0:T(8,128)(2,1)}, bf16[4,256,2048]{2,1,0:T(8,128)(2,1)}, u32[]{:S(2)}, u32[]{:S(2)}) collective-permute-start(bf16[4,256,2048]{2,1,0:T(8,128)(2,1)} %select_select_fusion), channel_id=1, source_target_pairs={{0,8},{8,0},{16,24},{24,16},{1,9},{9,1},{17,25},{25,17},{2,10},{10... | collective-permute-start | bytes 12582920 | tf_op jit(solution)/shard_map/ppermute | solution.py:446
  282.2 95.9 %all-to-all-start = ((f32[8,1,704]{2,1,0:T(1,128)}), f32[8,1,704]{2,1,0:T(1,128)S(1)}, u32[]{:S(2)}, u32[]{:S(2)}) async-start(f32[8,1,704]{2,1,0:T(1,128)} %copy.73), calls=%async_computation | async-start | bytes 49152 | tf_op jit(solution)/shard_map/all_to_all | solution.py:669
  285.5 1232.0 %all-reduce.2.cloned.1.call-start = ((), (), s32[]{:S(2)}) async-start(), calls=%async_computation.1 | async-start | bytes 262144 | tf_op jit(solution)/shard_map/psum | solution.py:894
  335.8 97.6 %collective-permute-start.51 = (bf16[704,2048]{1,0:T(8,128)(2,1)}, bf16[704,2048]{1,0:T(8,128)(2,1)}, u32[]{:S(2)}, u32[]{:S(2)}) collective-permute-start(bf16[704,2048]{1,0:T(8,128)(2,1)} %get-tuple-element.273), channel_id=1, source_target_pairs={{0,8},{8,0},{16,24},{24,16},{1,9},{9,1},{17,25},{25,17},{2,10},{10... | collective-permute-start | bytes 8650760 | tf_op jit(solution)/shard_map/ppermute | solution.py:446
  369.9 63.5 %collective-permute-start.40 = (bf16[704,2048]{1,0:T(8,128)(2,1)S(1)}, bf16[704,2048]{1,0:T(8,128)(2,1)}, u32[]{:S(2)}, u32[]{:S(2)}) collective-permute-start(bf16[704,2048]{1,0:T(8,128)(2,1)S(1)} %multiply_convert_fusion.1), channel_id=1, source_target_pairs={{0,4},{4,0},{1,5},{5,1},{2,6},{6,2},{3,7},{7,3},{8,12},{12,8},{9,1... | collective-permute-start | bytes 8650760 | tf_op jit(solution)/shard_map/ppermute | solution.py:450
  377.5 63.3 %collective-permute-start.42 = (bf16[704,2048]{1,0:T(8,128)(2,1)S(1)}, bf16[704,2048]{1,0:T(8,128)(2,1)}, u32[]{:S(2)}, u32[]{:S(2)}) collective-permute-start(bf16[704,2048]{1,0:T(8,128)(2,1)S(1)} %multiply_convert_fusion.1), channel_id=1, source_target_pairs={{0,16},{8,24},{16,0},{24,8},{1,17},{9,25},{17,1},{25,9},{2,18},{10... | collective-permute-start | bytes 8650760 | tf_op jit(solution)/shard_map/ppermute | solution.py:442
  378.1 67.8 %collective-permute-start.39 = (bf16[704,2048]{1,0:T(8,128)(2,1)S(1)}, bf16[704,2048]{1,0:T(8,128)(2,1)}, u32[]{:S(2)}, u32[]{:S(2)}) collective-permute-start(bf16[704,2048]{1,0:T(8,128)(2,1)S(1)} %multiply_convert_fusion.1), channel_id=1, source_target_pairs={{0,8},{8,0},{16,24},{24,16},{1,9},{9,1},{17,25},{25,17},{2,10},{10... | collective-permute-start | bytes 8650760 | tf_op jit(solution)/shard_map/ppermute | solution.py:446
  433.4 47.2 %collective-permute-start.41 = (bf16[704,2048]{1,0:T(8,128)(2,1)}, bf16[704,2048]{1,0:T(8,128)(2,1)S(1)}, u32[]{:S(2)}, u32[]{:S(2)}) collective-permute-start(bf16[704,2048]{1,0:T(8,128)(2,1)} %collective-permute-done.40), channel_id=1, source_target_pairs={{0,8},{8,0},{16,24},{24,16},{1,9},{9,1},{17,25},{25,17},{2,10},{10... | collective-permute-start | bytes 8650760 | tf_op jit(solution)/shard_map/ppermute | solution.py:446
  591.0 86.5 %collective-permute-start.52 = (bf16[704,2048]{1,0:T(8,128)(2,1)}, bf16[704,2048]{1,0:T(8,128)(2,1)}, u32[]{:S(2)}, u32[]{:S(2)}) collective-permute-start(bf16[704,2048]{1,0:T(8,128)(2,1)} %slice.969), channel_id=1, source_target_pairs={{0,8},{8,0},{16,24},{24,16},{1,9},{9,1},{17,25},{25,17},{2,10},{10... | collective-permute-start | bytes 8650760 | tf_op jit(solution)/shard_map/ppermute | solution.py:446
  634.9 60.0 %collective-permute-start.56 = (bf16[704,2048]{1,0:T(8,128)(2,1)}, bf16[704,2048]{1,0:T(8,128)(2,1)}, u32[]{:S(2)}, u32[]{:S(2)}) collective-permute-start(bf16[704,2048]{1,0:T(8,128)(2,1)} %slice.972), channel_id=1, source_target_pairs={{0,8},{8,0},{16,24},{24,16},{1,9},{9,1},{17,25},{25,17},{2,10},{10... | collective-permute-start | bytes 8650760 | tf_op jit(solution)/shard_map/ppermute | solution.py:446
  694.4 69.0 %collective-permute-start.48 = (bf16[704,2048]{1,0:T(8,128)(2,1)S(1)}, bf16[704,2048]{1,0:T(8,128)(2,1)S(1)}, u32[]{:S(2)}, u32[]{:S(2)}) collective-permute-start(bf16[704,2048]{1,0:T(8,128)(2,1)S(1)} %slice.963), channel_id=1, source_target_pairs={{0,8},{8,0},{16,24},{24,16},{1,9},{9,1},{17,25},{25,17},{2,10},{10... | collective-permute-start | bytes 8650760 | tf_op jit(solution)/shard_map/ppermute | solution.py:446
  719.7 75.2 %collective-permute-start.58 = (bf16[704,2048]{1,0:T(8,128)(2,1)}, bf16[704,2048]{1,0:T(8,128)(2,1)S(1)}, u32[]{:S(2)}, u32[]{:S(2)}) collective-permute-start(bf16[704,2048]{1,0:T(8,128)(2,1)} %pad_maximum_fusion.3), channel_id=1, source_target_pairs={{0,4},{4,0},{1,5},{5,1},{2,6},{6,2},{3,7},{7,3},{8,12},{12,8},{9,1... | collective-permute-start | bytes 8650760 | tf_op jit(solution)/shard_map/ppermute | solution.py:450
  736.5 63.0 %collective-permute-start.54 = (bf16[704,2048]{1,0:T(8,128)(2,1)}, bf16[704,2048]{1,0:T(8,128)(2,1)}, u32[]{:S(2)}, u32[]{:S(2)}) collective-permute-start(bf16[704,2048]{1,0:T(8,128)(2,1)} %pad_maximum_fusion.2), channel_id=1, source_target_pairs={{0,16},{8,24},{16,0},{24,8},{1,17},{9,25},{17,1},{25,9},{2,18},{10... | collective-permute-start | bytes 8650760 | tf_op jit(solution)/shard_map/ppermute | solution.py:442
  839.9 50.2 %collective-permute-start.64 = (bf16[704,2048]{1,0:T(8,128)(2,1)}, bf16[704,2048]{1,0:T(8,128)(2,1)}, u32[]{:S(2)}, u32[]{:S(2)}) collective-permute-start(bf16[704,2048]{1,0:T(8,128)(2,1)} %slice.778), channel_id=1, source_target_pairs={{0,8},{8,0},{16,24},{24,16},{1,9},{9,1},{17,25},{25,17},{2,10},{10... | collective-permute-start | bytes 8650760 | tf_op jit(solution)/shard_map/ppermute | solution.py:446
  841.8 54.3 %collective-permute-start.60 = (bf16[704,2048]{1,0:T(8,128)(2,1)}, bf16[704,2048]{1,0:T(8,128)(2,1)}, u32[]{:S(2)}, u32[]{:S(2)}) collective-permute-start(bf16[704,2048]{1,0:T(8,128)(2,1)} %slice.771), channel_id=1, source_target_pairs={{0,8},{8,0},{16,24},{24,16},{1,9},{9,1},{17,25},{25,17},{2,10},{10... | collective-permute-start | bytes 8650760 | tf_op jit(solution)/shard_map/ppermute | solution.py:446
  845.4 53.9 %collective-permute-start.65 = (bf16[352,2048]{1,0:T(8,128)(2,1)}, bf16[352,2048]{1,0:T(8,128)(2,1)}, u32[]{:S(2)}, u32[]{:S(2)}) collective-permute-start(bf16[352,2048]{1,0:T(8,128)(2,1)} %get-tuple-element.250), channel_id=1, source_target_pairs={{0,16},{8,24},{16,0},{24,8},{1,17},{9,25},{17,1},{25,9},{2,18},{10... | collective-permute-start | bytes 4325384 | tf_op jit(solution)/shard_map/ppermute | solution.py:442
  890.1 74.1 %collective-permute-start.59 = (bf16[704,2048]{1,0:T(8,128)(2,1)}, bf16[704,2048]{1,0:T(8,128)(2,1)}, u32[]{:S(2)}, u32[]{:S(2)}) collective-permute-start(bf16[704,2048]{1,0:T(8,128)(2,1)} %slice.769), channel_id=1, source_target_pairs={{0,8},{8,0},{16,24},{24,16},{1,9},{9,1},{17,25},{25,17},{2,10},{10... | collective-permute-start | bytes 8650760 | tf_op jit(solution)/shard_map/ppermute | solution.py:446
  903.0 88.3 %collective-permute-start.66 = (bf16[704,2048]{1,0:T(8,128)(2,1)}, bf16[704,2048]{1,0:T(8,128)(2,1)}, u32[]{:S(2)}, u32[]{:S(2)}) collective-permute-start(bf16[704,2048]{1,0:T(8,128)(2,1)} %pad_maximum_fusion.5), channel_id=1, source_target_pairs={{0,4},{4,0},{1,5},{5,1},{2,6},{6,2},{3,7},{7,3},{8,12},{12,8},{9,1... | collective-permute-start | bytes 8650760 | tf_op jit(solution)/shard_map/ppermute | solution.py:450
  932.3 65.7 %collective-permute-start.63 = (bf16[704,2048]{1,0:T(8,128)(2,1)}, bf16[704,2048]{1,0:T(8,128)(2,1)}, u32[]{:S(2)}, u32[]{:S(2)}) collective-permute-start(bf16[704,2048]{1,0:T(8,128)(2,1)} %pad_maximum_fusion.4), channel_id=1, source_target_pairs={{0,16},{8,24},{16,0},{24,8},{1,17},{9,25},{17,1},{25,9},{2,18},{10... | collective-permute-start | bytes 8650760 | tf_op jit(solution)/shard_map/ppermute | solution.py:442
  956.7 95.0 %collective-permute-start.122 = (bf16[1056,256]{1,0:T(8,128)(2,1)}, bf16[1056,256]{1,0:T(8,128)(2,1)S(1)}, u32[]{:S(2)}, u32[]{:S(2)}) collective-permute-start(bf16[1056,256]{1,0:T(8,128)(2,1)} %pad_maximum_fusion.23), channel_id=1, source_target_pairs={{0,16},{8,24},{16,0},{24,8},{1,17},{9,25},{17,1},{25,9},{2,18},{10... | collective-permute-start | bytes 1622024 | tf_op jit(solution)/shard_map/ppermute | solution.py:442
  1065.4 47.3 %collective-permute-start.124 = (bf16[2112,256]{1,0:T(8,128)(2,1)S(1)}, bf16[2112,256]{1,0:T(8,128)(2,1)S(1)}, u32[]{:S(2)}, u32[]{:S(2)}) collective-permute-start(bf16[2112,256]{1,0:T(8,128)(2,1)S(1)} %pad_maximum_fusion.12), channel_id=1, source_target_pairs={{0,8},{8,0},{16,24},{24,16},{1,9},{9,1},{17,25},{25,17},{2,10},{10... | collective-permute-start | bytes 3244040 | tf_op jit(solution)/shard_map/ppermute | solution.py:446
  1140.8 111.5 %collective-permute-start.76 = (bf16[176,2048]{1,0:T(8,128)(2,1)}, bf16[176,2048]{1,0:T(8,128)(2,1)}, u32[]{:S(2)}, u32[]{:S(2)}) collective-permute-start(bf16[176,2048]{1,0:T(8,128)(2,1)} %get-tuple-element.227), channel_id=1, source_target_pairs={{1,0},{2,1},{3,2},{5,4},{6,5},{7,6},{9,8},{10,9},{11,10},{13,12},{... | collective-permute-start | bytes 2162696 | tf_op jit(solution)/shard_map/ppermute | solution.py:549
  1142.3 111.3 %collective-permute-start.73 = (bf16[176,2048]{1,0:T(8,128)(2,1)}, bf16[176,2048]{1,0:T(8,128)(2,1)}, u32[]{:S(2)}, u32[]{:S(2)}) collective-permute-start(bf16[176,2048]{1,0:T(8,128)(2,1)} %get-tuple-element.227), channel_id=1, source_target_pairs={{0,1},{1,2},{2,3},{4,5},{5,6},{6,7},{8,9},{9,10},{10,11},{12,13},{... | collective-permute-start | bytes 2162696 | tf_op jit(solution)/shard_map/ppermute | solution.py:548
  1253.6 58.5 %collective-permute-start.74 = (bf16[176,2048]{1,0:T(8,128)(2,1)}, bf16[176,2048]{1,0:T(8,128)(2,1)S(1)}, u32[]{:S(2)}, u32[]{:S(2)}) collective-permute-start(bf16[176,2048]{1,0:T(8,128)(2,1)} %collective-permute-done.73), channel_id=1, source_target_pairs={{1,2},{2,3},{5,6},{6,7},{9,10},{10,11},{13,14},{14,15},{17,18},{18... | collective-permute-start | bytes 2162696 | tf_op jit(solution)/shard_map/ppermute | solution.py:548
  1394.8 127.1 %collective-permute-start.104 = (bf16[176,2048]{1,0:T(8,128)(2,1)}, bf16[176,2048]{1,0:T(8,128)(2,1)S(1)}, u32[]{:S(2)}, u32[]{:S(2)}) collective-permute-start(bf16[176,2048]{1,0:T(8,128)(2,1)} %collective-permute-done.103), channel_id=1, source_target_pairs={{1,0},{5,4},{9,8},{13,12},{17,16},{21,20},{25,24},{29,28}} | collective-permute-start | bytes 2162696 | tf_op jit(solution)/shard_map/ppermute | solution.py:549
  1396.1 125.8 %collective-permute-start.101 = (bf16[176,2048]{1,0:T(8,128)(2,1)}, bf16[176,2048]{1,0:T(8,128)(2,1)S(1)}, u32[]{:S(2)}, u32[]{:S(2)}) collective-permute-start(bf16[176,2048]{1,0:T(8,128)(2,1)} %collective-permute-done.100), channel_id=1, source_target_pairs={{2,3},{6,7},{10,11},{14,15},{18,19},{22,23},{26,27},{30,31}} | collective-permute-start | bytes 2162696 | tf_op jit(solution)/shard_map/ppermute | solution.py:548
  (308 other events, 6171.0 us)
Sparse Core Ops, SparseCore 0:
  1394.9 122.5 all-reduce.1

commit v2 on v0

--- a/solution.py
+++ b/solution.py
@@ -3,6 +3,8 @@
 import jax
 import jax.numpy as jnp
 from jax import lax
+from jax.experimental import pallas as pl
+from jax.experimental.pallas import tpu as pltpu
 from jax.sharding import PartitionSpec as P
 
 HEAD_DIM = 128
@@ -107,7 +109,7 @@
     return (grad_queries, grad_keys, grad_values)
 
 
-def on_device(
+def general_plan(
     hidden_in,
     doc_lengths,
     expert_ids,
@@ -434,6 +436,1170 @@
     )
 
 
+VMEM = pl.BlockSpec(memory_space=pltpu.VMEM)
+SMEM = pl.BlockSpec(memory_space=pltpu.SMEM)
+ANY = pl.BlockSpec(memory_space=pl.ANY)
+ROWS_COLS = (((1,), (0,)), ((), ()))
+ROWS_ROWS = (((1,), (1,)), ((), ()))
+COLS_COLS = (((0,), (0,)), ((), ()))
+
+
+def product(one, other, dims=ROWS_COLS):
+    return lax.dot_general(one, other, dims, preferred_element_type=jnp.float32)
+
+
+def call(kernel, shapes, flops, moved, **others):
+    return pl.pallas_call(
+        kernel,
+        out_shape=shapes,
+        compiler_params=pltpu.CompilerParams(vmem_limit_bytes=40 * 2**20),
+        cost_estimate=pl.CostEstimate(
+            flops=int(flops), bytes_accessed=int(moved), transcendentals=0
+        ),
+        **others,
+    )
+
+
+def after(values, *earlier):
+    return lax.optimization_barrier((values, earlier))[0]
+
+
+def swap_x(values):
+    return lax.ppermute(values, "fsdp", [(f, f ^ 2) for f in range(4)])
+
+
+def swap_core(values):
+    return lax.ppermute(values, "fsdp", [(f, f ^ 1) for f in range(4)])
+
+
+def swap_y(values):
+    return lax.ppermute(values, "ctx", [(0, 1), (1, 0)])
+
+
+def own_number():
+    return lax.axis_index("fsdp") * 2 + lax.axis_index("ctx")
+
+
+def exchange_order(parts):
+    number = own_number()
+    for bit in (4, 2, 1):
+        taken = (number & bit) != 0
+        parts = [jnp.where(taken, parts[i ^ bit], parts[i]) for i in range(8)]
+    return parts
+
+
+def add_low(one, other):
+    return (one.astype(jnp.float32) + other.astype(jnp.float32)).astype(jnp.bfloat16)
+
+
+def halves_sum(own, arrived):
+    half = own.shape[0] // 2
+    return add_low(own[:half], arrived[:half]), add_low(own[half:], arrived[half:])
+
+
+def first_hops(taken):
+    return swap_x(taken[1][0]), swap_y(taken[2][1]), swap_x(taken[3][0]), swap_y(taken[3][1])
+
+
+def last_hops(taken, hops):
+    _, _, both_low, both_high = hops
+    for_x, for_y = add_low(taken[1][1], both_high), add_low(taken[2][0], both_low)
+    return swap_x(for_x), swap_y(for_y)
+
+
+def hops_sum(taken, hops, ends):
+    x_low, y_high, _, _ = hops
+    x_high, y_low = ends
+    sums = [
+        mine.astype(jnp.float32) + along_x.astype(jnp.float32) + along_y.astype(jnp.float32)
+        for mine, along_x, along_y in ((taken[0][0], x_low, y_low), (taken[0][1], x_high, y_high))
+    ]
+    return jnp.concatenate(sums).astype(jnp.bfloat16)
+
+
+def sum_over(values, with_tp):
+    values = values + swap_core(values)
+    values = values + swap_x(values)
+    values = values + swap_y(values)
+    if with_tp:
+        count = lax.axis_size("tp")
+        bit = 1
+        while bit < count:
+            values = values + lax.ppermute(values, "tp", [(i, i ^ bit) for i in range(count)])
+            bit *= 2
+    return values
+
+
+def line_reduce(rows):
+    count = lax.axis_size("tp")
+    blocks = rows.reshape((count, rows.shape[0] // count) + rows.shape[1:])
+    arrived = lax.all_to_all(blocks, "tp", split_axis=0, concat_axis=0, tiled=True)
+    return jnp.sum(arrived.astype(jnp.float32), axis=0)
+
+
+def line_gather(block):
+    copies = jnp.broadcast_to(block[None], (lax.axis_size("tp"),) + block.shape)
+    return lax.all_to_all(copies, "tp", split_axis=0, concat_axis=0, tiled=True)
+
+
+def pick(blocks, index):
+    return lax.dynamic_index_in_dim(blocks, index, axis=0, keepdims=False)
+
+
+def hop_reduce(rows):
+    count = lax.axis_size("tp")
+    me = lax.axis_index("tp")
+    blocks = rows.reshape((count, rows.shape[0] // count) + rows.shape[1:])
+    right, left = None, None
+    for step in range(1, count):
+        to_right = pick(blocks, jnp.minimum(count - step + me, count - 1))
+        to_left = pick(blocks, jnp.maximum(step + me - count, 0))
+        if step > 1:
+            to_right, to_left = add_low(to_right, right), add_low(to_left, left)
+        right = lax.ppermute(to_right, "tp", [(i, i + 1) for i in range(min(step, count - 1))])
+        left = lax.ppermute(
+            to_left, "tp", [(i, i - 1) for i in range(max(count - step, 1), count)]
+        )
+    return (
+        pick(blocks, me).astype(jnp.float32)
+        + right.astype(jnp.float32)
+        + left.astype(jnp.float32)
+    )
+
+
+def hop_gather(block):
+    count = lax.axis_size("tp")
+    me = lax.axis_index("tp")
+    right, left = [block], [block]
+    for step in range(1, count):
+        right.append(
+            lax.ppermute(right[-1], "tp", [(i, i + 1) for i in range(step - 1, count - 1)])
+        )
+        left.append(
+            lax.ppermute(left[-1], "tp", [(i, i - 1) for i in range(1, count - step + 1)])
+        )
+    result = []
+    for place in range(count):
+        taken = block
+        for step in range(1, count):
+            taken = jnp.where(place == me - step, right[step], taken)
+            taken = jnp.where(place == me + step, left[step], taken)
+        result.append(taken)
+    return jnp.concatenate(result)
+
+
+def hop_trade(parts):
+    rows = parts[0].shape[0]
+    from_y = swap_y(jnp.concatenate([parts[1], parts[3]]))
+    from_x = swap_x(jnp.concatenate([parts[4], parts[6]]))
+    both = lax.ppermute(
+        jnp.concatenate([parts[5], parts[7]]),
+        ("fsdp", "ctx"),
+        [(d, d ^ 5) for d in range(8)],
+    )
+    sibling = swap_core(
+        jnp.concatenate([parts[2], from_y[rows:], from_x[rows:], both[rows:]])
+    )
+    return [
+        parts[0],
+        from_y[:rows],
+        sibling[:rows],
+        sibling[rows : 2 * rows],
+        from_x[:rows],
+        both[:rows],
+        sibling[2 * rows : 3 * rows],
+        sibling[3 * rows :],
+    ]
+
+
+def columns_of(values, count):
+    wide = values.shape[1] // count
+    return [values[:, i * wide : (i + 1) * wide] for i in range(count)]
+
+
+def block_columns(index, wide):
+    return pl.ds(pl.multiple_of(index * wide, wide), wide)
+
+
+def turn(values, cosine, signed_sine):
+    return values * cosine + pltpu.roll(values, HEAD_DIM // 2, 1) * signed_sine
+
+
+def pieces_of(lists):
+    flat, places = [], []
+    for pieces in lists:
+        places.append(range(len(flat), len(flat) + len(pieces)))
+        flat += pieces
+    return flat, places
+
+
+def project(number, hidden, gain, weights, bias, cosine, signed_sine):
+    tokens, width = hidden.shape
+    local_width = bias.shape[2]
+    deep = width // 8
+
+    flat, places = pieces_of(weights)
+
+    def kernel(number_ref, hidden_ref, gain_ref, bias_ref, cos_ref, sin_ref, *others):
+        weight_refs, (out_ref, normed_ref) = others[: len(flat)], others[len(flat) :]
+        part = pl.program_id(0)
+
+        @pl.when(part == 0)
+        def _():
+            values = hidden_ref[...].astype(jnp.float32)
+            normed_ref[...] = root_norm(values, gain_ref[...]).astype(jnp.bfloat16)
+
+        total = None
+        for r in range(8):
+            rows = normed_ref[:, block_columns(number_ref[0] ^ r, deep)]
+            terms = [product(rows, weight_refs[at][0]) for at in places[r]]
+            term = terms[0] if len(terms) == 1 else jnp.concatenate(terms, axis=1)
+            total = term if total is None else total + term
+        total = total + bias_ref[0]
+        cosine_now = jnp.where(part < 2, cos_ref[...], 1.0)
+        sine_now = jnp.where(part < 2, sin_ref[...], 0.0)
+        for h in range(local_width // HEAD_DIM):
+            at = slice(h * HEAD_DIM, (h + 1) * HEAD_DIM)
+            out_ref[0, :, at] = turn(total[:, at], cosine_now, sine_now).astype(jnp.bfloat16)
+
+    whole = lambda *shape: pl.BlockSpec(shape, lambda c: (0,) * len(shape))
+    return call(
+        kernel,
+        [
+            jax.ShapeDtypeStruct((3, tokens, local_width), jnp.bfloat16),
+            jax.ShapeDtypeStruct((tokens, width), jnp.bfloat16),
+        ],
+        2 * tokens * width * 3 * local_width,
+        2 * (2 * tokens * width + 3 * width * local_width + 3 * tokens * local_width),
+        grid=(3,),
+        in_specs=[
+            SMEM,
+            whole(tokens, width),
+            whole(1, width),
+            pl.BlockSpec((1, 1, local_width), lambda c: (c, 0, 0)),
+            whole(tokens, HEAD_DIM),
+            whole(tokens, HEAD_DIM),
+        ]
+        + [pl.BlockSpec((1,) + piece.shape[1:], lambda c: (c, 0, 0)) for piece in flat],
+        out_specs=[
+            pl.BlockSpec((1, tokens, local_width), lambda c: (c, 0, 0)),
+            whole(tokens, width),
+        ],
+    )(number, hidden, gain, bias, cosine, signed_sine, *flat)
+
+
+ATTEND_ROWS = 176
+
+
+def attend(projected, prior, masks, score_scale):
+    _, tokens, local_width = projected.shape
+    heads = local_width // HEAD_DIM
+    tiles = tokens // ATTEND_ROWS
+
+    def kernel(q_ref, own_ref, prior_ref, mask_own_ref, mask_prior_ref, mixed_ref, log_ref):
+        for h in range(heads):
+            at = slice(h * HEAD_DIM, (h + 1) * HEAD_DIM)
+            queries = q_ref[0, :, at]
+            score_own = product(queries, own_ref[1, :, at], ROWS_ROWS) * score_scale
+            score_own = score_own + mask_own_ref[...]
+            score_prior = product(queries, prior_ref[0, :, at], ROWS_ROWS) * score_scale
+            score_prior = score_prior + mask_prior_ref[...]
+            row_max = jnp.maximum(
+                jnp.max(score_own, axis=-1, keepdims=True),
+                jnp.max(score_prior, axis=-1, keepdims=True),
+            )
+            own = jnp.exp(score_own - row_max)
+            before = jnp.exp(score_prior - row_max)
+            total = jnp.sum(own, axis=-1, keepdims=True) + jnp.sum(before, axis=-1, keepdims=True)
+            scale = 1.0 / total
+            mixed = product((own * scale).astype(jnp.bfloat16), own_ref[2, :, at])
+            mixed = mixed + product((before * scale).astype(jnp.bfloat16), prior_ref[1, :, at])
+            mixed_ref[:, at] = mixed.astype(jnp.bfloat16)
+            log_ref[:, h : h + 1] = row_max + jnp.log(total)
+
+    return call(
+        kernel,
+        [
+            jax.ShapeDtypeStruct((tokens, local_width), jnp.bfloat16),
+            jax.ShapeDtypeStruct((tokens, heads), jnp.float32),
+        ],
+        8 * tokens * tokens * local_width,
+        8 * tokens * tokens + 12 * tokens * local_width,
+        grid=(tiles,),
+        in_specs=[
+            pl.BlockSpec((1, ATTEND_ROWS, local_width), lambda i: (0, i, 0)),
+            pl.BlockSpec((3, tokens, local_width), lambda i: (0, 0, 0)),
+            pl.BlockSpec((2, tokens, local_width), lambda i: (0, 0, 0)),
+            pl.BlockSpec((ATTEND_ROWS, tokens), lambda i: (i, 0)),
+            pl.BlockSpec((ATTEND_ROWS, tokens), lambda i: (i, 0)),
+        ],
+        out_specs=[
+            pl.BlockSpec((ATTEND_ROWS, local_width), lambda i: (i, 0)),
+            pl.BlockSpec((ATTEND_ROWS, heads), lambda i: (i, 0)),
+        ],
+    )(projected, projected, prior, *masks)
+
+
+def attend_back(projected, prior, masks, log_total, grad_mixed, cosine, signed_sine, score_scale):
+    _, tokens, local_width = projected.shape
+    heads = local_width // HEAD_DIM
+    tiles = tokens // ATTEND_ROWS
+
+    def kernel(
+        q_ref, own_ref, prior_ref, mask_own_ref, mask_prior_ref, log_ref, grad_ref, cos_ref, sin_ref,
+        query_out, own_out, prior_out, own_sum, prior_sum,
+    ):
+        tile = pl.program_id(0)
+
+        @pl.when(tile == 0)
+        def _():
+            own_sum[...] = jnp.zeros_like(own_sum)
+            prior_sum[...] = jnp.zeros_like(prior_sum)
+
+        for h in range(heads):
+            at = slice(h * HEAD_DIM, (h + 1) * HEAD_DIM)
+            queries = q_ref[0, :, at]
+            grads = grad_ref[:, at]
+            log_now = log_ref[:, h : h + 1]
+            soft, low, dots = [], [], []
+            for keys, values, mask_ref in (
+                (own_ref[1, :, at], own_ref[2, :, at], mask_own_ref),
+                (prior_ref[0, :, at], prior_ref[1, :, at], mask_prior_ref),
+            ):
+                score = product(queries, keys, ROWS_ROWS) * score_scale + mask_ref[...]
+                soft.append(jnp.exp(score - log_now))
+                dots.append(product(grads, values, ROWS_ROWS))
+            centre = jnp.sum(soft[0] * dots[0], axis=-1, keepdims=True)
+            centre = centre + jnp.sum(soft[1] * dots[1], axis=-1, keepdims=True)
+            grad_query = None
+            for side, sums, keys in (
+                (0, own_sum, own_ref[1, :, at]),
+                (1, prior_sum, prior_ref[0, :, at]),
+            ):
+                grad_score = (soft[side] * (dots[side] - centre)).astype(jnp.bfloat16)
+                term = product(grad_score, keys)
+                grad_query = term if grad_query is None else grad_query + term
+                sums[0, :, at] += product(grad_score, queries, COLS_COLS)
+                sums[1, :, at] += product(soft[side].astype(jnp.bfloat16), grads, COLS_COLS)
+            query_out[:, at] = turn(
+                grad_query * score_scale, cos_ref[...], -sin_ref[...]
+            ).astype(jnp.bfloat16)
+
+        @pl.when(tile == tiles - 1)
+        def _():
+            own_out[0] = own_sum[0] * score_scale
+            own_out[1] = own_sum[1]
+            prior_out[0] = (prior_sum[0] * score_scale).astype(jnp.bfloat16)
+            prior_out[1] = prior_sum[1].astype(jnp.bfloat16)
+
+    row_block = lambda wide: pl.BlockSpec((ATTEND_ROWS, wide), lambda i: (i, 0))
+    whole = lambda *shape: pl.BlockSpec(shape, lambda i: (0,) * len(shape))
+    pair = (2, tokens, local_width)
+    return call(
+        kernel,
+        [
+            jax.ShapeDtypeStruct((tokens, local_width), jnp.bfloat16),
+            jax.ShapeDtypeStruct(pair, jnp.float32),
+            jax.ShapeDtypeStruct(pair, jnp.bfloat16),
+        ],
+        20 * tokens * tokens * local_width,
+        8 * tokens * tokens + 30 * tokens * local_width,
+        grid=(tiles,),
+        in_specs=[
+            pl.BlockSpec((1, ATTEND_ROWS, local_width), lambda i: (0, i, 0)),
+            whole(3, tokens, local_width),
+            whole(2, tokens, local_width),
+            row_block(tokens),
+            row_block(tokens),
+            row_block(heads),
+            row_block(local_width),
+            row_block(HEAD_DIM),
+            row_block(HEAD_DIM),
+        ],
+        out_specs=[row_block(local_width), whole(*pair), whole(*pair)],
+        scratch_shapes=[pltpu.VMEM(pair, jnp.float32), pltpu.VMEM(pair, jnp.float32)],
+    )(projected, projected, prior, *masks, log_total, grad_mixed, cosine, signed_sine)
+
+
+def project_back(number, grad_query, grad_own, arrived, cosine, signed_sine, hidden, weights):
+    tokens, local_width = grad_query.shape
+    flat, places = pieces_of(weights)
+    deep = flat[0].shape[1]
+    width = 8 * deep
+    rows = tokens // 2
+
+    def kernel(number_ref, query_ref, own_ref, arrived_ref, cos_ref, sin_ref, hidden_ref, *others):
+        weight_refs = others[: len(flat)]
+        linear_ref, bias_ref, gain_ref, out_ref = others[len(flat) :]
+
+        @pl.when(pl.program_id(0) == 0)
+        def _():
+            bias_ref[...] = jnp.zeros_like(bias_ref)
+            gain_ref[...] = jnp.zeros_like(gain_ref)
+
+        residual = hidden_ref[...].astype(jnp.float32)
+        scale = lax.rsqrt(jnp.mean(residual * residual, axis=-1, keepdims=True) + norm_epsilon)
+
+        keys = own_ref[0] + arrived_ref[0].astype(jnp.float32)
+        linear_ref[0] = query_ref[...]
+        for h in range(local_width // HEAD_DIM):
+            at = slice(h * HEAD_DIM, (h + 1) * HEAD_DIM)
+            linear_ref[1, :, at] = turn(keys[:, at], cos_ref[...], -sin_ref[...]).astype(
+                jnp.bfloat16
+            )
+        linear_ref[2] = (own_ref[1] + arrived_ref[1].astype(jnp.float32)).astype(jnp.bfloat16)
+        for c in range(3):
+            bias_ref[c] += jnp.sum(linear_ref[c].astype(jnp.float32), axis=0, keepdims=True)
+        for r in range(8):
+            total = None
+            for c in range(3):
+                first = 0
+                for at in places[r]:
+                    last = first + flat[at].shape[2]
+                    term = product(linear_ref[c, :, first:last], weight_refs[at][c], ROWS_ROWS)
+                    total = term if total is None else total + term
+                    first = last
+            columns = block_columns(number_ref[0] ^ r, deep)
+            out_ref[:, columns] = total.astype(jnp.bfloat16)
+            scaled = hidden_ref[:, columns].astype(jnp.float32) * scale
+            gain_ref[:, columns] += jnp.sum(total * scaled, axis=0, keepdims=True)
+
+    whole = lambda *shape: pl.BlockSpec(shape, lambda i: (0,) * len(shape))
+    row_block = lambda wide: pl.BlockSpec((rows, wide), lambda i: (i, 0))
+    pair_block = pl.BlockSpec((2, rows, local_width), lambda i: (0, i, 0))
+    return call(
+        kernel,
+        [
+            jax.ShapeDtypeStruct((3, tokens, local_width), jnp.bfloat16),
+            jax.ShapeDtypeStruct((3, 1, local_width), jnp.float32),
+            jax.ShapeDtypeStruct((1, width), jnp.float32),
+            jax.ShapeDtypeStruct((tokens, width), jnp.bfloat16),
+        ],
+        6 * tokens * local_width * width,
+        2 * (tokens * width + 3 * width * local_width + 12 * tokens * local_width),
+        grid=(2,),
+        in_specs=[
+            SMEM,
+            row_block(local_width),
+            pair_block,
+            pair_block,
+            row_block(HEAD_DIM),
+            row_block(HEAD_DIM),
+            row_block(width),
+        ]
+        + [whole(*piece.shape) for piece in flat],
+        out_specs=[
+            pl.BlockSpec((3, rows, local_width), lambda i: (0, i, 0)),
+            whole(3, 1, local_width),
+            whole(1, width),
+            row_block(width),
+        ],
+    )(number, grad_query, grad_own, arrived, cosine, signed_sine, hidden, *flat)
+
+
+def project_weights(normed, grad_linear):
+    tokens, width = normed.shape
+    local_width = grad_linear.shape[2]
+    deep = width // 8
+
+    def kernel(normed_ref, linear_ref, out_ref):
+        columns = block_columns(pl.program_id(0), deep)
+        for c in range(3):
+            out_ref[0, c] = product(normed_ref[:, columns], linear_ref[c], COLS_COLS).astype(
+                jnp.bfloat16
+            )
+
+    whole = lambda *shape: pl.BlockSpec(shape, lambda i: (0,) * len(shape))
+    return call(
+        kernel,
+        jax.ShapeDtypeStruct((8, 3, deep, local_width), jnp.bfloat16),
+        6 * tokens * local_width * width,
+        2 * (tokens * width + 3 * width * local_width + 3 * tokens * local_width),
+        grid=(8,),
+        in_specs=[whole(tokens, width), whole(3, tokens, local_width)],
+        out_specs=pl.BlockSpec((1, 3, deep, local_width), lambda i: (i, 0, 0, 0)),
+    )(normed, grad_linear)
+
+
+def lay_weights(expert_t, expert_outer, shared_rows, router_rows, pad):
+    _, hid_e, width = expert_t.shape
+    hid_s = shared_rows.shape[0] // 3
+    hid = hid_e + hid_s
+    last = hid + router_rows.shape[0]
+
+    def kernel(expert_ref, outer_ref, shared_ref, router_ref, inner_out, outer_out):
+        zeros = jnp.zeros((pad - hid, width), jnp.bfloat16)
+        inner_out[:hid_e] = expert_ref[0]
+        inner_out[hid_e:hid] = shared_ref[:hid_s]
+        inner_out[hid:last] = router_ref[...]
+        inner_out[last:pad] = zeros[: pad - last]
+        inner_out[pad : pad + hid_e] = expert_ref[1]
+        inner_out[pad + hid_e : pad + hid] = shared_ref[hid_s : 2 * hid_s]
+        inner_out[pad + hid :] = zeros
+        outer_out[:hid_e] = outer_ref[...]
+        outer_out[hid_e:hid] = shared_ref[2 * hid_s :]
+        outer_out[hid:] = zeros
+
+    return call(
+        kernel,
+        [
+            jax.ShapeDtypeStruct((2 * pad, width), jnp.bfloat16),
+            jax.ShapeDtypeStruct((pad, width), jnp.bfloat16),
+        ],
+        0,
+        12 * pad * width,
+        in_specs=[VMEM] * 4,
+        out_specs=[VMEM] * 2,
+    )(expert_t, expert_outer, shared_rows, router_rows)
+
+
+MIX_ROWS = 352
+LANES = 128
+
+
+def tiles_of(pieces):
+    return [(at, first) for at, p in enumerate(pieces) for first in range(0, p.shape[0], MIX_ROWS)]
+
+
+def next_tile(refs, starts, buffer, sems):
+    tile = pl.program_id(0)
+
+    def copy(number):
+        at, first = starts[number]
+        return pltpu.make_async_copy(
+            refs[at].at[pl.ds(first, MIX_ROWS)], buffer.at[number % 2], sems.at[number % 2]
+        )
+
+    for number in range(len(starts)):
+
+        @pl.when(tile == number)
+        def _():
+            if number == 0:
+                copy(0).start()
+            if number + 1 < len(starts):
+                copy(number + 1).start()
+            copy(number).wait()
+
+    return buffer[lax.rem(tile, 2)]
+
+
+def narrow(pieces, other):
+    starts = tiles_of(pieces)
+    units, width = other.shape
+
+    def kernel(other_ref, *refs):
+        piece_refs, (out_ref, buffer, sems) = refs[: len(pieces)], refs[len(pieces) :]
+        rows = next_tile(piece_refs, starts, buffer, sems)
+        out_ref[...] = product(rows, other_ref[...], ROWS_ROWS)
+
+    tokens = len(starts) * MIX_ROWS
+    return call(
+        kernel,
+        jax.ShapeDtypeStruct((tokens, units), jnp.float32),
+        2 * tokens * units * width,
+        2 * (tokens * width + units * width + 2 * tokens * units),
+        grid=(len(starts),),
+        in_specs=[pl.BlockSpec((units, width), lambda i: (0, 0))] + [ANY] * len(pieces),
+        out_specs=pl.BlockSpec((MIX_ROWS, units), lambda i: (i, 0)),
+        scratch_shapes=[
+            pltpu.VMEM((2, MIX_ROWS, width), jnp.bfloat16),
+            pltpu.SemaphoreType.DMA((2,)),
+        ],
+    )(other, *pieces)
+
+
+def widen(parts, other):
+    starts = tiles_of(parts)
+    units, width = other.shape
+    rows = parts[0].shape[0] // 2
+    each = rows // MIX_ROWS
+    count = 2 * len(parts)
+
+    def kernel(other_ref, *refs):
+        part_refs = refs[: len(parts)]
+        outs, (buffer, sems) = refs[len(parts) : len(parts) + count], refs[len(parts) + count :]
+        value = product(next_tile(part_refs, starts, buffer, sems), other_ref[...])
+        for at in range(count):
+
+            @pl.when(pl.program_id(0) // each == at)
+            def _():
+                outs[at][...] = value.astype(jnp.bfloat16)
+
+    def place(at):
+        return pl.BlockSpec(
+            (MIX_ROWS, width), lambda i: (jnp.clip(i - at * each, 0, each - 1), 0)
+        )
+
+    tokens = count * rows
+    return call(
+        kernel,
+        [jax.ShapeDtypeStruct((rows, width), jnp.bfloat16)] * count,
+        2 * tokens * units * width,
+        2 * (tokens * width + units * width + tokens * units),
+        grid=(len(starts),),
+        in_specs=[pl.BlockSpec((units, width), lambda i: (0, 0))] + [ANY] * len(parts),
+        out_specs=[place(at) for at in range(count)],
+        scratch_shapes=[
+            pltpu.VMEM((2, MIX_ROWS, units), jnp.bfloat16),
+            pltpu.SemaphoreType.DMA((2,)),
+        ],
+    )(other, *parts)
+
+
+def mixture(row_pieces, upstream, kept, mine, inner, hid_e, hid, experts):
+    tokens, pad = upstream.shape
+    width = inner.shape[1]
+    starts = tiles_of(row_pieces)
+    tiles = len(starts)
+    count = len(row_pieces)
+    first_router = hid - (pad - LANES)
+
+    def kernel(kept_ref, mine_ref, inner_ref, upstream_ref, *others):
+        row_refs = others[:count]
+        pre_out, weighted_out, other_out, own_out, buffer, sems = others[count:]
+        tile = pl.program_id(0)
+        rows = next_tile(row_refs, starts, buffer, sems)
+        pre = product(rows, inner_ref[...], ROWS_ROWS)
+        upstream = upstream_ref[...]
+        gate_pre, up_pre = pre[:, :pad], pre[:, pad:]
+        tail = gate_pre[:, pad - LANES :]
+        lane = lax.broadcasted_iota(jnp.int32, tail.shape, 1) - first_router
+        routed = (lane >= 0) & (lane < experts)
+        logits = jnp.where(routed, tail, -1e30)
+        raised = jnp.exp(logits - jnp.max(logits, axis=-1, keepdims=True))
+        probs = raised / jnp.sum(raised, axis=-1, keepdims=True)
+        own_prob = jnp.sum(probs * mine_ref[...], axis=-1, keepdims=True)
+        blend = jax.nn.sigmoid(
+            jnp.sum(jnp.where(lane == experts, tail, 0.0), axis=-1, keepdims=True)
+        )
+        kept_now = kept_ref[...]
+        of_expert = lax.broadcasted_iota(jnp.int32, gate_pre.shape, 1) < hid_e
+        weight = jnp.where(of_expert, kept_now * own_prob, blend)
+        sigma = jax.nn.sigmoid(gate_pre)
+        act = gate_pre * sigma
+        slope = sigma + act * (1.0 - sigma)
+        hidden = (act * up_pre).astype(jnp.bfloat16).astype(jnp.float32)
+        inner_dot = hidden * upstream
+        gate_dot = jnp.sum(jnp.where(of_expert, inner_dot, 0.0), axis=-1, keepdims=True)
+        blend_dot = jnp.sum(jnp.where(of_expert, 0.0, inner_dot), axis=-1, keepdims=True)
+        grad_router = probs * (kept_now * gate_dot) * (mine_ref[...] - own_prob)
+        grad_blend = blend * (1.0 - blend) * blend_dot
+        scaled = weight * upstream
+        grad_gate = scaled * up_pre * slope
+        grad_tail = grad_gate[:, pad - LANES :] + jnp.where(
+            lane == experts, grad_blend, grad_router
+        )
+        pre_out[:, : pad - LANES] = grad_gate[:, : pad - LANES].astype(jnp.bfloat16)
+        pre_out[:, pad - LANES : pad] = grad_tail.astype(jnp.bfloat16)
+        pre_out[:, pad:] = (scaled * act).astype(jnp.bfloat16)
+        weighted_out[...] = (weight * hidden).astype(jnp.bfloat16)
+        back = product(pre_out[...], inner_ref[...]).astype(jnp.bfloat16)
+
+        @pl.when(tile < tiles // 2)
+        def _():
+            other_out[...] = back
+
+        @pl.when(tile >= tiles // 2)
+        def _():
+            own_out[...] = back
+
+    whole = lambda *shape: pl.BlockSpec(shape, lambda i: (0,) * len(shape))
+    row_block = lambda wide: pl.BlockSpec((MIX_ROWS, wide), lambda i: (i, 0))
+    half = jax.ShapeDtypeStruct((tokens // 2, width), jnp.bfloat16)
+    return call(
+        kernel,
+        [
+            jax.ShapeDtypeStruct((tokens, 2 * pad), jnp.bfloat16),
+            jax.ShapeDtypeStruct((tokens, pad), jnp.bfloat16),
+            half,
+            half,
+        ],
+        8 * tokens * pad * width,
+        2 * (2 * tokens * width + 5 * tokens * pad + 2 * pad * width),
+        grid=(tiles,),
+        in_specs=[row_block(1), whole(1, LANES), whole(2 * pad, width), row_block(pad)]
+        + [ANY] * count,
+        out_specs=[
+            row_block(2 * pad),
+            row_block(pad),
+            pl.BlockSpec((MIX_ROWS, width), lambda i: (jnp.minimum(i, tiles // 2 - 1), 0)),
+            pl.BlockSpec((MIX_ROWS, width), lambda i: (jnp.maximum(i - tiles // 2, 0), 0)),
+        ],
+        scratch_shapes=[
+            pltpu.VMEM((2, MIX_ROWS, width), jnp.bfloat16),
+            pltpu.SemaphoreType.DMA((2,)),
+        ],
+    )(kept, mine, inner, upstream, *row_pieces)
+
+
+def attend_out(numbers, hidden, gain, mixed, own_weights, other_weights):
+    tokens, width = hidden.shape
+    count, _, local_width = mixed.shape
+    deep = own_weights[0].shape[1]
+    long = count * local_width
+    rows = tokens // count
+
+    def kernel(numbers_ref, hidden_ref, gain_ref, mixed_ref, *others):
+        own_refs, (other_ref, normed_ref, kept_ref, sum_ref) = others[:4], others[4:]
+        heads = jnp.concatenate([mixed_ref[i] for i in range(count)], axis=1)
+        for r in range(8):
+            chip = (r // 4) * 2 + r % 2
+            if (r // 2) % 2:
+                weight = other_ref[chip * long : (chip + 1) * long]
+            else:
+                weight = own_refs[chip][...]
+            columns = block_columns(numbers_ref[0] ^ r, deep)
+            sum_ref[:, columns] = hidden_ref[:, columns].astype(jnp.float32) + product(
+                heads, weight
+            )
+        values = sum_ref[...]
+        normed_ref[...] = root_norm(values, gain_ref[...]).astype(jnp.bfloat16)
+
+        @pl.when(pl.program_id(0) == numbers_ref[1])
+        def _():
+            kept_ref[...] = values
+
+    whole = lambda *shape: pl.BlockSpec(shape, lambda i: (0,) * len(shape))
+    row_block = lambda wide: pl.BlockSpec((rows, wide), lambda i: (i, 0))
+    return call(
+        kernel,
+        [
+            jax.ShapeDtypeStruct((tokens, width), jnp.bfloat16),
+            jax.ShapeDtypeStruct((rows, width), jnp.float32),
+        ],
+        2 * tokens * width * long,
+        2 * (3 * tokens * width + long * width),
+        grid=(count,),
+        in_specs=[
+            SMEM,
+            row_block(width),
+            whole(1, width),
+            pl.BlockSpec((count, rows, local_width), lambda i: (0, i, 0)),
+        ]
+        + [whole(long, deep)] * 4
+        + [whole(4 * long, deep)],
+        out_specs=[row_block(width), whole(rows, width)],
+        scratch_shapes=[pltpu.VMEM((rows, width), jnp.float32)],
+    )(numbers, hidden, gain, mixed, *own_weights, other_weights)
+
+
+def attend_out_back(numbers, grads, own_weights, other_weights, count):
+    rows, width = grads.shape
+    long, deep = own_weights[0].shape
+    local_width = long // count
+
+    def kernel(numbers_ref, grads_ref, *others):
+        own_refs, (other_ref, mixed_ref) = others[:4], others[4:]
+        for i in range(count):
+            total = None
+            for r in range(8):
+                chip = (r // 4) * 2 + r % 2
+                first = i * local_width
+                if (r // 2) % 2:
+                    weight = other_ref[chip * long + first : chip * long + first + local_width]
+                else:
+                    weight = own_refs[chip][first : first + local_width]
+                taken = grads_ref[:, block_columns(numbers_ref[0] ^ r, deep)]
+                term = product(taken, weight, ROWS_ROWS)
+                total = term if total is None else total + term
+            mixed_ref[i] = total.astype(jnp.bfloat16)
+
+    whole = lambda *shape: pl.BlockSpec(shape, lambda i: (0,) * len(shape))
+    return call(
+        kernel,
+        jax.ShapeDtypeStruct((count, rows, local_width), jnp.bfloat16),
+        2 * rows * width * long,
+        2 * (2 * rows * width + long * width),
+        grid=(1,),
+        in_specs=[SMEM, whole(rows, width)] + [whole(long, deep)] * 4 + [whole(4 * long, deep)],
+        out_specs=whole(count, rows, local_width),
+    )(numbers, grads, *own_weights, other_weights)
+
+
+def weight_gradients(parts, row_pieces, tile):
+    units = parts[0].shape[1]
+    width = row_pieces[0][0].shape[1]
+    tokens = parts[0].shape[0]
+    pieces = [piece for chip in row_pieces for piece in chip]
+    firsts = [sum(p.shape[0] for p in pieces[:i]) for i in range(len(pieces))]
+    chips = len(parts)
+
+    def kernel(*refs):
+        part_refs, piece_refs = refs[:chips], refs[chips : chips + len(pieces)]
+        out_ref, buffer, sems = refs[chips + len(pieces) :]
+        copies = [
+            pltpu.make_async_copy(
+                ref, buffer.at[pl.ds(firsts[i], pieces[i].shape[0])], sems.at[i]
+            )
+            for i, ref in enumerate(piece_refs)
+        ]
+
+        @pl.when(pl.program_id(0) == 0)
+        def _():
+            for copy in copies:
+                copy.start()
+            for copy in copies:
+                copy.wait()
+
+        total = None
+        for chip in range(chips):
+            rows = buffer[chip * tokens : (chip + 1) * tokens]
+            term = product(part_refs[chip][...], rows, COLS_COLS)
+            total = term if total is None else total + term
+        out_ref[...] = total
+
+    return call(
+        kernel,
+        jax.ShapeDtypeStruct((units, width), jnp.float32),
+        2 * chips * tokens * units * width,
+        2 * chips * tokens * (units + width) + 4 * units * width,
+        grid=(units // tile,),
+        in_specs=[pl.BlockSpec((tokens, tile), lambda i: (0, i))] * chips + [ANY] * len(pieces),
+        out_specs=pl.BlockSpec((tile, width), lambda i: (i, 0)),
+        scratch_shapes=[
+            pltpu.VMEM((chips * tokens, width), jnp.bfloat16),
+            pltpu.SemaphoreType.DMA((len(pieces),)),
+        ],
+    )(*parts, *pieces)
+
+
+def eight_plan(
+    hidden_in,
+    doc_lengths,
+    expert_ids,
+    fill_rank,
+    norm_gains,
+    qkv_weight,
+    qkv_bias,
+    out_weight,
+    router_weight,
+    blend_weight,
+    shared_inner,
+    shared_outer,
+    expert_inner,
+    expert_outer,
+    cotangent,
+):
+    _, tokens, width = hidden_in.shape
+    local_width = qkv_weight.shape[2]
+    experts = router_weight.shape[1]
+    capacity = tokens * TOP // experts
+    score_scale = 1.0 / math.sqrt(HEAD_DIM)
+    gains = norm_gains.astype(jnp.float32)
+    me_tp = lax.axis_index("tp")
+    tp = lax.axis_size("tp")
+    share = tokens // tp
+    number = own_number()
+    numbers = jnp.stack([number, me_tp])
+    deep = width // 8
+    half_width = local_width // 2
+
+    def own_rows(values):
+        return lax.dynamic_slice_in_dim(values, me_tp * share, share, axis=0)
+
+    def own_columns(heads):
+        return lax.dynamic_slice_in_dim(heads, me_tp * share, share, axis=1)
+
+    qkv_own = jnp.transpose(qkv_weight, (1, 0, 2))
+    qkv_x, qkv_y = swap_x(qkv_own), swap_y(qkv_own)
+    qkv_sibling = swap_core(qkv_own)
+    out_line = lax.all_gather(out_weight, "tp", axis=0, tiled=True)
+
+    route_rows = expert_ids.reshape(tokens, TOP)
+    named = jnp.sum(
+        (route_rows[:, :, None] == jnp.arange(experts, dtype=jnp.int32)[None, None, :]).astype(
+            jnp.float32
+        ),
+        axis=1,
+    )
+    priority = fill_rank.reshape(tokens)
+    earlier = (priority[None, :] < priority[:, None]).astype(jnp.bfloat16)
+    slot_counts = jnp.dot(
+        earlier, named.astype(jnp.bfloat16), preferred_element_type=jnp.float32
+    )
+    kept_all = named * (slot_counts < capacity).astype(jnp.float32)
+    kept_blocks = lax.all_to_all(
+        kept_all.T.reshape(experts, 1, tokens),
+        ("fsdp", "ctx"),
+        split_axis=0,
+        concat_axis=0,
+        tiled=True,
+    )
+
+    positions = lax.axis_index("ctx") * tokens + jnp.arange(tokens, dtype=jnp.int32)
+    earlier_pos = positions - tokens
+    doc_number, doc_place = document_layout(doc_lengths[0], positions)
+    prior_number = document_layout(doc_lengths[0], earlier_pos)[0]
+    cosine, sine_table = rotary_tables(doc_place)
+    half_dim = HEAD_DIM // 2
+    signed_sine = jnp.concatenate([-sine_table[:, :half_dim], sine_table[:, half_dim:]], axis=1)
+    masks = []
+    for places, doc_numbers in ((positions, doc_number), (earlier_pos, prior_number)):
+        distance = positions[:, None] - places[None, :]
+        allowed = (
+            (distance >= 0)
+            & (distance < WINDOW)
+            & (places[None, :] >= 0)
+            & (doc_number[:, None] == doc_numbers[None, :])
+        )
+        masks.append(jnp.where(allowed, 0.0, masked_score))
+
+    shared_t = jnp.transpose(shared_inner, (1, 2, 0))
+    hid_s = shared_t.shape[1] // 8
+    to_trade = jnp.concatenate(
+        [
+            shared_t.reshape(2, 8, hid_s, deep)[0],
+            shared_t.reshape(2, 8, hid_s, deep)[1],
+            shared_outer.reshape(8, hid_s, deep),
+        ],
+        axis=1,
+    )
+
+    (qkv_x, qkv_y), early_kept = after((qkv_x, qkv_y), kept_all), kept_blocks
+    qkv_low = swap_x(qkv_y[:, :, :half_width])
+    qkv_high = swap_y(qkv_x[:, :, half_width:])
+    qkv_parts = [
+        [qkv_own],
+        [qkv_y],
+        [qkv_sibling],
+        [swap_core(qkv_y)],
+        [qkv_x],
+        [qkv_low, qkv_high],
+        [swap_core(qkv_x)],
+        [swap_core(qkv_low), swap_core(qkv_high)],
+    ]
+    hidden_rows = hidden_in.reshape(tokens, width)
+    hidden_first, (cosine, signed_sine), masks = after(
+        (hidden_rows, (cosine, signed_sine), masks), early_kept
+    )
+    projected, first_normalized = project(
+        numbers,
+        hidden_first,
+        gains[:1],
+        qkv_parts,
+        qkv_bias.astype(jnp.float32)[:, None],
+        cosine,
+        signed_sine,
+    )
+    prior = from_behind(projected[1:], "ctx", 1)
+
+    grad_rows = cotangent.reshape(tokens, width)
+    grads_share = after(own_rows(grad_rows), qkv_low, qkv_high)
+    grads_x, grads_y = swap_x(grads_share), swap_y(grads_share)
+    grads_both = lax.ppermute(grads_share, ("fsdp", "ctx"), [(d, d ^ 5) for d in range(8)])
+    grads_x, grads_y, grads_both = after((grads_x, grads_y, grads_both), projected)
+    grads_x = line_gather(grads_x).reshape(tokens, width)
+
+    out_own = after(out_line, qkv_low, qkv_high)
+    out_x = swap_x(out_own)
+
+    prior = after(prior, grads_y, grads_both)
+    mixed_result, log_total = attend(projected, prior, masks, score_scale)
+    mixed_all = line_gather(after(mixed_result, grads_x))
+
+    to_trade, out_late = after((to_trade, out_own), mixed_result)
+    out_y = swap_y(out_late)
+    out_both = swap_x(out_y)
+    traded = hop_trade(exchange_order([to_trade[d] for d in range(8)]))
+    out_mine = [out_own, out_y, out_x, out_both]
+    out_other = swap_core(after(jnp.concatenate(out_mine), mixed_result))
+    grads_sibling = swap_core(after(grad_rows, projected))
+    hidden_rows = hidden_in.reshape(tokens, width)
+
+    kept_rel = exchange_order([kept_blocks[i].reshape(tokens, 1) for i in range(8)])
+    kept_chips = [jnp.concatenate([kept_rel[p + 2], kept_rel[p]]) for p in (0, 4, 1, 5)]
+    shared_rows = jnp.concatenate(exchange_order(after(traded, mixed_result)), axis=1)
+    hid_e = expert_inner.shape[3]
+    hid = hid_e + hid_s
+    router_rows = jnp.concatenate(
+        [
+            router_weight.T,
+            blend_weight[None],
+            jnp.zeros((-(experts + 1) % 16, width), jnp.bfloat16),
+        ]
+    )
+    pad = -(-(hid + router_rows.shape[0]) // LANES) * LANES
+    inner, outer = lay_weights(
+        jnp.transpose(expert_inner[0], (1, 2, 0)),
+        expert_outer[0],
+        shared_rows,
+        router_rows,
+        pad,
+    )
+    mine = (
+        jnp.arange(LANES, dtype=jnp.int32) == number + (hid - (pad - LANES))
+    ).astype(jnp.float32)[None]
+    grad_chips = [[grads_sibling, grad_rows], [swap_core(grads_x), grads_x]]
+    upstream = [narrow(grad_chips[0], outer)]
+    upstream.append(narrow(after(grad_chips[1], upstream[0]), outer))
+    mixed_all, upstream = after((mixed_all, upstream))
+    second_normalized, after_own = attend_out(
+        numbers, hidden_rows, gains[1:], mixed_all, out_mine, out_other
+    )
+    grads_y = line_gather(after(grads_y, second_normalized)).reshape(tokens, width)
+    rows_x, rows_y = swap_x(second_normalized), swap_y(second_normalized)
+    row_chips = [[swap_core(second_normalized), second_normalized]]
+
+    def mix(chip, *earlier):
+        return mixture(
+            row_chips[chip],
+            upstream[chip],
+            after(kept_chips[chip], earlier),
+            mine,
+            inner,
+            hid_e,
+            hid,
+            experts,
+        )
+
+    mixes = [mix(0)]
+    back_arrived = [swap_core(mixes[0][2])]
+    rows_x, rows_y = after((rows_x, rows_y), mixes[0][0])
+    rows_low = swap_x(rows_y[: tokens // 2])
+    rows_high = swap_y(rows_x[tokens // 2 :])
+    row_chips += [[swap_core(rows_x), rows_x], [swap_core(rows_y), rows_y]]
+    grads_y = after(grads_y, mixes[0][0])
+    grad_chips.append([swap_core(grads_y), grads_y])
+    grads_both = line_gather(after(grads_both, grads_y)).reshape(tokens, width)
+    upstream.append(narrow(grad_chips[2], outer))
+    mixes.append(mix(1, upstream[2]))
+    back_arrived.append(swap_core(mixes[1][2]))
+    rows_low, rows_high = after((rows_low, rows_high), mixes[1][0])
+    mixes.append(mix(2, back_arrived[0], rows_low, rows_high))
+    back_arrived.append(swap_core(mixes[2][2]))
+    taken = [halves_sum(mixes[chip][3], back_arrived[chip]) for chip in range(2)]
+    x_low = swap_x(taken[1][0])
+    row_chips.append([swap_core(rows_low), swap_core(rows_high), rows_low, rows_high])
+    grads_both = after(grads_both, mixes[1][0])
+    grad_chips.append([swap_core(grads_both), grads_both])
+    upstream.append(narrow(after(grad_chips[3], mixes[2][0], taken), outer))
+    taken.append(halves_sum(mixes[2][3], after(back_arrived[2], upstream[3])))
+    y_high = swap_y(taken[2][1])
+    mixes.append(mix(3, taken[2], row_chips[3]))
+    back_arrived.append(swap_core(after(mixes[3][2], x_low, y_high)))
+    taken.append(halves_sum(mixes[3][3], back_arrived[3]))
+    hops = [x_low, y_high, swap_x(taken[3][0]), swap_y(taken[3][1])]
+
+    pre_list = [m[0] for m in mixes]
+    weighted_list = after([m[1] for m in mixes], taken[3])
+    forward = widen(weighted_list, outer)
+    hops = after(hops, forward)
+    ends = last_hops(taken, hops)
+    forward = after(forward, hops)
+    arrived_forward = [swap_core(forward[2 * chip]) for chip in range(4)]
+    forward_taken = [halves_sum(forward[2 * c + 1], arrived_forward[c]) for c in range(4)]
+    back_sum = hops_sum(taken, hops, after(ends, forward_taken))
+    grad_normed_two = line_reduce(back_sum)
+    forward_hops = first_hops(after(forward_taken, back_sum))
+    outer_grad = weight_gradients(after(weighted_list, back_sum), grad_chips, LANES)
+    inner_grad = weight_gradients(after(pre_list, outer_grad), row_chips, 256)
+    grad_normed_two, forward_hops = after((grad_normed_two, forward_hops), inner_grad)
+    forward_ends = last_hops(forward_taken, forward_hops)
+
+    grad_y = own_rows(grad_rows).astype(jnp.float32)
+    after_norm_grad, gain_two_grad = jax.vjp(root_norm, after_own, gains[1])[1](grad_normed_two)
+    grad_after = grad_y + after_norm_grad
+    grad_attn = grad_after.astype(jnp.bfloat16)
+
+    grad_heads = attend_out_back(numbers, grad_attn, out_mine, out_other, tp)
+    grad_mixed = lax.all_to_all(
+        grad_heads, "tp", split_axis=0, concat_axis=0, tiled=True
+    ).reshape(tokens, local_width)
+    heads_own = after(own_columns(mixed_all), grad_heads)
+    projection_full = lax.dot_general(
+        heads_own, grad_attn, (((1,), (0,)), ((), ())), preferred_element_type=jnp.float32
+    ).astype(jnp.bfloat16)
+    projection_grad = lax.psum_scatter(
+        projection_full.reshape(tp * local_width, width),
+        ("fsdp", "ctx"),
+        scatter_dimension=1,
+        tiled=True,
+    )
+    projection_grad = lax.psum_scatter(
+        projection_grad, "tp", scatter_dimension=0, tiled=True
+    ).astype(jnp.float32)
+
+    grad_mixed, forward_ends = after((grad_mixed, forward_ends))
+    forward_sum = hops_sum(forward_taken, forward_hops, forward_ends)
+    grad_query, grad_own, grad_prior = attend_back(
+        projected, prior, masks, log_total, grad_mixed, cosine, signed_sine, score_scale
+    )
+    arrived = from_behind(grad_prior, "ctx", -1)
+    layer_own = after_own + hop_reduce(after(forward_sum, grad_prior))
+    shared_grad = jnp.concatenate(
+        [inner_grad[hid_e:hid], inner_grad[pad + hid_e : pad + hid], outer_grad[hid_e:hid]]
+    ).astype(jnp.bfloat16)
+    shared_parts = exchange_order(columns_of(after(shared_grad, grad_mixed), 8))
+    shared_parts = hop_trade(after(shared_parts, grad_prior))
+    arrived, layer_own, shared_parts = after((arrived, layer_own, shared_parts))
+    grad_linear, bias_part, gain_one_part, grad_one_part = project_back(
+        numbers, grad_query, grad_own, arrived, cosine, signed_sine, hidden_rows, qkv_parts
+    )
+    grad_normed_one = hop_reduce(grad_one_part)
+    residual_own = own_rows(hidden_rows).astype(jnp.float32)
+    residual_norm_grad, _ = jax.vjp(root_norm, residual_own, gains[0])[1](grad_normed_one)
+    input_own = (grad_after + residual_norm_grad).astype(jnp.bfloat16)
+    input_grad = line_gather(input_own).reshape(1, tokens, width)
+    layer_out = hop_gather(after(layer_own.astype(jnp.bfloat16), grad_one_part))
+    input_grad = after(input_grad, layer_out)
+    layer_out = layer_out.reshape(1, tokens, width)
+
+    grad_linear, late = after((grad_linear, grad_normed_one), grad_one_part)
+    qkv_full = project_weights(first_normalized, grad_linear)
+    qkv_grad = jnp.transpose(
+        lax.psum_scatter(
+            qkv_full.reshape(8 * 3 * deep, local_width),
+            ("fsdp", "ctx"),
+            scatter_dimension=0,
+            tiled=True,
+        ).reshape(3, deep, local_width),
+        (1, 0, 2),
+    ).astype(jnp.float32)
+
+    inner_grad, outer_grad = after((inner_grad, outer_grad), late)
+    inner_expert = jnp.transpose(
+        jnp.stack([inner_grad[:hid_e], inner_grad[pad : pad + hid_e]]), (2, 0, 1)
+    )[None]
+    outer_expert = outer_grad[:hid_e][None]
+    shared_back = jnp.stack(exchange_order(after(shared_parts, late)))
+    inner_shared = jnp.transpose(
+        jnp.stack([shared_back[:, :hid_s], shared_back[:, hid_s : 2 * hid_s]]).reshape(
+            2, 8 * hid_s, deep
+        ),
+        (2, 0, 1),
+    ).astype(jnp.float32)
+    outer_shared = shared_back[:, 2 * hid_s :].reshape(8 * hid_s, deep).astype(jnp.float32)
+
+    small = sum_over(
+        jnp.concatenate(
+            [
+                inner_grad[hid : hid + experts + 1],
+                after(gain_one_part, late),
+                gain_two_grad[None],
+            ]
+        ),
+        True,
+    )
+    router_grad = small[:experts].T
+    blend_grad = small[experts]
+    gains_grad = small[experts + 1 :]
+    bias_grad = sum_over(after(bias_part, late).reshape(3, local_width), False)
+    return (
+        layer_out,
+        input_grad,
+        gains_grad,
+        qkv_grad,
+        bias_grad,
+        projection_grad,
+        router_grad,
+        blend_grad,
+        inner_shared,
+        outer_shared,
+        inner_expert,
+        outer_expert,
+    )
+
+
 def solution(mesh):
     placed = (
         P("fsdp", "ctx", None),
@@ -452,8 +1618,9 @@
         P(("fsdp", "ctx"), "tp", None),
         P("fsdp", "ctx", None),
     )
+    plan = eight_plan if mesh.shape["fsdp"] == 4 and mesh.shape["ctx"] == 2 else general_plan
     return jax.shard_map(
-        on_device,
+        plan,
         mesh=mesh,
         in_specs=placed,
         out_specs=(

time: 2280 us -> 1120 us (0.49)
  waiting for transfers between devices: 900 us -> 363 us
  blocking collectives: 323 us -> 0 us
  local copies, waits for them, and re-layouts: 456 us -> 136 us
  Pallas kernels: 0 us -> 317 us
  matrix products: 253 us -> 6.16 us
  other arithmetic: 299 us -> 125 us
  starting transfers between devices: 20.3 us -> 144 us
    psum x3 -> x0, waiting for transfers between devices: 543 us -> none  [the longest x1 207 us: on_device(): lax.psum((blend[:, None] * shared_part + expert_part).astype(jnp.bfloat16...]
    pallas_call x0 -> x19, Pallas kernels: none -> 317 us  [the longest x4 105 us: mixture(): call(kernel, [jax.ShapeDtypeStruct((tokens, 2 * pad), jnp.bfloat16), jax....]
    ppermute x0 -> x83, waiting for transfers between devices: none -> 300 us  [the longest x16 87.9 us: swap_y(): return lax.ppermute(values, 'ctx', [(0, 1), (1, 0)])]
    all_to_all x2 -> x0, blocking collectives: 279 us -> none  [the longest x1 150 us: on_device(): lax.all_to_all(dispatch.reshape(groups, expert_local, capacity, width), (...]
    dot_general x30 -> x2, matrix products: 253 us -> 6.16 us  [the longest x1 5.65 us: eight_plan(): lax.dot_general(heads_own, grad_attn, (((1,), (0,)), ((), ())), preferred...]
    gather x10 -> x0, local copies, waits for them, and re-layouts: 167 us -> none  [the longest x4 58.9 us: on_device(): returned[pair_index[:, route_slot]]]
    all_to_all x2 -> x8, waiting for transfers between devices: 215 us -> 57.7 us  [the longest x5 51.5 us: line_gather(): return lax.all_to_all(copies, 'tp', split_axis=0, concat_axis=0, tiled=True)]
    unnamed x5 -> x16, other arithmetic: 138 us -> 3.7 us
  transfers between devices with their start and end apart: 17 -> 97, of which waited for: 11 -> 43; matrix products, arithmetic and copies ran while one was open for 29% -> 16% of each run, Pallas kernels for 0% -> 27%
where the time goes in v2:
time: 1120 us; the launch traced here: 1110 us
  waiting for transfers between devices  363 us (32%)
  Pallas kernels  317 us (28%)
  starting transfers between devices  144 us (13%)
  local copies, waits for them, and re-layouts  136 us (12%)
  other arithmetic  125 us (11%)
  between operations  16.2 us (1%)
    pallas_call x4, Pallas kernels, mixture(): call(kernel, [jax.ShapeDtypeStruct((tokens, 2 * pad), jnp.bfloat16), jax....  105 us
    ppermute x16, waiting for transfers between devices, swap_y(): return lax.ppermute(values, 'ctx', [(0, 1), (1, 0)])  87.9 us
    unnamed x250, local copies, waits for them, and re-layouts  71.9 us
    pallas_call x2, Pallas kernels, weight_gradients(): call(kernel, jax.ShapeDtypeStruct((units, width), jnp.float32), 2 * chips...  69.7 us
    all_to_all x5, waiting for transfers between devices, line_gather(): return lax.all_to_all(copies, 'tp', split_axis=0, concat_axis=0, tiled=True)  51.5 us
    convert_element_type x18, other arithmetic, add_low(): (one.astype(jnp.float32) + other.astype(jnp.float32)).astype(jnp.bfloat16)  46.6 us
    ppermute x17, waiting for transfers between devices, swap_x(): return lax.ppermute(values, 'fsdp', [(f, f ^ 2) for f in range(4)])  45.4 us
    ppermute x6, waiting for transfers between devices, hop_reduce(): lax.ppermute(to_right, 'tp', [(i, i + 1) for i in range(min(step, count -...  44.8 us
  transfers between devices with their start and end apart: 97, of which 43 were waited for; matrix products, arithmetic and copies ran while one was open for 16% of the time, Pallas kernels for 27%

profile of v2, /device:TPU:0, one launch (start us, length us, event | category | flops | bytes accessed | tf_op | source)
XLA Modules:
  0.0 1106.9 jit_solution(1098413809671143578)
XLA Ops:
  55.0 9.2 shard_map.238
  71.4 9.1 collective-permute-done.11
  113.5 13.2 %shard_map.239 = (bf16[704,512]{1,0:T(8,128)(2,1)S(1)}, f32[704,4]{1,0:T(8,128)S(1)}) custom-call(bf16[3,704,512]{2,1,0:T(8,128)(2,1)S(1)} %get-tuple-element.177.q_ref.own_ref, bf16[3,704,512]{2,1,0:T(8,128)(2,1)S(1)} %get-tuple-element.177.q_ref.own_ref, bf16[2,704,512]{2,1,0:T(8,128)(2,1)} %collective-permute-done.9.prior_ref, f32[704,704]{1,0:T(8,128)S(1)} %copy-done.5, ...), custom_call_target="tpu_custom_call" | custom-call | flops 2030043136 | bytes 8290304 | tf_op jit(solution)/shard_map/pallas_call | solution.py:720
  135.1 30.1 %collective-permute-done.19.others_1_ = bf16[2048,256]{1,0:T(8,128)(2,1)} collective-permute-done((bf16[2048,256]{1,0:T(8,128)(2,1)}, bf16[2048,256]{1,0:T(8,128)(2,1)}, u32[]{:S(2)}, u32[]{:S(2)}) %collective-permute-start.19) | collective-permute-done | bytes 1048608 | tf_op jit(solution)/shard_map/ppermute | solution.py:476
  167.6 8.4 collective-permute-done.13
  184.8 15.7 %collective-permute-done.21.others_3_ = bf16[2048,256]{1,0:T(8,128)(2,1)} collective-permute-done((bf16[2048,256]{1,0:T(8,128)(2,1)}, bf16[2048,256]{1,0:T(8,128)(2,1)}, u32[]{:S(2)}, u32[]{:S(2)}) %collective-permute-start.21) | collective-permute-done | bytes 1048608 | tf_op jit(solution)/shard_map/ppermute | solution.py:468
  242.7 7.8 all-to-all-done.2.mixed_ref
  255.7 11.6 %shard_map.243 = (bf16[704,2048]{1,0:T(8,128)(2,1)S(1)}, f32[176,2048]{1,0:T(8,128)S(1)}) custom-call(s32[2]{0:T(128)S(1)} %pad_add_fusion.number_ref.numbers_ref, bf16[704,2048]{1,0:T(8,128)(2,1)S(1)} %bitcast.187, f32[1,2048]{1,0:T(1,128)S(1)} %get-tuple-element.479.gain_ref, bf16[4,704,512]{2,1,0:T(8,128)(2,1)S(1)} %copy-done.9, ...), custom_call_target="tpu_custom_call" | custom-call | flops 5905580032 | bytes 17039360 | tf_op jit(solution)/shard_map/pallas_call | solution.py:1164
  284.4 26.6 %shard_map.244 = (bf16[1408,1280]{1,0:T(8,128)(2,1)}, bf16[1408,640]{1,0:T(8,128)(2,1)S(1)}, bf16[704,2048]{1,0:T(8,128)(2,1)S(1)}, bf16[704,2048]{1,0:T(8,128)(2,1)S(1)}) custom-call(f32[1408,1]{1,0:T(8,128)S(1)} %copy.58.kept_ref, f32[1,128]{1,0:T(1,128)S(1)} %compare_convert_fusion.mine_ref, bf16[1280,2048]{1,0:T(8,128)(2,1)} %copy-done.31, ...), custom_call_target="tpu_custom_call" | custom-call | flops 14763950080 | bytes 25788416 | tf_op jit(solution)/shard_map/pallas_call | solution.py:1109
  315.5 26.3 %all-to-all-done.3 = bf16[4,176,2048]{2,1,0:T(8,128)(2,1)} async-done(((bf16[4,176,2048]{2,1,0:T(8,128)(2,1)}), bf16[4,176,2048]{2,1,0:T(8,128)(2,1)}, u32[]{:S(2)}, u32[]{:S(2)}) %all-to-all-start.3) | async-done | bytes 2883616 | tf_op jit(solution)/shard_map/all_to_all | solution.py:542
  367.6 26.1 %shard_map.246 = (bf16[1408,1280]{1,0:T(8,128)(2,1)}, bf16[1408,640]{1,0:T(8,128)(2,1)S(1)}, bf16[704,2048]{1,0:T(8,128)(2,1)S(1)}, bf16[704,2048]{1,0:T(8,128)(2,1)S(1)}) custom-call(f32[1408,1]{1,0:T(8,128)S(1)} %copy.59.kept_ref, f32[1,128]{1,0:T(1,128)S(1)} %compare_convert_fusion.mine_ref, bf16[1280,2048]{1,0:T(8,128)(2,1)} %copy-done.31, ...), custom_call_target="tpu_custom_call" | custom-call | flops 14763950080 | bytes 25788416 | tf_op jit(solution)/shard_map/pallas_call | solution.py:1109
  398.6 17.5 %all-to-all-done.4 = bf16[4,176,2048]{2,1,0:T(8,128)(2,1)} async-done(((bf16[4,176,2048]{2,1,0:T(8,128)(2,1)}), bf16[4,176,2048]{2,1,0:T(8,128)(2,1)}, u32[]{:S(2)}, u32[]{:S(2)}) %all-to-all-start.4) | async-done | bytes 2883616 | tf_op jit(solution)/shard_map/all_to_all | solution.py:542
  416.1 26.9 %shard_map.247 = (bf16[1408,1280]{1,0:T(8,128)(2,1)}, bf16[1408,640]{1,0:T(8,128)(2,1)S(1)}, bf16[704,2048]{1,0:T(8,128)(2,1)}, bf16[704,2048]{1,0:T(8,128)(2,1)S(1)}) custom-call(f32[1408,1]{1,0:T(8,128)S(1)} %copy.60.kept_ref, f32[1,128]{1,0:T(1,128)S(1)} %compare_convert_fusion.mine_ref, bf16[1280,2048]{1,0:T(8,128)(2,1)} %copy-done.31, ...), custom_call_target="tpu_custom_call" | custom-call | flops 14763950080 | bytes 25788416 | tf_op jit(solution)/shard_map/pallas_call | solution.py:1109
  474.9 25.2 %shard_map.249 = (bf16[1408,1280]{1,0:T(8,128)(2,1)}, bf16[1408,640]{1,0:T(8,128)(2,1)S(1)}, bf16[704,2048]{1,0:T(8,128)(2,1)S(1)}, bf16[704,2048]{1,0:T(8,128)(2,1)S(1)}) custom-call(f32[1408,1]{1,0:T(8,128)S(1)} %copy.61.kept_ref, f32[1,128]{1,0:T(1,128)S(1)} %compare_convert_fusion.mine_ref, bf16[1280,2048]{1,0:T(8,128)(2,1)} %copy-done.31, ...), custom_call_target="tpu_custom_call" | custom-call | flops 14763950080 | bytes 25788416 | tf_op jit(solution)/shard_map/pallas_call | solution.py:1109
  513.0 35.5 %shard_map.250 = (bf16[704,2048]{1,0:T(8,128)(2,1)S(1)}, bf16[704,2048]{1,0:T(8,128)(2,1)}, bf16[704,2048]{1,0:T(8,128)(2,1)}, bf16[704,2048]{1,0:T(8,128)(2,1)}...) custom-call(bf16[640,2048]{1,0:T(8,128)(2,1)S(1)} %copy-done.44, ...), custom_call_target="tpu_custom_call" | custom-call | flops 14763950080 | bytes 32899072 | tf_op jit(solution)/shard_map/pallas_call | solution.py:1034
  569.5 16.9 %collective-permute-done.43 = bf16[352,2048]{1,0:T(8,128)(2,1)S(1)} collective-permute-done((bf16[352,2048]{1,0:T(8,128)(2,1)S(1)}, bf16[352,2048]{1,0:T(8,128)(2,1)S(1)}, u32[]{:S(2)}, u32[]{:S(2)}) %collective-permute-start.43) | collective-permute-done | bytes 1441824 | tf_op jit(solution)/shard_map/ppermute | solution.py:476
  610.1 26.8 %shard_map.251 = f32[640,2048]{1,0:T(8,128)} custom-call(bf16[1408,640]{1,0:T(8,128)(2,1)S(1)} %copy-done.74, bf16[1408,640]{1,0:T(8,128)(2,1)S(1)} %copy-done.77, bf16[1408,640]{1,0:T(8,128)(2,1)S(1)} %copy-done.80, bf16[1408,640]{1,0:T(8,128)(2,1)S(1)} %copy-done.82, bf16[704,2048]{1,0:T(8,128)(2,1)S(1)} %copy-done.34, bf16[704,2048]{1,0:T(8,128)(2,1)S(1)} %bitcast.183, ...), custom_call_target="tpu_custom_call" | custom-call | flops 14763950080 | bytes 35520512 | tf_op jit(solution)/shard_map/pallas_call | solution.py:1251
  641.0 42.9 %shard_map.252 = f32[1280,2048]{1,0:T(8,128)} custom-call(bf16[1408,1280]{1,0:T(8,128)(2,1)} %get-tuple-element.274.refs_0_, bf16[1408,1280]{1,0:T(8,128)(2,1)} %get-tuple-element.275.refs_1_, bf16[1408,1280]{1,0:T(8,128)(2,1)} %get-tuple-element.276.refs_2_, bf16[1408,1280]{1,0:T(8,128)(2,1)} %get-tuple-element.277.refs_3_, ...), custom_call_target="tpu_custom_call" | custom-call | flops 29527900160 | bytes 47972352 | tf_op jit(solution)/shard_map/pallas_call | solution.py:1251
  686.6 14.4 %collective-permute-done.50 = bf16[352,2048]{1,0:T(8,128)(2,1)} collective-permute-done((bf16[352,2048]{1,0:T(8,128)(2,1)}, bf16[352,2048]{1,0:T(8,128)(2,1)}, u32[]{:S(2)}, u32[]{:S(2)}) %collective-permute-start.50) | collective-permute-done | bytes 1441824 | tf_op jit(solution)/shard_map/ppermute | solution.py:468
  759.1 22.8 %shard_map.254 = (bf16[704,512]{1,0:T(8,128)(2,1)S(1)}, f32[2,704,512]{2,1,0:T(8,128)}, bf16[2,704,512]{2,1,0:T(8,128)(2,1)S(1)}) custom-call(bf16[3,704,512]{2,1,0:T(8,128)(2,1)S(1)} %copy-done.1, bf16[3,704,512]{2,1,0:T(8,128)(2,1)S(1)} %copy-done.1, bf16[2,704,512]{2,1,0:T(8,128)(2,1)} %collective-permute-done.9.prior_ref, f32[704,704]{1,0:T(8,128)S(1)} %copy-done.6, ...), custom_call_target="tpu_custom_call" | custom-call | flops 5075107840 | bytes 14778368 | tf_op jit(solution)/shard_map/pallas_call | solution.py:798
  790.6 7.6 collective-permute-done.55
  808.9 8.4 collective-permute-done.62
  834.4 9.5 collective-permute-done.57
  843.9 14.8 %collective-permute-done.60 = bf16[176,2048]{1,0:T(8,128)(2,1)} collective-permute-done((bf16[176,2048]{1,0:T(8,128)(2,1)}, bf16[176,2048]{1,0:T(8,128)(2,1)}, u32[]{:S(2)}, u32[]{:S(2)}) %collective-permute-start.60) | collective-permute-done | bytes 720928 | tf_op jit(solution)/shard_map/ppermute | solution.py:560
  861.5 8.7 shard_map.255
  874.8 11.8 %collective-permute-done.71 = bf16[176,2048]{1,0:T(8,128)(2,1)S(1)} collective-permute-done((bf16[176,2048]{1,0:T(8,128)(2,1)S(1)}, bf16[176,2048]{1,0:T(8,128)(2,1)S(1)}, u32[]{:S(2)}, u32[]{:S(2)}) %collective-permute-start.71) | collective-permute-done | bytes 720928 | tf_op jit(solution)/shard_map/ppermute | solution.py:559
  891.7 11.3 %collective-permute-done.72 = bf16[176,2048]{1,0:T(8,128)(2,1)S(1)} collective-permute-done((bf16[176,2048]{1,0:T(8,128)(2,1)S(1)}, bf16[176,2048]{1,0:T(8,128)(2,1)S(1)}, u32[]{:S(2)}, u32[]{:S(2)}) %collective-permute-start.72) | collective-permute-done | bytes 720928 | tf_op jit(solution)/shard_map/ppermute | solution.py:559
  920.3 20.1 %collective-permute-done.68 = bf16[176,2048]{1,0:T(8,128)(2,1)} collective-permute-done((bf16[176,2048]{1,0:T(8,128)(2,1)S(1)}, bf16[176,2048]{1,0:T(8,128)(2,1)}, u32[]{:S(2)}, u32[]{:S(2)}) %collective-permute-start.68) | collective-permute-done | bytes 720928 | tf_op jit(solution)/shard_map/ppermute | solution.py:576
  953.6 10.3 collective-permute-done.76
  979.2 21.7 %collective-permute-done.67 = bf16[176,2048]{1,0:T(8,128)(2,1)} collective-permute-done((bf16[176,2048]{1,0:T(8,128)(2,1)}, bf16[176,2048]{1,0:T(8,128)(2,1)}, u32[]{:S(2)}, u32[]{:S(2)}) %collective-permute-start.67) | collective-permute-done | bytes 720928 | tf_op jit(solution)/shard_map/ppermute | solution.py:579
  1054.3 14.4 %collective-permute-done.80 = f32[11,2048]{1,0:T(8,128)S(1)} collective-permute-done((f32[11,2048]{1,0:T(8,128)S(1)}, f32[11,2048]{1,0:T(8,128)S(1)}, u32[]{:S(2)}, u32[]{:S(2)}) %collective-permute-start.80) | collective-permute-done | bytes 90144 | tf_op jit(solution)/shard_map/ppermute | solution.py:528
  1078.9 11.1 %collective-permute-done.81 = f32[11,2048]{1,0:T(8,128)S(1)} collective-permute-done((f32[11,2048]{1,0:T(8,128)S(1)}, f32[11,2048]{1,0:T(8,128)S(1)}, u32[]{:S(2)}, u32[]{:S(2)}) %collective-permute-start.81) | collective-permute-done | bytes 90144 | tf_op jit(solution)/shard_map/ppermute | solution.py:528
  (593 shorter events, 528.1 us)
Async XLA Ops:
  7.2 97.9 %all-gather.2.cloned.1.call-start = ((), (), s32[]{:S(2)}) async-start(), calls=%async_computation.11 | async-start | bytes 1310720 | tf_op jit(solution)/shard_map/all_gather | solution.py:1306
  67.1 43.2 %collective-permute-start.9 = (bf16[2,704,512]{2,1,0:T(8,128)(2,1)}, bf16[2,704,512]{2,1,0:T(8,128)(2,1)}, u32[]{:S(2)}, u32[]{:S(2)}) collective-permute-start(bf16[2,704,512]{2,1,0:T(8,128)(2,1)} %slice.310), channel_id=1, source_target_pairs={{0,4},{1,5},{2,6},{3,7},{8,12},{9,13},{10,14},{11,15},{16,20},{17,... | collective-permute-start | bytes 4325384 | tf_op jit(solution)/shard_map/ppermute | solution.py:23
  83.5 94.3 %all-to-all-start.1 = ((bf16[4,176,2048]{2,1,0:T(8,128)(2,1)}), bf16[4,176,2048]{2,1,0:T(8,128)(2,1)}, u32[]{:S(2)}, u32[]{:S(2)}) async-start(bf16[4,176,2048]{2,1,0:T(8,128)(2,1)} %broadcast_in_dim.59), calls=%async_computation.1 | async-start | bytes 5767168 | tf_op jit(solution)/shard_map/all_to_all | solution.py:542
  126.8 38.4 %collective-permute-start.19 = (bf16[2048,256]{1,0:T(8,128)(2,1)}, bf16[2048,256]{1,0:T(8,128)(2,1)}, u32[]{:S(2)}, u32[]{:S(2)}) collective-permute-start(bf16[2048,256]{1,0:T(8,128)(2,1)} %all-gather.2.cloned.1.call-done.others_0_), channel_id=1, source_target_pairs={{0,4},{4,0},{1,5},{5,1},{2,6},{6,2},{3,7},{7,3},{8,12},{12,8},{9,1... | collective-permute-start | bytes 3145736 | tf_op jit(solution)/shard_map/ppermute | solution.py:476
  132.6 43.5 %collective-permute-start.13 = (bf16[1056,256]{1,0:T(8,128)(2,1)S(1)}, bf16[1056,256]{1,0:T(8,128)(2,1)S(1)}, u32[]{:S(2)}, u32[]{:S(2)}) collective-permute-start(bf16[1056,256]{1,0:T(8,128)(2,1)S(1)} %pad_maximum_fusion.7), channel_id=1, source_target_pairs={{0,4},{4,0},{1,5},{5,1},{2,6},{6,2},{3,7},{7,3},{8,12},{12,8},{9,1... | collective-permute-start | bytes 1622024 | tf_op jit(solution)/shard_map/ppermute | solution.py:476
  134.2 50.6 %collective-permute-start.20 = (bf16[2048,256]{1,0:T(8,128)(2,1)}, bf16[2048,256]{1,0:T(8,128)(2,1)}, u32[]{:S(2)}, u32[]{:S(2)}) collective-permute-start(bf16[2048,256]{1,0:T(8,128)(2,1)} %all-gather.2.cloned.1.call-done.others_0_), channel_id=1, source_target_pairs={{0,16},{8,24},{16,0},{24,8},{1,17},{9,25},{17,1},{25,9},{2,18},{10... | collective-permute-start | bytes 3145736 | tf_op jit(solution)/shard_map/ppermute | solution.py:468
  179.6 70.8 %all-to-all-start.2 = ((bf16[4,704,512]{2,1,0:T(8,128)(2,1)}), bf16[4,704,512]{2,1,0:T(8,128)(2,1)S(1)}, u32[]{:S(2)}, u32[]{:S(2)}) async-start(bf16[4,704,512]{2,1,0:T(8,128)(2,1)} %broadcast_in_dim.60), calls=%async_computation.2 | async-start | bytes 5767168 | tf_op jit(solution)/shard_map/all_to_all | solution.py:542
  204.2 47.9 %collective-permute-start.22 = (bf16[8192,256]{1,0:T(8,128)(2,1)}, bf16[8192,256]{1,0:T(8,128)(2,1)}, u32[]{:S(2)}, u32[]{:S(2)}) collective-permute-start(bf16[8192,256]{1,0:T(8,128)(2,1)} %pad_maximum_fusion), channel_id=1, source_target_pairs={{0,8},{8,0},{16,24},{24,16},{1,9},{9,1},{17,25},{25,17},{2,10},{10... | collective-permute-start | bytes 12582920 | tf_op jit(solution)/shard_map/ppermute | solution.py:472
  272.0 69.9 %all-to-all-start.3 = ((bf16[4,176,2048]{2,1,0:T(8,128)(2,1)}), bf16[4,176,2048]{2,1,0:T(8,128)(2,1)}, u32[]{:S(2)}, u32[]{:S(2)}) async-start(bf16[4,176,2048]{2,1,0:T(8,128)(2,1)} %broadcast_in_dim.61), calls=%async_computation.3 | async-start | bytes 5767168 | tf_op jit(solution)/shard_map/all_to_all | solution.py:542
  277.0 73.1 %collective-permute-start.27 = (bf16[704,2048]{1,0:T(8,128)(2,1)}, bf16[704,2048]{1,0:T(8,128)(2,1)}, u32[]{:S(2)}, u32[]{:S(2)}) collective-permute-start(bf16[704,2048]{1,0:T(8,128)(2,1)} %copy-done.35), channel_id=1, source_target_pairs={{0,4},{4,0},{1,5},{5,1},{2,6},{6,2},{3,7},{7,3},{8,12},{12,8},{9,1... | collective-permute-start | bytes 8650760 | tf_op jit(solution)/shard_map/ppermute | solution.py:476
  278.8 71.3 %collective-permute-start.26 = (bf16[704,2048]{1,0:T(8,128)(2,1)}, bf16[704,2048]{1,0:T(8,128)(2,1)}, u32[]{:S(2)}, u32[]{:S(2)}) collective-permute-start(bf16[704,2048]{1,0:T(8,128)(2,1)} %copy-done.35), channel_id=1, source_target_pairs={{0,16},{8,24},{16,0},{24,8},{1,17},{9,25},{17,1},{25,9},{2,18},{10... | collective-permute-start | bytes 8650760 | tf_op jit(solution)/shard_map/ppermute | solution.py:468
  344.9 71.2 %all-to-all-start.4 = ((bf16[4,176,2048]{2,1,0:T(8,128)(2,1)}), bf16[4,176,2048]{2,1,0:T(8,128)(2,1)}, u32[]{:S(2)}, u32[]{:S(2)}) async-start(bf16[4,176,2048]{2,1,0:T(8,128)(2,1)} %broadcast_in_dim.62), calls=%async_computation.4 | async-start | bytes 5767168 | tf_op jit(solution)/shard_map/all_to_all | solution.py:542
  350.6 47.6 %collective-permute-start.24 = (bf16[704,2048]{1,0:T(8,128)(2,1)}, bf16[704,2048]{1,0:T(8,128)(2,1)}, u32[]{:S(2)}, u32[]{:S(2)}) collective-permute-start(bf16[704,2048]{1,0:T(8,128)(2,1)} %copy-done.38), channel_id=1, source_target_pairs={{0,8},{8,0},{16,24},{24,16},{1,9},{9,1},{17,25},{25,17},{2,10},{10... | collective-permute-start | bytes 8650760 | tf_op jit(solution)/shard_map/ppermute | solution.py:472
  350.7 65.4 %collective-permute-start.33 = (bf16[704,2048]{1,0:T(8,128)(2,1)}, bf16[704,2048]{1,0:T(8,128)(2,1)}, u32[]{:S(2)}, u32[]{:S(2)}) collective-permute-start(bf16[704,2048]{1,0:T(8,128)(2,1)} %collective-permute-done.27.others_1_.refs_9_), channel_id=1, source_target_pairs={{0,8},{8,0},{16,24},{24,16},{1,9},{9,1},{17,25},{25,17},{2,10},{10... | collective-permute-start | bytes 8650760 | tf_op jit(solution)/shard_map/ppermute | solution.py:472
  356.7 41.6 %collective-permute-start.31 = (bf16[352,2048]{1,0:T(8,128)(2,1)}, bf16[352,2048]{1,0:T(8,128)(2,1)}, u32[]{:S(2)}, u32[]{:S(2)}) collective-permute-start(bf16[352,2048]{1,0:T(8,128)(2,1)} %slice.344), channel_id=1, source_target_pairs={{0,16},{8,24},{16,0},{24,8},{1,17},{9,25},{17,1},{25,9},{2,18},{10... | collective-permute-start | bytes 4325384 | tf_op jit(solution)/shard_map/ppermute | solution.py:468
  357.0 41.3 %collective-permute-start.32 = (bf16[352,2048]{1,0:T(8,128)(2,1)}, bf16[352,2048]{1,0:T(8,128)(2,1)}, u32[]{:S(2)}, u32[]{:S(2)}) collective-permute-start(bf16[352,2048]{1,0:T(8,128)(2,1)} %slice.345), channel_id=1, source_target_pairs={{0,4},{4,0},{1,5},{5,1},{2,6},{6,2},{3,7},{7,3},{8,12},{12,8},{9,1... | collective-permute-start | bytes 4325384 | tf_op jit(solution)/shard_map/ppermute | solution.py:476
  398.6 51.3 %collective-permute-start.29 = (bf16[704,2048]{1,0:T(8,128)(2,1)}, bf16[704,2048]{1,0:T(8,128)(2,1)}, u32[]{:S(2)}, u32[]{:S(2)}) collective-permute-start(bf16[704,2048]{1,0:T(8,128)(2,1)} %copy-done.39), channel_id=1, source_target_pairs={{0,8},{8,0},{16,24},{24,16},{1,9},{9,1},{17,25},{25,17},{2,10},{10... | collective-permute-start | bytes 8650760 | tf_op jit(solution)/shard_map/ppermute | solution.py:472
  416.1 38.8 %collective-permute-start.35 = (bf16[704,2048]{1,0:T(8,128)(2,1)}, bf16[704,2048]{1,0:T(8,128)(2,1)}, u32[]{:S(2)}, u32[]{:S(2)}) collective-permute-start(bf16[704,2048]{1,0:T(8,128)(2,1)} %bitcast.37.refs_1_.refs_11_), channel_id=1, source_target_pairs={{0,8},{8,0},{16,24},{24,16},{1,9},{9,1},{17,25},{25,17},{2,10},{10... | collective-permute-start | bytes 8650760 | tf_op jit(solution)/shard_map/ppermute | solution.py:472
  454.6 45.6 %collective-permute-start.30 = (bf16[352,2048]{1,0:T(8,128)(2,1)}, bf16[352,2048]{1,0:T(8,128)(2,1)}, u32[]{:S(2)}, u32[]{:S(2)}) collective-permute-start(bf16[352,2048]{1,0:T(8,128)(2,1)} %get-tuple-element.404), channel_id=1, source_target_pairs={{0,16},{8,24},{16,0},{24,8},{1,17},{9,25},{17,1},{25,9},{2,18},{10... | collective-permute-start | bytes 4325384 | tf_op jit(solution)/shard_map/ppermute | solution.py:468
  509.5 39.0 %collective-permute-start.41 = (bf16[352,2048]{1,0:T(8,128)(2,1)}, bf16[352,2048]{1,0:T(8,128)(2,1)S(1)}, u32[]{:S(2)}, u32[]{:S(2)}) collective-permute-start(bf16[352,2048]{1,0:T(8,128)(2,1)} %get-tuple-element.399), channel_id=1, source_target_pairs={{0,4},{4,0},{1,5},{5,1},{2,6},{6,2},{3,7},{7,3},{8,12},{12,8},{9,1... | collective-permute-start | bytes 4325384 | tf_op jit(solution)/shard_map/ppermute | solution.py:476
  593.7 90.2 %all-to-all-start.5 = ((bf16[4,176,2048]{2,1,0:T(8,128)(2,1)}), bf16[4,176,2048]{2,1,0:T(8,128)(2,1)}, u32[]{:S(2)}, u32[]{:S(2)}) async-start(bf16[4,176,2048]{2,1,0:T(8,128)(2,1)} %bitcast.205), calls=%async_computation.5 | async-start | bytes 5767168 | tf_op jit(solution)/shard_map/all_to_all | solution.py:536
  598.4 307.8 %reduce-scatter.6.cloned.1.call-start = ((), (), s32[]{:S(2)}) async-start(), calls=%async_computation.13 | async-start | bytes 9437184 | tf_op jit(solution)/shard_map/reduce_scatter | solution.py:1512
  636.9 49.7 %collective-permute-start.48 = (bf16[352,2048]{1,0:T(8,128)(2,1)}, bf16[352,2048]{1,0:T(8,128)(2,1)}, u32[]{:S(2)}, u32[]{:S(2)}) collective-permute-start(bf16[352,2048]{1,0:T(8,128)(2,1)} %get-tuple-element.265), channel_id=1, source_target_pairs={{0,16},{8,24},{16,0},{24,8},{1,17},{9,25},{17,1},{25,9},{2,18},{10... | collective-permute-start | bytes 4325384 | tf_op jit(solution)/shard_map/ppermute | solution.py:468
  637.5 49.1 %collective-permute-start.49 = (bf16[352,2048]{1,0:T(8,128)(2,1)}, bf16[352,2048]{1,0:T(8,128)(2,1)}, u32[]{:S(2)}, u32[]{:S(2)}) collective-permute-start(bf16[352,2048]{1,0:T(8,128)(2,1)} %get-tuple-element.266), channel_id=1, source_target_pairs={{0,4},{4,0},{1,5},{5,1},{2,6},{6,2},{3,7},{7,3},{8,12},{12,8},{9,1... | collective-permute-start | bytes 4325384 | tf_op jit(solution)/shard_map/ppermute | solution.py:476
  638.4 62.5 %collective-permute-start.50 = (bf16[352,2048]{1,0:T(8,128)(2,1)}, bf16[352,2048]{1,0:T(8,128)(2,1)}, u32[]{:S(2)}, u32[]{:S(2)}) collective-permute-start(bf16[352,2048]{1,0:T(8,128)(2,1)} %get-tuple-element.267), channel_id=1, source_target_pairs={{0,16},{8,24},{16,0},{24,8},{1,17},{9,25},{17,1},{25,9},{2,18},{10... | collective-permute-start | bytes 4325384 | tf_op jit(solution)/shard_map/ppermute | solution.py:468
  640.1 60.9 %collective-permute-start.51 = (bf16[352,2048]{1,0:T(8,128)(2,1)}, bf16[352,2048]{1,0:T(8,128)(2,1)}, u32[]{:S(2)}, u32[]{:S(2)}) collective-permute-start(bf16[352,2048]{1,0:T(8,128)(2,1)} %get-tuple-element.268), channel_id=1, source_target_pairs={{0,4},{4,0},{1,5},{5,1},{2,6},{6,2},{3,7},{7,3},{8,12},{12,8},{9,1... | collective-permute-start | bytes 4325384 | tf_op jit(solution)/shard_map/ppermute | solution.py:476
  729.5 362.4 %reduce-scatter.8.cloned.1.call-start = ((), (), s32[]{:S(2)}) async-start(), calls=%async_computation.14 | async-start | bytes 1310720 | tf_op jit(solution)/shard_map/reduce_scatter | solution.py:1518
  823.1 38.4 %collective-permute-start.54 = (bf16[2,704,512]{2,1,0:T(8,128)(2,1)}, bf16[2,704,512]{2,1,0:T(8,128)(2,1)}, u32[]{:S(2)}, u32[]{:S(2)}) collective-permute-start(bf16[2,704,512]{2,1,0:T(8,128)(2,1)} %copy-done.51), channel_id=1, source_target_pairs={{4,0},{5,1},{6,2},{7,3},{12,8},{13,9},{14,10},{15,11},{20,16},{21,... | collective-permute-start | bytes 4325384 | tf_op jit(solution)/shard_map/ppermute | solution.py:23
  906.3 187.4 %reduce-scatter.4.cloned.1.call-start = ((), (), s32[]{:S(2)}) async-start(), calls=%async_computation.12 | async-start | bytes 7077888 | tf_op jit(solution)/shard_map/reduce_scatter | solution.py:1550
  912.7 40.9 %collective-permute-start.73 = (bf16[176,2048]{1,0:T(8,128)(2,1)}, bf16[176,2048]{1,0:T(8,128)(2,1)S(1)}, u32[]{:S(2)}, u32[]{:S(2)}) collective-permute-start(bf16[176,2048]{1,0:T(8,128)(2,1)} %get-tuple-element.413), channel_id=1, source_target_pairs={{0,1},{1,2},{2,3},{4,5},{5,6},{6,7},{8,9},{9,10},{10,11},{12,13},{... | collective-permute-start | bytes 2162696 | tf_op jit(solution)/shard_map/ppermute | solution.py:559
  919.0 44.9 %collective-permute-start.76 = (bf16[176,2048]{1,0:T(8,128)(2,1)S(1)}, bf16[176,2048]{1,0:T(8,128)(2,1)S(1)}, u32[]{:S(2)}, u32[]{:S(2)}) collective-permute-start(bf16[176,2048]{1,0:T(8,128)(2,1)S(1)} %fusion.16), channel_id=1, source_target_pairs={{1,0},{2,1},{3,2},{5,4},{6,5},{7,6},{9,8},{10,9},{11,10},{13,12},{... | collective-permute-start | bytes 2162696 | tf_op jit(solution)/shard_map/ppermute | solution.py:560
  1013.5 78.3 %all-to-all-start.7 = ((bf16[4,176,2048]{2,1,0:T(8,128)(2,1)}), bf16[4,176,2048]{2,1,0:T(8,128)(2,1)}, u32[]{:S(2)}, u32[]{:S(2)}) async-start(bf16[4,176,2048]{2,1,0:T(8,128)(2,1)} %broadcast_in_dim.116), calls=%async_computation.7 | async-start | bytes 5767168 | tf_op jit(solution)/shard_map/all_to_all | solution.py:542
  (189 other events, 2447.8 us)
Sparse Core Ops, SparseCore 0:
  12.0 28.2 all-gather.1
  724.8 76.3 reduce-scatter.5
  906.4 44.5 reduce-scatter.7
  976.4 72.2 reduce-scatter.3

commit v3 on v2

--- a/solution.py
+++ b/solution.py
@@ -448,11 +448,11 @@
     return lax.dot_general(one, other, dims, preferred_element_type=jnp.float32)
 
 
-def call(kernel, shapes, flops, moved, **others):
+def call(kernel, shapes, flops, moved, room=40, **others):
     return pl.pallas_call(
         kernel,
         out_shape=shapes,
-        compiler_params=pltpu.CompilerParams(vmem_limit_bytes=40 * 2**20),
+        compiler_params=pltpu.CompilerParams(vmem_limit_bytes=room * 2**20),
         cost_estimate=pl.CostEstimate(
             flops=int(flops), bytes_accessed=int(moved), transcendentals=0
         ),
@@ -501,10 +501,13 @@
     return swap_x(taken[1][0]), swap_y(taken[2][1]), swap_x(taken[3][0]), swap_y(taken[3][1])
 
 
-def last_hops(taken, hops):
+def last_parts(taken, hops):
     _, _, both_low, both_high = hops
-    for_x, for_y = add_low(taken[1][1], both_high), add_low(taken[2][0], both_low)
-    return swap_x(for_x), swap_y(for_y)
+    return add_low(taken[1][1], both_high), add_low(taken[2][0], both_low)
+
+
+def last_hops(parts):
+    return swap_x(parts[0]), swap_y(parts[1])
 
 
 def hops_sum(taken, hops, ends):
@@ -517,16 +520,18 @@
     return jnp.concatenate(sums).astype(jnp.bfloat16)
 
 
-def sum_over(values, with_tp):
+def sum_eight(values):
     values = values + swap_core(values)
     values = values + swap_x(values)
-    values = values + swap_y(values)
-    if with_tp:
-        count = lax.axis_size("tp")
-        bit = 1
-        while bit < count:
-            values = values + lax.ppermute(values, "tp", [(i, i ^ bit) for i in range(count)])
-            bit *= 2
+    return values + swap_y(values)
+
+
+def sum_line(values):
+    count = lax.axis_size("tp")
+    bit = 1
+    while bit < count:
+        values = values + lax.ppermute(values, "tp", [(i, i ^ bit) for i in range(count)])
+        bit *= 2
     return values
 
 
@@ -546,12 +551,14 @@
     return lax.dynamic_index_in_dim(blocks, index, axis=0, keepdims=False)
 
 
-def hop_reduce(rows):
+def hop_reduce(rows, earlier=()):
     count = lax.axis_size("tp")
     me = lax.axis_index("tp")
     blocks = rows.reshape((count, rows.shape[0] // count) + rows.shape[1:])
-    right, left = None, None
+    right, left, first = None, None, None
     for step in range(1, count):
+        if step == 2:
+            right, left = first = after((right, left), earlier)
         to_right = pick(blocks, jnp.minimum(count - step + me, count - 1))
         to_left = pick(blocks, jnp.maximum(step + me - count, 0))
         if step > 1:
@@ -560,11 +567,12 @@
         left = lax.ppermute(
             to_left, "tp", [(i, i - 1) for i in range(max(count - step, 1), count)]
         )
-    return (
+    total = (
         pick(blocks, me).astype(jnp.float32)
         + right.astype(jnp.float32)
         + left.astype(jnp.float32)
     )
+    return total, first
 
 
 def hop_gather(block):
@@ -588,15 +596,21 @@
     return jnp.concatenate(result)
 
 
-def hop_trade(parts):
+def trade_chips(parts):
+    return (
+        swap_y(jnp.concatenate([parts[1], parts[3]])),
+        swap_x(jnp.concatenate([parts[4], parts[6]])),
+        lax.ppermute(
+            jnp.concatenate([parts[5], parts[7]]),
+            ("fsdp", "ctx"),
+            [(d, d ^ 5) for d in range(8)],
+        ),
+    )
+
+
+def trade_cores(parts, arrived):
     rows = parts[0].shape[0]
-    from_y = swap_y(jnp.concatenate([parts[1], parts[3]]))
-    from_x = swap_x(jnp.concatenate([parts[4], parts[6]]))
-    both = lax.ppermute(
-        jnp.concatenate([parts[5], parts[7]]),
-        ("fsdp", "ctx"),
-        [(d, d ^ 5) for d in range(8)],
-    )
+    from_y, from_x, both = arrived
     sibling = swap_core(
         jnp.concatenate([parts[2], from_y[rows:], from_x[rows:], both[rows:]])
     )
@@ -983,14 +997,41 @@
     return buffer[lax.rem(tile, 2)]
 
 
-def narrow(pieces, other):
-    starts = tiles_of(pieces)
-    units, width = other.shape
-
-    def kernel(other_ref, *refs):
-        piece_refs, (out_ref, buffer, sems) = refs[: len(pieces)], refs[len(pieces) :]
-        rows = next_tile(piece_refs, starts, buffer, sems)
-        out_ref[...] = product(rows, other_ref[...], ROWS_ROWS)
+CHIPS = (2, 0, 6, 4, 3, 1, 7, 5)
+
+
+def narrow(numbers, blocks, chosen, other):
+    gathered = not isinstance(blocks, list)
+    blocks = [blocks] if gathered else blocks
+    each, width = blocks[0].shape[-2:]
+    units = other.shape[0]
+    tiles = each // MIX_ROWS
+    starts = [(at, t * MIX_ROWS) for at in range(len(chosen)) for t in range(tiles)]
+
+    def kernel(numbers_ref, other_ref, *refs):
+        block_refs, (out_ref, buffer, sems) = refs[: len(blocks)], refs[len(blocks) :]
+        tile = pl.program_id(0)
+
+        def copy(number):
+            at, first = starts[number]
+            block = block_refs[0].at[numbers_ref[0] ^ chosen[at]] if gathered else block_refs[at]
+            return pltpu.make_async_copy(
+                block.at[pl.ds(first, MIX_ROWS)],
+                buffer.at[number % 2],
+                sems.at[number % 2],
+            )
+
+        for number in range(len(starts)):
+
+            @pl.when(tile == number)
+            def _():
+                if number == 0:
+                    copy(0).start()
+                if number + 1 < len(starts):
+                    copy(number + 1).start()
+                copy(number).wait()
+
+        out_ref[...] = product(buffer[lax.rem(tile, 2)], other_ref[...], ROWS_ROWS)
 
     tokens = len(starts) * MIX_ROWS
     return call(
@@ -999,13 +1040,13 @@
         2 * tokens * units * width,
         2 * (tokens * width + units * width + 2 * tokens * units),
         grid=(len(starts),),
-        in_specs=[pl.BlockSpec((units, width), lambda i: (0, 0))] + [ANY] * len(pieces),
+        in_specs=[SMEM, pl.BlockSpec((units, width), lambda i: (0, 0))] + [ANY] * len(blocks),
         out_specs=pl.BlockSpec((MIX_ROWS, units), lambda i: (i, 0)),
         scratch_shapes=[
             pltpu.VMEM((2, MIX_ROWS, width), jnp.bfloat16),
             pltpu.SemaphoreType.DMA((2,)),
         ],
-    )(other, *pieces)
+    )(numbers, other, *blocks)
 
 
 def widen(parts, other):
@@ -1046,8 +1087,8 @@
     )(other, *parts)
 
 
-def mixture(row_pieces, upstream, kept, mine, inner, hid_e, hid, experts):
-    tokens, pad = upstream.shape
+def mixture(row_pieces, upstream, chip, kept, mine, inner, hid_e, hid, experts):
+    tokens, pad = kept.shape[0], upstream.shape[1]
     width = inner.shape[1]
     starts = tiles_of(row_pieces)
     tiles = len(starts)
@@ -1117,7 +1158,12 @@
         8 * tokens * pad * width,
         2 * (2 * tokens * width + 5 * tokens * pad + 2 * pad * width),
         grid=(tiles,),
-        in_specs=[row_block(1), whole(1, LANES), whole(2 * pad, width), row_block(pad)]
+        in_specs=[
+            row_block(1),
+            whole(1, LANES),
+            whole(2 * pad, width),
+            pl.BlockSpec((MIX_ROWS, pad), lambda i: (i + chip * tiles, 0)),
+        ]
         + [ANY] * count,
         out_specs=[
             row_block(2 * pad),
@@ -1169,6 +1215,7 @@
         ],
         2 * tokens * width * long,
         2 * (3 * tokens * width + long * width),
+        room=62,
         grid=(count,),
         in_specs=[
             SMEM,
@@ -1216,51 +1263,58 @@
     )(numbers, grads, *own_weights, other_weights)
 
 
-def weight_gradients(parts, row_pieces, tile):
-    units = parts[0].shape[1]
-    width = row_pieces[0][0].shape[1]
+def weight_gradients(numbers, parts, pieces, units, first=0, blocks=None):
     tokens = parts[0].shape[0]
-    pieces = [piece for chip in row_pieces for piece in chip]
-    firsts = [sum(p.shape[0] for p in pieces[:i]) for i in range(len(pieces))]
     chips = len(parts)
-
-    def kernel(*refs):
+    if blocks is None:
+        pieces = [piece for chip in pieces for piece in chip]
+        long = [p.shape[0] for p in pieces]
+    else:
+        pieces = [blocks]
+        long = [blocks.shape[1]] * 8
+    width = pieces[0].shape[-1]
+    firsts = [sum(long[:i]) for i in range(len(long))]
+
+    def kernel(numbers_ref, *refs):
         part_refs, piece_refs = refs[:chips], refs[chips : chips + len(pieces)]
         out_ref, buffer, sems = refs[chips + len(pieces) :]
+
+        def source(i):
+            return piece_refs[i] if blocks is None else piece_refs[0].at[numbers_ref[0] ^ CHIPS[i]]
+
         copies = [
-            pltpu.make_async_copy(
-                ref, buffer.at[pl.ds(firsts[i], pieces[i].shape[0])], sems.at[i]
-            )
-            for i, ref in enumerate(piece_refs)
+            pltpu.make_async_copy(source(i), buffer.at[pl.ds(firsts[i], long[i])], sems.at[i])
+            for i in range(len(long))
         ]
-
-        @pl.when(pl.program_id(0) == 0)
-        def _():
-            for copy in copies:
-                copy.start()
-            for copy in copies:
-                copy.wait()
-
-        total = None
+        for copy in copies:
+            copy.start()
+        waited = 0
         for chip in range(chips):
+            while waited < len(long) and firsts[waited] < (chip + 1) * tokens:
+                copies[waited].wait()
+                waited += 1
             rows = buffer[chip * tokens : (chip + 1) * tokens]
             term = product(part_refs[chip][...], rows, COLS_COLS)
-            total = term if total is None else total + term
-        out_ref[...] = total
+            if chip == 0:
+                out_ref[...] = term
+            else:
+                out_ref[...] += term
 
     return call(
         kernel,
         jax.ShapeDtypeStruct((units, width), jnp.float32),
         2 * chips * tokens * units * width,
         2 * chips * tokens * (units + width) + 4 * units * width,
-        grid=(units // tile,),
-        in_specs=[pl.BlockSpec((tokens, tile), lambda i: (0, i))] * chips + [ANY] * len(pieces),
-        out_specs=pl.BlockSpec((tile, width), lambda i: (i, 0)),
+        grid=(1,),
+        in_specs=[SMEM]
+        + [pl.BlockSpec((tokens, units), lambda i: (0, first))] * chips
+        + [ANY] * len(pieces),
+        out_specs=pl.BlockSpec((units, width), lambda i: (0, 0)),
         scratch_shapes=[
             pltpu.VMEM((chips * tokens, width), jnp.bfloat16),
-            pltpu.SemaphoreType.DMA((len(pieces),)),
-        ],
-    )(*parts, *pieces)
+            pltpu.SemaphoreType.DMA((len(long),)),
+        ],
+    )(numbers, *parts, *pieces)
 
 
 def eight_plan(
@@ -1297,9 +1351,6 @@
     def own_rows(values):
         return lax.dynamic_slice_in_dim(values, me_tp * share, share, axis=0)
 
-    def own_columns(heads):
-        return lax.dynamic_slice_in_dim(heads, me_tp * share, share, axis=1)
-
     qkv_own = jnp.transpose(qkv_weight, (1, 0, 2))
     qkv_x, qkv_y = swap_x(qkv_own), swap_y(qkv_own)
     qkv_sibling = swap_core(qkv_own)
@@ -1355,7 +1406,7 @@
         axis=1,
     )
 
-    (qkv_x, qkv_y), early_kept = after((qkv_x, qkv_y), kept_all), kept_blocks
+    qkv_x, qkv_y, cosine, signed_sine = after((qkv_x, qkv_y, cosine, signed_sine), kept_all)
     qkv_low = swap_x(qkv_y[:, :, :half_width])
     qkv_high = swap_y(qkv_x[:, :, half_width:])
     qkv_parts = [
@@ -1369,12 +1420,9 @@
         [swap_core(qkv_low), swap_core(qkv_high)],
     ]
     hidden_rows = hidden_in.reshape(tokens, width)
-    hidden_first, (cosine, signed_sine), masks = after(
-        (hidden_rows, (cosine, signed_sine), masks), early_kept
-    )
     projected, first_normalized = project(
         numbers,
-        hidden_first,
+        hidden_rows,
         gains[:1],
         qkv_parts,
         qkv_bias.astype(jnp.float32)[:, None],
@@ -1383,32 +1431,38 @@
     )
     prior = from_behind(projected[1:], "ctx", 1)
 
+    out_own = after(out_line, qkv_low, qkv_high)
+    out_x, out_y = swap_x(out_own), swap_y(out_own)
+    out_both = swap_x(out_y)
+    prior = after(prior, out_x, out_both, kept_blocks)
     grad_rows = cotangent.reshape(tokens, width)
-    grads_share = after(own_rows(grad_rows), qkv_low, qkv_high)
-    grads_x, grads_y = swap_x(grads_share), swap_y(grads_share)
-    grads_both = lax.ppermute(grads_share, ("fsdp", "ctx"), [(d, d ^ 5) for d in range(8)])
-    grads_x, grads_y, grads_both = after((grads_x, grads_y, grads_both), projected)
-    grads_x = line_gather(grads_x).reshape(tokens, width)
-
-    out_own = after(out_line, qkv_low, qkv_high)
-    out_x = swap_x(out_own)
-
-    prior = after(prior, grads_y, grads_both)
+    all_grads = lax.all_gather(
+        after(grad_rows, prior), ("fsdp", "ctx"), axis=0, tiled=False
+    )
+
+    grads_sibling = swap_core(after(grad_rows, projected))
+
     mixed_result, log_total = attend(projected, prior, masks, score_scale)
-    mixed_all = line_gather(after(mixed_result, grads_x))
-
-    to_trade, out_late = after((to_trade, out_own), mixed_result)
-    out_y = swap_y(out_late)
-    out_both = swap_x(out_y)
-    traded = hop_trade(exchange_order([to_trade[d] for d in range(8)]))
+    mixed_all = line_gather(mixed_result)
+
     out_mine = [out_own, out_y, out_x, out_both]
     out_other = swap_core(after(jnp.concatenate(out_mine), mixed_result))
-    grads_sibling = swap_core(after(grad_rows, projected))
+    to_trade = after(to_trade, mixed_result)
+    parts_to_trade = exchange_order([to_trade[d] for d in range(8)])
     hidden_rows = hidden_in.reshape(tokens, width)
+
+    trade_arrived = trade_chips(parts_to_trade)
+    mixed_all, trade_arrived = after((mixed_all, trade_arrived))
+    second_normalized, after_own = attend_out(
+        numbers, hidden_rows, gains[1:], mixed_all, out_mine, out_other
+    )
+    rows_x, rows_y = swap_x(second_normalized), swap_y(second_normalized)
+    row_chips = [[swap_core(second_normalized), second_normalized]]
+    traded = trade_cores(parts_to_trade, after(trade_arrived, row_chips[0]))
 
     kept_rel = exchange_order([kept_blocks[i].reshape(tokens, 1) for i in range(8)])
     kept_chips = [jnp.concatenate([kept_rel[p + 2], kept_rel[p]]) for p in (0, 4, 1, 5)]
-    shared_rows = jnp.concatenate(exchange_order(after(traded, mixed_result)), axis=1)
+    shared_rows = jnp.concatenate(exchange_order(after(traded, second_normalized)), axis=1)
     hid_e = expert_inner.shape[3]
     hid = hid_e + hid_s
     router_rows = jnp.concatenate(
@@ -1429,21 +1483,13 @@
     mine = (
         jnp.arange(LANES, dtype=jnp.int32) == number + (hid - (pad - LANES))
     ).astype(jnp.float32)[None]
-    grad_chips = [[grads_sibling, grad_rows], [swap_core(grads_x), grads_x]]
-    upstream = [narrow(grad_chips[0], outer)]
-    upstream.append(narrow(after(grad_chips[1], upstream[0]), outer))
-    mixed_all, upstream = after((mixed_all, upstream))
-    second_normalized, after_own = attend_out(
-        numbers, hidden_rows, gains[1:], mixed_all, out_mine, out_other
-    )
-    grads_y = line_gather(after(grads_y, second_normalized)).reshape(tokens, width)
-    rows_x, rows_y = swap_x(second_normalized), swap_y(second_normalized)
-    row_chips = [[swap_core(second_normalized), second_normalized]]
+    upstream_own = narrow(numbers, [grads_sibling, grad_rows], CHIPS[:2], outer)
 
     def mix(chip, *earlier):
         return mixture(
             row_chips[chip],
-            upstream[chip],
+            upstream if chip else upstream_own,
+            max(chip - 1, 0),
             after(kept_chips[chip], earlier),
             mine,
             inner,
@@ -1452,49 +1498,52 @@
             experts,
         )
 
+    half = tokens // 2
     mixes = [mix(0)]
+    upstream = narrow(numbers, after(all_grads, mixes[0][0]), CHIPS[2:], outer)
     back_arrived = [swap_core(mixes[0][2])]
-    rows_x, rows_y = after((rows_x, rows_y), mixes[0][0])
+    rows_x, rows_y = after((rows_x, rows_y), upstream)
     rows_low = swap_x(rows_y[: tokens // 2])
     rows_high = swap_y(rows_x[tokens // 2 :])
     row_chips += [[swap_core(rows_x), rows_x], [swap_core(rows_y), rows_y]]
-    grads_y = after(grads_y, mixes[0][0])
-    grad_chips.append([swap_core(grads_y), grads_y])
-    grads_both = line_gather(after(grads_both, grads_y)).reshape(tokens, width)
-    upstream.append(narrow(grad_chips[2], outer))
-    mixes.append(mix(1, upstream[2]))
+    mixes.append(mix(1))
     back_arrived.append(swap_core(mixes[1][2]))
     rows_low, rows_high = after((rows_low, rows_high), mixes[1][0])
     mixes.append(mix(2, back_arrived[0], rows_low, rows_high))
     back_arrived.append(swap_core(mixes[2][2]))
-    taken = [halves_sum(mixes[chip][3], back_arrived[chip]) for chip in range(2)]
-    x_low = swap_x(taken[1][0])
     row_chips.append([swap_core(rows_low), swap_core(rows_high), rows_low, rows_high])
-    grads_both = after(grads_both, mixes[1][0])
-    grad_chips.append([swap_core(grads_both), grads_both])
-    upstream.append(narrow(after(grad_chips[3], mixes[2][0], taken), outer))
-    taken.append(halves_sum(mixes[2][3], after(back_arrived[2], upstream[3])))
-    y_high = swap_y(taken[2][1])
-    mixes.append(mix(3, taken[2], row_chips[3]))
+    own_part, x_part = after((mixes[0][3], mixes[1][3]), mixes[2][0])
+    x_low_part = add_low(x_part[:half], back_arrived[1][:half])
+    x_low = swap_x(x_low_part)
+    back_two, x_low_part = after((back_arrived[2], x_low_part))
+    y_taken = halves_sum(mixes[2][3], back_two)
+    y_high = swap_y(y_taken[1])
+    mixes.append(mix(3, y_taken, row_chips[3]))
     back_arrived.append(swap_core(after(mixes[3][2], x_low, y_high)))
-    taken.append(halves_sum(mixes[3][3], back_arrived[3]))
-    hops = [x_low, y_high, swap_x(taken[3][0]), swap_y(taken[3][1])]
+    diagonal = halves_sum(mixes[3][3], back_arrived[3])
+    hops = [x_low, y_high, swap_x(diagonal[0]), swap_y(diagonal[1])]
+    own_part, x_part = after((own_part, x_part), diagonal)
+    own_taken = halves_sum(own_part, back_arrived[0])
+    x_high_part = add_low(x_part[half:], back_arrived[1][half:])
+    taken = [own_taken, (x_low_part, x_high_part), y_taken, diagonal]
 
     pre_list = [m[0] for m in mixes]
     weighted_list = after([m[1] for m in mixes], taken[3])
     forward = widen(weighted_list, outer)
     hops = after(hops, forward)
-    ends = last_hops(taken, hops)
+    ends = last_hops(last_parts(taken, hops))
     forward = after(forward, hops)
     arrived_forward = [swap_core(forward[2 * chip]) for chip in range(4)]
     forward_taken = [halves_sum(forward[2 * c + 1], arrived_forward[c]) for c in range(4)]
     back_sum = hops_sum(taken, hops, after(ends, forward_taken))
     grad_normed_two = line_reduce(back_sum)
     forward_hops = first_hops(after(forward_taken, back_sum))
-    outer_grad = weight_gradients(after(weighted_list, back_sum), grad_chips, LANES)
-    inner_grad = weight_gradients(after(pre_list, outer_grad), row_chips, 256)
-    grad_normed_two, forward_hops = after((grad_normed_two, forward_hops), inner_grad)
-    forward_ends = last_hops(forward_taken, forward_hops)
+    gate_grad = weight_gradients(numbers, after(pre_list, back_sum), row_chips, pad, 0)
+    up_grad = weight_gradients(numbers, after(pre_list, gate_grad), row_chips, pad, 1)
+    forward_hops = after(forward_hops, up_grad)
+    forward_lasts = last_parts(forward_taken, forward_hops)
+    grad_normed_two, forward_lasts = after((grad_normed_two, forward_lasts))
+    forward_ends = last_hops(forward_lasts)
 
     grad_y = own_rows(grad_rows).astype(jnp.float32)
     after_norm_grad, gain_two_grad = jax.vjp(root_norm, after_own, gains[1])[1](grad_normed_two)
@@ -1505,63 +1554,65 @@
     grad_mixed = lax.all_to_all(
         grad_heads, "tp", split_axis=0, concat_axis=0, tiled=True
     ).reshape(tokens, local_width)
-    heads_own = after(own_columns(mixed_all), grad_heads)
+    grad_mixed, forward_ends = after((grad_mixed, forward_ends))
+    forward_sum = hops_sum(forward_taken, forward_hops, forward_ends)
+    grad_mixed, forward_sum = after((grad_mixed, forward_sum))
+    grad_query, grad_own, grad_prior = attend_back(
+        projected, prior, masks, log_total, grad_mixed, cosine, signed_sine, score_scale
+    )
+    arrived = from_behind(grad_prior, "ctx", -1)
+    layer_own = lax.psum_scatter(forward_sum, "tp", scatter_dimension=0, tiled=True)
+    outer_grad = weight_gradients(
+        numbers, after(weighted_list, grad_prior), None, pad, 0, all_grads
+    )
+    layer_own = (after_own + layer_own.astype(jnp.float32)).astype(jnp.bfloat16)
+    heads_own = after(
+        lax.dynamic_slice_in_dim(mixed_all, me_tp * share, share, axis=1), outer_grad
+    )
     projection_full = lax.dot_general(
         heads_own, grad_attn, (((1,), (0,)), ((), ())), preferred_element_type=jnp.float32
     ).astype(jnp.bfloat16)
+    arrived, outer_grad, layer_own = after((arrived, outer_grad, layer_own))
     projection_grad = lax.psum_scatter(
-        projection_full.reshape(tp * local_width, width),
+        after(projection_full, arrived).reshape(tp * local_width, width),
         ("fsdp", "ctx"),
         scatter_dimension=1,
         tiled=True,
     )
-    projection_grad = lax.psum_scatter(
-        projection_grad, "tp", scatter_dimension=0, tiled=True
-    ).astype(jnp.float32)
-
-    grad_mixed, forward_ends = after((grad_mixed, forward_ends))
-    forward_sum = hops_sum(forward_taken, forward_hops, forward_ends)
-    grad_query, grad_own, grad_prior = attend_back(
-        projected, prior, masks, log_total, grad_mixed, cosine, signed_sine, score_scale
-    )
-    arrived = from_behind(grad_prior, "ctx", -1)
-    layer_own = after_own + hop_reduce(after(forward_sum, grad_prior))
-    shared_grad = jnp.concatenate(
-        [inner_grad[hid_e:hid], inner_grad[pad + hid_e : pad + hid], outer_grad[hid_e:hid]]
-    ).astype(jnp.bfloat16)
-    shared_parts = exchange_order(columns_of(after(shared_grad, grad_mixed), 8))
-    shared_parts = hop_trade(after(shared_parts, grad_prior))
-    arrived, layer_own, shared_parts = after((arrived, layer_own, shared_parts))
     grad_linear, bias_part, gain_one_part, grad_one_part = project_back(
         numbers, grad_query, grad_own, arrived, cosine, signed_sine, hidden_rows, qkv_parts
     )
-    grad_normed_one = hop_reduce(grad_one_part)
-    residual_own = own_rows(hidden_rows).astype(jnp.float32)
-    residual_norm_grad, _ = jax.vjp(root_norm, residual_own, gains[0])[1](grad_normed_one)
-    input_own = (grad_after + residual_norm_grad).astype(jnp.bfloat16)
-    input_grad = line_gather(input_own).reshape(1, tokens, width)
-    layer_out = hop_gather(after(layer_own.astype(jnp.bfloat16), grad_one_part))
-    input_grad = after(input_grad, layer_out)
-    layer_out = layer_out.reshape(1, tokens, width)
-
-    grad_linear, late = after((grad_linear, grad_normed_one), grad_one_part)
-    qkv_full = project_weights(first_normalized, grad_linear)
-    qkv_grad = jnp.transpose(
-        lax.psum_scatter(
-            qkv_full.reshape(8 * 3 * deep, local_width),
-            ("fsdp", "ctx"),
-            scatter_dimension=0,
-            tiled=True,
-        ).reshape(3, deep, local_width),
-        (1, 0, 2),
+    layer_out = hop_gather(layer_own).reshape(1, tokens, width)
+    grad_normed_one = lax.psum_scatter(
+        grad_one_part, "tp", scatter_dimension=0, tiled=True
     ).astype(jnp.float32)
-
-    inner_grad, outer_grad = after((inner_grad, outer_grad), late)
-    inner_expert = jnp.transpose(
-        jnp.stack([inner_grad[:hid_e], inner_grad[pad : pad + hid_e]]), (2, 0, 1)
-    )[None]
+    first = grad_one_part
+    gate_grad, up_grad, outer_grad = after((gate_grad, up_grad, outer_grad), first)
+    inner_expert = jnp.transpose(jnp.stack([gate_grad[:hid_e], up_grad[:hid_e]]), (2, 0, 1))[None]
     outer_expert = outer_grad[:hid_e][None]
-    shared_back = jnp.stack(exchange_order(after(shared_parts, late)))
+    shared_grad = jnp.concatenate(
+        [gate_grad[hid_e:hid], up_grad[hid_e:hid], outer_grad[hid_e:hid]]
+    ).astype(jnp.bfloat16)
+    shared_parts = exchange_order(columns_of(shared_grad, 8))
+
+    small = sum_eight(
+        jnp.concatenate(
+            [
+                gate_grad[hid : hid + experts + 1],
+                after(gain_one_part, first),
+                gain_two_grad[None],
+                jnp.pad(
+                    after(bias_part, first).reshape(1, 3 * local_width),
+                    ((0, 0), (0, width - 3 * local_width)),
+                ),
+            ]
+        )
+    )
+    bias_grad = small[experts + 3, : 3 * local_width].reshape(3, local_width)
+    small = small[: experts + 3]
+    shared_parts = after(shared_parts, small)
+    shared_parts = trade_cores(shared_parts, trade_chips(shared_parts))
+    shared_back = jnp.stack(exchange_order(shared_parts))
     inner_shared = jnp.transpose(
         jnp.stack([shared_back[:, :hid_s], shared_back[:, hid_s : 2 * hid_s]]).reshape(
             2, 8 * hid_s, deep
@@ -1569,21 +1620,26 @@
         (2, 0, 1),
     ).astype(jnp.float32)
     outer_shared = shared_back[:, 2 * hid_s :].reshape(8 * hid_s, deep).astype(jnp.float32)
-
-    small = sum_over(
-        jnp.concatenate(
-            [
-                inner_grad[hid : hid + experts + 1],
-                after(gain_one_part, late),
-                gain_two_grad[None],
-            ]
-        ),
-        True,
-    )
+    qkv_full = project_weights(first_normalized, after(grad_linear, grad_one_part))
+    qkv_arrived = lax.all_to_all(
+        after(qkv_full, small), ("fsdp", "ctx"), split_axis=0, concat_axis=0, tiled=True
+    )
+    qkv_grad = jnp.transpose(jnp.sum(qkv_arrived.astype(jnp.float32), axis=0), (1, 0, 2))
+
+    residual_own = own_rows(hidden_rows).astype(jnp.float32)
+    residual_norm_grad, _ = jax.vjp(root_norm, residual_own, gains[0])[1](grad_normed_one)
+    input_own = (grad_after + residual_norm_grad).astype(jnp.bfloat16)
+    small = sum_line(small)
+    input_own, layer_out, inner_shared, outer_shared, inner_expert, small = after(
+        (input_own, layer_out, inner_shared, outer_shared, inner_expert, small)
+    )
+    input_grad = hop_gather(input_own).reshape(1, tokens, width)
+    projection_grad = lax.psum_scatter(
+        projection_grad, "tp", scatter_dimension=0, tiled=True
+    ).astype(jnp.float32)
     router_grad = small[:experts].T
     blend_grad = small[experts]
     gains_grad = small[experts + 1 :]
-    bias_grad = sum_over(after(bias_part, late).reshape(3, local_width), False)
     return (
         layer_out,
         input_grad,

time: 1120 us -> 951 us (0.85)
  waiting for transfers between devices: 363 us -> 226 us
  blocking collectives: 0 us -> 63.3 us
  starting transfers between devices: 144 us -> 93 us
  other arithmetic: 125 us -> 99.7 us
  local copies, waits for them, and re-layouts: 136 us -> 118 us
    all_to_all x0 -> x2, blocking collectives: none -> 63.3 us  [the longest x1 42.3 us: eight_plan(): lax.all_to_all(kept_all.T.reshape(experts, 1, tokens), ('fsdp', 'ctx'), s...]
    ppermute x17 -> x4, waiting for transfers between devices: 99.7 us -> 48.2 us  [the longest x2 36.2 us: trade_chips(): lax.ppermute(jnp.concatenate([parts[5], parts[7]]), ('fsdp', 'ctx'), [(d,...]
    all_to_all x5 -> x1, waiting for transfers between devices: 51.5 us -> 7.48 us  [line_gather(): return lax.all_to_all(copies, 'tp', split_axis=0, concat_axis=0, tiled=True)]
    ppermute x16 -> x14, waiting for transfers between devices: 87.9 us -> 45.1 us  [swap_y(): return lax.ppermute(values, 'ctx', [(0, 1), (1, 0)])]
    ppermute x17 -> x4, starting transfers between devices: 43.7 us -> 13.4 us  [the longest x2 11 us: sum_line(): lax.ppermute(values, 'tp', [(i, i ^ bit) for i in range(count)])]
    convert_element_type x18 -> x11, other arithmetic: 46.6 us -> 24.1 us  [add_low(): (one.astype(jnp.float32) + other.astype(jnp.float32)).astype(jnp.bfloat16)]
    all_to_all x5 -> x1, starting transfers between devices: 25.4 us -> 5.35 us  [line_gather(): return lax.all_to_all(copies, 'tp', split_axis=0, concat_axis=0, tiled=True)]
    reduce_scatter x2 -> x3, waiting for transfers between devices: 0.01 us -> 14.4 us  [the longest x1 14.4 us: eight_plan(): lax.psum_scatter(after(projection_full, arrived).reshape(tp * local_width...]
  transfers between devices with their start and end apart: 97 -> 79, of which waited for: 43 -> 32; matrix products, arithmetic and copies ran while one was open for 16% -> 15% of each run, Pallas kernels for 27% -> 33%
where the time goes in v3:
time: 951 us; the launch traced here: 940 us
  Pallas kernels  318 us (33%)
  waiting for transfers between devices  226 us (24%)
  local copies, waits for them, and re-layouts  118 us (12%)
  other arithmetic  99.7 us (10%)
  starting transfers between devices  93 us (10%)
  blocking collectives  63.3 us (7%)
  between operations  16.2 us (2%)
    pallas_call x4, Pallas kernels, mixture(): call(kernel, [jax.ShapeDtypeStruct((tokens, 2 * pad), jnp.bfloat16), jax....  105 us
    pallas_call x3, Pallas kernels, weight_gradients(): call(kernel, jax.ShapeDtypeStruct((units, width), jnp.float32), 2 * chips...  67.8 us
    unnamed x250, local copies, waits for them, and re-layouts  64.3 us
    ppermute x14, waiting for transfers between devices, swap_y(): return lax.ppermute(values, 'ctx', [(0, 1), (1, 0)])  45.1 us
    ppermute x15, waiting for transfers between devices, swap_x(): return lax.ppermute(values, 'fsdp', [(f, f ^ 2) for f in range(4)])  43.4 us
    all_to_all x1, blocking collectives, eight_plan(): lax.all_to_all(kept_all.T.reshape(experts, 1, tokens), ('fsdp', 'ctx'), s...  42.3 us
    ppermute x2, waiting for transfers between devices, trade_chips(): lax.ppermute(jnp.concatenate([parts[5], parts[7]]), ('fsdp', 'ctx'), [(d,...  36.2 us
    pallas_call x1, Pallas kernels, widen(): call(kernel, [jax.ShapeDtypeStruct((rows, width), jnp.bfloat16)] * count,...  35.3 us
  transfers between devices with their start and end apart: 79, of which 32 were waited for; matrix products, arithmetic and copies ran while one was open for 15% of the time, Pallas kernels for 33%

profile of v3, /device:TPU:0, one launch (start us, length us, event | category | flops | bytes accessed | tf_op | source)
XLA Modules:
  0.0 940.1 jit_solution(1222773038520544333)
XLA Ops:
  15.3 13.3 %collective-permute-done.1.others_1_ = bf16[3,256,512]{2,1,0:T(8,128)(2,1)S(1)} collective-permute-done((bf16[3,256,512]{2,1,0:T(8,128)(2,1)}, bf16[3,256,512]{2,1,0:T(8,128)(2,1)S(1)}, u32[]{:S(2)}, u32[]{:S(2)}) %collective-permute-start.1) | collective-permute-done | bytes 786464 | tf_op jit(solution)/shard_map/ppermute | solution.py:476
  33.7 7.1 collective-permute-done.5.others_6_
  48.9 9.3 shard_map.238
  70.1 42.3 %all_to_all.25 = f32[8,1,704]{2,1,0:T(1,128)S(1)} all-to-all(f32[8,1,704]{2,1,0:T(1,128)S(1)} %copy.55), channel_id=1, replica_groups=mesh['fsdp'=4,'ctx'=2,'tp'=4] {'fsdp','ctx'}, dimensions={0} | all-to-all | bytes 45056 | tf_op jit(solution)/shard_map/all_to_all | solution.py:1372
  114.1 14.2 %shard_map.239 = (bf16[704,512]{1,0:T(8,128)(2,1)S(1)}, f32[704,4]{1,0:T(8,128)S(1)}) custom-call(bf16[3,704,512]{2,1,0:T(8,128)(2,1)S(1)} %get-tuple-element.165.q_ref.own_ref, bf16[3,704,512]{2,1,0:T(8,128)(2,1)S(1)} %get-tuple-element.165.q_ref.own_ref, bf16[2,704,512]{2,1,0:T(8,128)(2,1)} %collective-permute-done.9.prior_ref, ...), custom_call_target="tpu_custom_call" | custom-call | flops 2030043136 | bytes 8290304 | tf_op jit(solution)/shard_map/pallas_call | solution.py:734
  154.8 15.4 %collective-permute-done.14 = bf16[1056,256]{1,0:T(8,128)(2,1)} collective-permute-done((bf16[1056,256]{1,0:T(8,128)(2,1)S(1)}, bf16[1056,256]{1,0:T(8,128)(2,1)}, u32[]{:S(2)}, u32[]{:S(2)}) %collective-permute-start.14) | collective-permute-done | bytes 540704 | tf_op jit(solution)/shard_map/ppermute | solution.py:468
  170.2 23.9 %collective-permute-done.15 = bf16[1056,256]{1,0:T(8,128)(2,1)} collective-permute-done((bf16[1056,256]{1,0:T(8,128)(2,1)S(1)}, bf16[1056,256]{1,0:T(8,128)(2,1)}, u32[]{:S(2)}, u32[]{:S(2)}) %collective-permute-start.15) | collective-permute-done | bytes 540704 | tf_op jit(solution)/shard_map/ppermute | solution.py:603
  194.1 7.5 all-to-all-done.1.mixed_ref
  201.6 13.3 %shard_map.240 = (bf16[704,2048]{1,0:T(8,128)(2,1)}, f32[176,2048]{1,0:T(8,128)}) custom-call(s32[2]{0:T(128)} %copy-done.35, bf16[704,2048]{1,0:T(8,128)(2,1)} %bitcast.152, f32[1,2048]{1,0:T(1,128)} %get-tuple-element.436.gain_ref, bf16[4,704,512]{2,1,0:T(8,128)(2,1)} %all-to-all-done.1.mixed_ref, ...), custom_call_target="tpu_custom_call" | custom-call | flops 5905580032 | bytes 17039360 | tf_op jit(solution)/shard_map/pallas_call | solution.py:1210
  241.0 9.1 shard_map.242.upstream_ref
  252.0 26.6 %shard_map.243 = (bf16[1408,1280]{1,0:T(8,128)(2,1)}, bf16[1408,640]{1,0:T(8,128)(2,1)S(1)}, bf16[704,2048]{1,0:T(8,128)(2,1)}, bf16[704,2048]{1,0:T(8,128)(2,1)S(1)}) custom-call(f32[1408,1]{1,0:T(8,128)S(1)} %copy-done.17, f32[1,128]{1,0:T(1,128)S(1)} %compare_convert_fusion.mine_ref, bf16[1280,2048]{1,0:T(8,128)(2,1)} %copy-done.37, ...), custom_call_target="tpu_custom_call" | custom-call | flops 14763950080 | bytes 25788416 | tf_op jit(solution)/shard_map/pallas_call | solution.py:1150
  281.6 18.7 %shard_map.244.upstream_ref = f32[4224,640]{1,0:T(8,128)S(1)} custom-call(s32[2]{0:T(128)S(1)} %copy-done.36, bf16[640,2048]{1,0:T(8,128)(2,1)S(1)} %copy-done.45, bf16[8,704,2048]{2,1,0:T(8,128)(2,1)} %bitcast.164), custom_call_target="tpu_custom_call" | custom-call | flops 11072962560 | bytes 30736384 | tf_op jit(solution)/shard_map/pallas_call | solution.py:1037
  314.9 26.1 %shard_map.245 = (bf16[1408,1280]{1,0:T(8,128)(2,1)}, bf16[1408,640]{1,0:T(8,128)(2,1)S(1)}, bf16[704,2048]{1,0:T(8,128)(2,1)S(1)}, bf16[704,2048]{1,0:T(8,128)(2,1)S(1)}) custom-call(f32[1408,1]{1,0:T(8,128)S(1)} %copy-done.20, f32[1,128]{1,0:T(1,128)S(1)} %compare_convert_fusion.mine_ref, bf16[1280,2048]{1,0:T(8,128)(2,1)} %copy-done.37, ...), custom_call_target="tpu_custom_call" | custom-call | flops 14763950080 | bytes 25788416 | tf_op jit(solution)/shard_map/pallas_call | solution.py:1150
  348.5 26.3 %shard_map.246 = (bf16[1408,1280]{1,0:T(8,128)(2,1)}, bf16[1408,640]{1,0:T(8,128)(2,1)S(1)}, bf16[704,2048]{1,0:T(8,128)(2,1)S(1)}, bf16[704,2048]{1,0:T(8,128)(2,1)S(1)}) custom-call(f32[1408,1]{1,0:T(8,128)S(1)} %copy-done.19, f32[1,128]{1,0:T(1,128)S(1)} %compare_convert_fusion.mine_ref, bf16[1280,2048]{1,0:T(8,128)(2,1)} %copy-done.37, ...), custom_call_target="tpu_custom_call" | custom-call | flops 14763950080 | bytes 25788416 | tf_op jit(solution)/shard_map/pallas_call | solution.py:1150
  394.8 25.7 %shard_map.247 = (bf16[1408,1280]{1,0:T(8,128)(2,1)}, bf16[1408,640]{1,0:T(8,128)(2,1)S(1)}, bf16[704,2048]{1,0:T(8,128)(2,1)S(1)}, bf16[704,2048]{1,0:T(8,128)(2,1)S(1)}) custom-call(f32[1408,1]{1,0:T(8,128)S(1)} %copy-done.21, f32[1,128]{1,0:T(1,128)S(1)} %compare_convert_fusion.mine_ref, bf16[1280,2048]{1,0:T(8,128)(2,1)} %copy-done.37, ...), custom_call_target="tpu_custom_call" | custom-call | flops 14763950080 | bytes 25788416 | tf_op jit(solution)/shard_map/pallas_call | solution.py:1150
  430.6 35.3 %shard_map.248 = (bf16[704,2048]{1,0:T(8,128)(2,1)S(1)}, bf16[704,2048]{1,0:T(8,128)(2,1)}, bf16[704,2048]{1,0:T(8,128)(2,1)}, bf16[704,2048]{1,0:T(8,128)(2,1)}...) custom-call(bf16[640,2048]{1,0:T(8,128)(2,1)S(1)} %copy-done.46, ...), custom_call_target="tpu_custom_call" | custom-call | flops 14763950080 | bytes 32899072 | tf_op jit(solution)/shard_map/pallas_call | solution.py:1075
  487.4 14.3 %collective-permute-done.37 = bf16[352,2048]{1,0:T(8,128)(2,1)S(1)} collective-permute-done((bf16[352,2048]{1,0:T(8,128)(2,1)S(1)}, bf16[352,2048]{1,0:T(8,128)(2,1)S(1)}, u32[]{:S(2)}, u32[]{:S(2)}) %collective-permute-start.37) | collective-permute-done | bytes 1441824 | tf_op jit(solution)/shard_map/ppermute | solution.py:476
  530.5 23.6 %shard_map.249 = f32[640,2048]{1,0:T(8,128)} custom-call(s32[2]{0:T(128)S(1)} %copy-done.36, bf16[1408,1280]{1,0:T(8,128)(2,1)} %get-tuple-element.254.refs_0_, bf16[1408,1280]{1,0:T(8,128)(2,1)} %get-tuple-element.255.refs_1_, bf16[1408,1280]{1,0:T(8,128)(2,1)} %get-tuple-element.256.refs_2_, bf16[1408,1280]{1,0:T(8,128)(2,1)} %get-tuple-element.257.refs_3_, ...), custom_call_target="tpu_custom_call" | custom-call | flops 14763950080 | bytes 35520512 | tf_op jit(solution)/shard_map/pallas_call | solution.py:1303
  554.1 23.8 %shard_map.250 = f32[640,2048]{1,0:T(8,128)} custom-call(s32[2]{0:T(128)S(1)} %copy-done.36, bf16[1408,1280]{1,0:T(8,128)(2,1)} %get-tuple-element.254.refs_0_, bf16[1408,1280]{1,0:T(8,128)(2,1)} %get-tuple-element.255.refs_1_, bf16[1408,1280]{1,0:T(8,128)(2,1)} %get-tuple-element.256.refs_2_, bf16[1408,1280]{1,0:T(8,128)(2,1)} %get-tuple-element.257.refs_3_, ...), custom_call_target="tpu_custom_call" | custom-call | flops 14763950080 | bytes 35520512 | tf_op jit(solution)/shard_map/pallas_call | solution.py:1303
  578.0 7.7 collective-permute-done.44
  604.6 21.0 %all_to_all.26 = bf16[4,176,512]{2,1,0:T(8,128)(2,1)} all-to-all(bf16[4,176,512]{2,1,0:T(8,128)(2,1)S(1)} %shard_map.251), channel_id=1, replica_groups=mesh['fsdp'=4,'ctx'=2,'tp'=4] {'tp'}, dimensions={0} | all-to-all | bytes 1441792 | tf_op jit(solution)/shard_map/all_to_all | solution.py:1554
  639.4 23.3 %shard_map.252 = (bf16[704,512]{1,0:T(8,128)(2,1)S(1)}, f32[2,704,512]{2,1,0:T(8,128)}, bf16[2,704,512]{2,1,0:T(8,128)(2,1)}) custom-call(bf16[3,704,512]{2,1,0:T(8,128)(2,1)S(1)} %copy-done.1, bf16[3,704,512]{2,1,0:T(8,128)(2,1)S(1)} %copy-done.1, bf16[2,704,512]{2,1,0:T(8,128)(2,1)} %collective-permute-done.9.prior_ref, f32[704,704]{1,0:T(8,128)S(1)} %copy-done.5, ...), custom_call_target="tpu_custom_call" | custom-call | flops 5075107840 | bytes 14778368 | tf_op jit(solution)/shard_map/pallas_call | solution.py:812
  665.1 20.3 %shard_map.253 = f32[640,2048]{1,0:T(8,128)S(1)} custom-call(s32[2]{0:T(128)S(1)} %copy-done.36, bf16[1408,640]{1,0:T(8,128)(2,1)S(1)} %copy-done.70, bf16[1408,640]{1,0:T(8,128)(2,1)S(1)} %copy-done.73, bf16[1408,640]{1,0:T(8,128)(2,1)S(1)} %copy-done.76, bf16[1408,640]{1,0:T(8,128)(2,1)S(1)} %copy-done.78, bf16[8,704,2048]{2,1,0:T(8,128)(2,1)} %bitcast.165), custom_call_target="tpu_custom_call" | custom-call | flops 14763950080 | bytes 35520512 | tf_op jit(solution)/shard_map/pallas_call | solution.py:1303
  699.0 9.1 shard_map.254
  745.3 12.2 %collective-permute-done.60 = bf16[1056,256]{1,0:T(8,128)(2,1)S(1)} collective-permute-done((bf16[1056,256]{1,0:T(8,128)(2,1)S(1)}, bf16[1056,256]{1,0:T(8,128)(2,1)S(1)}, u32[]{:S(2)}, u32[]{:S(2)}) %collective-permute-start.60) | collective-permute-done | bytes 540704 | tf_op jit(solution)/shard_map/ppermute | solution.py:603
  769.1 6.6 shard_map.255
  781.9 8.4 collective-permute-start.63
  798.7 12.1 %collective-permute-done.63 = f32[11,2048]{1,0:T(8,128)} collective-permute-done((f32[11,2048]{1,0:T(8,128)}, f32[11,2048]{1,0:T(8,128)}, u32[]{:S(2)}, u32[]{:S(2)}) %collective-permute-start.63) | collective-permute-done | bytes 90144 | tf_op jit(solution)/shard_map/ppermute | solution.py:533
  854.0 12.9 %collective-permute-done.67 = bf16[176,2048]{1,0:T(8,128)(2,1)S(1)} collective-permute-done((bf16[176,2048]{1,0:T(8,128)(2,1)S(1)}, bf16[176,2048]{1,0:T(8,128)(2,1)S(1)}, u32[]{:S(2)}, u32[]{:S(2)}) %collective-permute-start.67) | collective-permute-done | bytes 720928 | tf_op jit(solution)/shard_map/ppermute | solution.py:584
  878.3 10.5 %collective-permute-done.65 = bf16[176,2048]{1,0:T(8,128)(2,1)} collective-permute-done((bf16[176,2048]{1,0:T(8,128)(2,1)S(1)}, bf16[176,2048]{1,0:T(8,128)(2,1)}, u32[]{:S(2)}, u32[]{:S(2)}) %collective-permute-start.65) | collective-permute-done | bytes 720928 | tf_op jit(solution)/shard_map/ppermute | solution.py:587
  890.0 14.4 %reduce-scatter.9.cloned.1.call-done = bf16[2048,256]{1,0:T(8,128)(2,1)} async-done(((bf16[2048,2048]{1,0:T(8,128)(2,1)}), bf16[2048,256]{1,0:T(8,128)(2,1)}) %reduce-scatter.9.cloned.1.call-update) | async-done | bytes 1048592 | tf_op jit(solution)/shard_map/reduce_scatter | solution.py:1576
  916.7 14.3 %reduce-scatter.11.cloned.1.call-done = bf16[512,256]{1,0:T(8,128)(2,1)} async-done(((bf16[2048,256]{1,0:T(8,128)(2,1)}), bf16[512,256]{1,0:T(8,128)(2,1)}) %reduce-scatter.11.cloned.1.call-update) | async-done | bytes 262160 | tf_op jit(solution)/shard_map/reduce_scatter | solution.py:1637
  (547 shorter events, 375.3 us)
Async XLA Ops:
  7.2 34.2 %all-gather.4.cloned.1.call-start = ((), (), s32[]{:S(2)}) async-start(), calls=%async_computation.9 | async-start | bytes 1310720 | tf_op jit(solution)/shard_map/all_gather | solution.py:1357
  11.9 268.0 %all-gather.6.cloned.1.call-start = ((), (), s32[]{:S(2)}) async-start(), calls=%async_computation.14 | async-start | bytes 25952256 | tf_op jit(solution)/shard_map/all_gather | solution.py:1439
  61.0 51.4 %collective-permute-start.9 = (bf16[2,704,512]{2,1,0:T(8,128)(2,1)}, bf16[2,704,512]{2,1,0:T(8,128)(2,1)}, u32[]{:S(2)}, u32[]{:S(2)}) collective-permute-start(bf16[2,704,512]{2,1,0:T(8,128)(2,1)} %slice.326), channel_id=1, source_target_pairs={{0,4},{1,5},{2,6},{3,7},{8,12},{9,13},{10,14},{11,15},{16,20},{17,... | collective-permute-start | bytes 4325384 | tf_op jit(solution)/shard_map/ppermute | solution.py:23
  64.7 47.7 %collective-permute-start.10 = (bf16[2048,256]{1,0:T(8,128)(2,1)S(1)}, bf16[2048,256]{1,0:T(8,128)(2,1)}, u32[]{:S(2)}, u32[]{:S(2)}) collective-permute-start(bf16[2048,256]{1,0:T(8,128)(2,1)S(1)} %copy-done.8), channel_id=1, source_target_pairs={{0,16},{8,24},{16,0},{24,8},{1,17},{9,25},{17,1},{25,9},{2,18},{10... | collective-permute-start | bytes 3145736 | tf_op jit(solution)/shard_map/ppermute | solution.py:468
  68.0 44.4 %collective-permute-start.12 = (bf16[2048,256]{1,0:T(8,128)(2,1)}, bf16[2048,256]{1,0:T(8,128)(2,1)}, u32[]{:S(2)}, u32[]{:S(2)}) collective-permute-start(bf16[2048,256]{1,0:T(8,128)(2,1)} %collective-permute-done.11.others_1_), channel_id=1, source_target_pairs={{0,16},{8,24},{16,0},{24,8},{1,17},{9,25},{17,1},{25,9},{2,18},{10... | collective-permute-start | bytes 3145736 | tf_op jit(solution)/shard_map/ppermute | solution.py:468
  130.9 70.7 %all-to-all-start.1 = ((bf16[4,704,512]{2,1,0:T(8,128)(2,1)}), bf16[4,704,512]{2,1,0:T(8,128)(2,1)}, u32[]{:S(2)}, u32[]{:S(2)}) async-start(bf16[4,704,512]{2,1,0:T(8,128)(2,1)} %broadcast_in_dim.84), calls=%async_computation.1 | async-start | bytes 5767168 | tf_op jit(solution)/shard_map/all_to_all | solution.py:547
  139.9 61.8 %collective-permute-start.16 = (bf16[8192,256]{1,0:T(8,128)(2,1)}, bf16[8192,256]{1,0:T(8,128)(2,1)}, u32[]{:S(2)}, u32[]{:S(2)}) collective-permute-start(bf16[8192,256]{1,0:T(8,128)(2,1)} %pad_maximum_fusion), channel_id=1, source_target_pairs={{0,8},{8,0},{16,24},{24,16},{1,9},{9,1},{17,25},{25,17},{2,10},{10... | collective-permute-start | bytes 12582920 | tf_op jit(solution)/shard_map/ppermute | solution.py:472
  152.5 41.6 %collective-permute-start.15 = (bf16[1056,256]{1,0:T(8,128)(2,1)S(1)}, bf16[1056,256]{1,0:T(8,128)(2,1)}, u32[]{:S(2)}, u32[]{:S(2)}) collective-permute-start(bf16[1056,256]{1,0:T(8,128)(2,1)S(1)} %pad_maximum_fusion.8), channel_id=1, source_target_pairs={{0,20},{4,16},{8,28},{12,24},{16,4},{20,0},{24,12},{28,8},{1,21},{... | collective-permute-start | bytes 1622024 | tf_op jit(solution)/shard_map/ppermute | solution.py:603
  154.1 40.0 %collective-permute-start.13 = (bf16[1056,256]{1,0:T(8,128)(2,1)S(1)}, bf16[1056,256]{1,0:T(8,128)(2,1)}, u32[]{:S(2)}, u32[]{:S(2)}) collective-permute-start(bf16[1056,256]{1,0:T(8,128)(2,1)S(1)} %pad_maximum_fusion.6), channel_id=1, source_target_pairs={{0,4},{4,0},{1,5},{5,1},{2,6},{6,2},{3,7},{7,3},{8,12},{12,8},{9,1... | collective-permute-start | bytes 1622024 | tf_op jit(solution)/shard_map/ppermute | solution.py:476
  230.8 73.9 %collective-permute-start.21 = (bf16[704,2048]{1,0:T(8,128)(2,1)}, bf16[704,2048]{1,0:T(8,128)(2,1)}, u32[]{:S(2)}, u32[]{:S(2)}) collective-permute-start(bf16[704,2048]{1,0:T(8,128)(2,1)} %get-tuple-element.175.others_1_.refs_5_), channel_id=1, source_target_pairs={{0,4},{4,0},{1,5},{5,1},{2,6},{6,2},{3,7},{7,3},{8,12},{12,8},{9,1... | collective-permute-start | bytes 8650760 | tf_op jit(solution)/shard_map/ppermute | solution.py:476
  232.0 72.6 %collective-permute-start.20 = (bf16[704,2048]{1,0:T(8,128)(2,1)}, bf16[704,2048]{1,0:T(8,128)(2,1)}, u32[]{:S(2)}, u32[]{:S(2)}) collective-permute-start(bf16[704,2048]{1,0:T(8,128)(2,1)} %get-tuple-element.175.others_1_.refs_5_), channel_id=1, source_target_pairs={{0,16},{8,24},{16,0},{24,8},{1,17},{9,25},{17,1},{25,9},{2,18},{10... | collective-permute-start | bytes 8650760 | tf_op jit(solution)/shard_map/ppermute | solution.py:468
  304.7 41.4 %collective-permute-start.23 = (bf16[704,2048]{1,0:T(8,128)(2,1)}, bf16[704,2048]{1,0:T(8,128)(2,1)}, u32[]{:S(2)}, u32[]{:S(2)}) collective-permute-start(bf16[704,2048]{1,0:T(8,128)(2,1)} %get-tuple-element.196), channel_id=1, source_target_pairs={{0,8},{8,0},{16,24},{24,16},{1,9},{9,1},{17,25},{25,17},{2,10},{10... | collective-permute-start | bytes 8650760 | tf_op jit(solution)/shard_map/ppermute | solution.py:472
  305.2 42.0 %collective-permute-start.26 = (bf16[704,2048]{1,0:T(8,128)(2,1)}, bf16[704,2048]{1,0:T(8,128)(2,1)}, u32[]{:S(2)}, u32[]{:S(2)}) collective-permute-start(bf16[704,2048]{1,0:T(8,128)(2,1)} %collective-permute-done.21.others_1_.refs_9_), channel_id=1, source_target_pairs={{0,8},{8,0},{16,24},{24,16},{1,9},{9,1},{17,25},{25,17},{2,10},{10... | collective-permute-start | bytes 8650760 | tf_op jit(solution)/shard_map/ppermute | solution.py:472
  310.6 34.8 %collective-permute-start.24 = (bf16[352,2048]{1,0:T(8,128)(2,1)}, bf16[352,2048]{1,0:T(8,128)(2,1)}, u32[]{:S(2)}, u32[]{:S(2)}) collective-permute-start(bf16[352,2048]{1,0:T(8,128)(2,1)} %slice.346), channel_id=1, source_target_pairs={{0,16},{8,24},{16,0},{24,8},{1,17},{9,25},{17,1},{25,9},{2,18},{10... | collective-permute-start | bytes 4325384 | tf_op jit(solution)/shard_map/ppermute | solution.py:468
  377.8 42.7 %collective-permute-start.31 = (bf16[352,2048]{1,0:T(8,128)(2,1)}, bf16[352,2048]{1,0:T(8,128)(2,1)}, u32[]{:S(2)}, u32[]{:S(2)}) collective-permute-start(bf16[352,2048]{1,0:T(8,128)(2,1)} %add_convert_fusion.21), channel_id=1, source_target_pairs={{0,16},{8,24},{16,0},{24,8},{1,17},{9,25},{17,1},{25,9},{2,18},{10... | collective-permute-start | bytes 4325384 | tf_op jit(solution)/shard_map/ppermute | solution.py:468
  385.6 34.9 %collective-permute-start.32 = (bf16[352,2048]{1,0:T(8,128)(2,1)}, bf16[352,2048]{1,0:T(8,128)(2,1)}, u32[]{:S(2)}, u32[]{:S(2)}) collective-permute-start(bf16[352,2048]{1,0:T(8,128)(2,1)} %get-tuple-element.379), channel_id=1, source_target_pairs={{0,4},{4,0},{1,5},{5,1},{2,6},{6,2},{3,7},{7,3},{8,12},{12,8},{9,1... | collective-permute-start | bytes 4325384 | tf_op jit(solution)/shard_map/ppermute | solution.py:476
  428.9 37.1 %collective-permute-start.35 = (bf16[352,2048]{1,0:T(8,128)(2,1)}, bf16[352,2048]{1,0:T(8,128)(2,1)S(1)}, u32[]{:S(2)}, u32[]{:S(2)}) collective-permute-start(bf16[352,2048]{1,0:T(8,128)(2,1)} %get-tuple-element.376), channel_id=1, source_target_pairs={{0,4},{4,0},{1,5},{5,1},{2,6},{6,2},{3,7},{7,3},{8,12},{12,8},{9,1... | collective-permute-start | bytes 4325384 | tf_op jit(solution)/shard_map/ppermute | solution.py:476
  430.0 35.9 %collective-permute-start.34 = (bf16[352,2048]{1,0:T(8,128)(2,1)}, bf16[352,2048]{1,0:T(8,128)(2,1)S(1)}, u32[]{:S(2)}, u32[]{:S(2)}) collective-permute-start(bf16[352,2048]{1,0:T(8,128)(2,1)} %get-tuple-element.377), channel_id=1, source_target_pairs={{0,16},{8,24},{16,0},{24,8},{1,17},{9,25},{17,1},{25,9},{2,18},{10... | collective-permute-start | bytes 4325384 | tf_op jit(solution)/shard_map/ppermute | solution.py:468
  515.3 75.1 %all-to-all-start.2 = ((bf16[4,176,2048]{2,1,0:T(8,128)(2,1)}), bf16[4,176,2048]{2,1,0:T(8,128)(2,1)}, u32[]{:S(2)}, u32[]{:S(2)}) async-start(bf16[4,176,2048]{2,1,0:T(8,128)(2,1)} %bitcast.142), calls=%async_computation.2 | async-start | bytes 5767168 | tf_op jit(solution)/shard_map/all_to_all | solution.py:541
  520.2 167.6 %reduce-scatter.5.cloned.1.call-start = ((), (), s32[]{:S(2)}) async-start(), calls=%async_computation.10 | async-start | bytes 3604480 | tf_op jit(solution)/shard_map/reduce_scatter | solution.py:1564
  521.8 56.2 %collective-permute-start.42 = (bf16[352,2048]{1,0:T(8,128)(2,1)}, bf16[352,2048]{1,0:T(8,128)(2,1)S(1)}, u32[]{:S(2)}, u32[]{:S(2)}) collective-permute-start(bf16[352,2048]{1,0:T(8,128)(2,1)} %get-tuple-element.245), channel_id=1, source_target_pairs={{0,16},{8,24},{16,0},{24,8},{1,17},{9,25},{17,1},{25,9},{2,18},{10... | collective-permute-start | bytes 4325384 | tf_op jit(solution)/shard_map/ppermute | solution.py:468
  523.3 54.7 %collective-permute-start.43 = (bf16[352,2048]{1,0:T(8,128)(2,1)}, bf16[352,2048]{1,0:T(8,128)(2,1)S(1)}, u32[]{:S(2)}, u32[]{:S(2)}) collective-permute-start(bf16[352,2048]{1,0:T(8,128)(2,1)} %get-tuple-element.246), channel_id=1, source_target_pairs={{0,4},{4,0},{1,5},{5,1},{2,6},{6,2},{3,7},{7,3},{8,12},{12,8},{9,1... | collective-permute-start | bytes 4325384 | tf_op jit(solution)/shard_map/ppermute | solution.py:476
  524.2 61.6 %collective-permute-start.44 = (bf16[352,2048]{1,0:T(8,128)(2,1)}, bf16[352,2048]{1,0:T(8,128)(2,1)S(1)}, u32[]{:S(2)}, u32[]{:S(2)}) collective-permute-start(bf16[352,2048]{1,0:T(8,128)(2,1)} %get-tuple-element.247), channel_id=1, source_target_pairs={{0,16},{8,24},{16,0},{24,8},{1,17},{9,25},{17,1},{25,9},{2,18},{10... | collective-permute-start | bytes 4325384 | tf_op jit(solution)/shard_map/ppermute | solution.py:468
  524.8 62.1 %collective-permute-start.45 = (bf16[352,2048]{1,0:T(8,128)(2,1)}, bf16[352,2048]{1,0:T(8,128)(2,1)S(1)}, u32[]{:S(2)}, u32[]{:S(2)}) collective-permute-start(bf16[352,2048]{1,0:T(8,128)(2,1)} %get-tuple-element.248), channel_id=1, source_target_pairs={{0,4},{4,0},{1,5},{5,1},{2,6},{6,2},{3,7},{7,3},{8,12},{12,8},{9,1... | collective-permute-start | bytes 4325384 | tf_op jit(solution)/shard_map/ppermute | solution.py:476
  631.4 211.1 %reduce-scatter.7.cloned.1.call-start = ((), (), s32[]{:S(2)}) async-start(), calls=%async_computation.11 | async-start | bytes 3604480 | tf_op jit(solution)/shard_map/reduce_scatter | solution.py:1586
  711.1 193.3 %reduce-scatter.9.cloned.1.call-start = ((), (), s32[]{:S(2)}) async-start(), calls=%async_computation.12 | async-start | bytes 9437184 | tf_op jit(solution)/shard_map/reduce_scatter | solution.py:1576
  720.6 57.8 %collective-permute-start.52 = (bf16[176,2048]{1,0:T(8,128)(2,1)S(1)}, bf16[176,2048]{1,0:T(8,128)(2,1)S(1)}, u32[]{:S(2)}, u32[]{:S(2)}) collective-permute-start(bf16[176,2048]{1,0:T(8,128)(2,1)S(1)} %copy-done.83), channel_id=1, source_target_pairs={{0,1},{1,2},{2,3},{4,5},{5,6},{6,7},{8,9},{9,10},{10,11},{12,13},{... | collective-permute-start | bytes 2162696 | tf_op jit(solution)/shard_map/ppermute | solution.py:584
  723.0 56.9 %collective-permute-start.49 = (bf16[176,2048]{1,0:T(8,128)(2,1)S(1)}, bf16[176,2048]{1,0:T(8,128)(2,1)}, u32[]{:S(2)}, u32[]{:S(2)}) collective-permute-start(bf16[176,2048]{1,0:T(8,128)(2,1)S(1)} %copy-done.83), channel_id=1, source_target_pairs={{1,0},{2,1},{3,2},{5,4},{6,5},{7,6},{9,8},{10,9},{11,10},{13,12},{... | collective-permute-start | bytes 2162696 | tf_op jit(solution)/shard_map/ppermute | solution.py:587
  769.0 46.2 %collective-permute-start.61 = (bf16[2112,256]{1,0:T(8,128)(2,1)}, bf16[2112,256]{1,0:T(8,128)(2,1)S(1)}, u32[]{:S(2)}, u32[]{:S(2)}) collective-permute-start(bf16[2112,256]{1,0:T(8,128)(2,1)} %pad_maximum_fusion.5), channel_id=1, source_target_pairs={{0,8},{8,0},{16,24},{24,16},{1,9},{9,1},{17,25},{25,17},{2,10},{10... | collective-permute-start | bytes 3244040 | tf_op jit(solution)/shard_map/ppermute | solution.py:472
  793.6 112.7 %all-to-all-start.4 = ((bf16[8,3,256,512]{3,2,1,0:T(8,128)(2,1)}), bf16[8,3,256,512]{3,2,1,0:T(8,128)(2,1)}, u32[]{:S(2)}, u32[]{:S(2)}) async-start(bf16[8,3,256,512]{3,2,1,0:T(8,128)(2,1)} %copy-done.7), calls=%async_computation.6 | async-start | bytes 12582912 | tf_op jit(solution)/shard_map/all_to_all | solution.py:1624
  798.6 132.4 %reduce-scatter.11.cloned.1.call-start = ((), (), s32[]{:S(2)}) async-start(), calls=%async_computation.13 | async-start | bytes 1310720 | tf_op jit(solution)/shard_map/reduce_scatter | solution.py:1637
  876.7 34.6 %collective-permute-start.69 = (bf16[176,2048]{1,0:T(8,128)(2,1)S(1)}, bf16[176,2048]{1,0:T(8,128)(2,1)}, u32[]{:S(2)}, u32[]{:S(2)}) collective-permute-start(bf16[176,2048]{1,0:T(8,128)(2,1)S(1)} %collective-permute-done.68), channel_id=1, source_target_pairs={{2,3},{6,7},{10,11},{14,15},{18,19},{22,23},{26,27},{30,31}} | collective-permute-start | bytes 2162696 | tf_op jit(solution)/shard_map/ppermute | solution.py:584
  (172 other events, 1934.6 us)
Sparse Core Ops, SparseCore 0:
  12.0 28.2 all-gather.3
  112.6 141.9 all-gather.5
  631.5 56.0 reduce-scatter.4
  711.2 72.8 reduce-scatter.6
  787.4 116.9 reduce-scatter.8
  906.6 24.3 reduce-scatter.10
